TPU v7x, 32 devices: a whole 2x2x4 slice. The times are simulated.
32 devices in a mesh: gx: 4 (over y, x), gy: 8 (over z, core).
Axes of the slice: x: 2, y: 2, z: 4, core: 2. Of those that a mesh axis runs over, the one named last changes fastest.
Arguments:
- tokens: bfloat16 [65536, 768], P(('gx', 'gy')), may hold values from -6 to 6
- segment_ids: int32 [128, 512], P(('gx', 'gy')), may hold values from 0 to 7, never falling along the last dimension, each value on 1 to 128 neighbouring positions
- pad_counts: int32 [128], P(('gx', 'gy')), may hold values from 0 to 64
- out_cotangent: bfloat16 [65536, 768], P(('gx', 'gy')), may hold values from -6 to 6
- qkv_master: float32 [768, 2304], P(('gx', 'gy')), may hold values from -0.21875 to 0.21875
- proj_master: float32 [768, 768], P(('gx', 'gy')), may hold values from -0.875 to 0.875
- up_master: float32 [768, 3072], P(('gx', 'gy')), may hold values from -0.21875 to 0.21875
- down_master: float32 [3072, 768], P(('gx', 'gy')), may hold values from -0.109375 to 0.109375
- gain_master: float32 [1536], P(('gx', 'gy')), may hold values from 0.5 to 1.5
- bias_master: float32 [7680], P(('gx', 'gy')), may hold values from -1.8 to 1.8
- qkv_moment: float32 [768, 2304], P(('gx', 'gy')), may hold values from -0.0234375 to 0.0234375
- proj_moment: float32 [768, 768], P(('gx', 'gy')), may hold values from -0.0234375 to 0.0234375
- up_moment: float32 [768, 3072], P(('gx', 'gy')), may hold values from -0.0234375 to 0.0234375
- down_moment: float32 [3072, 768], P(('gx', 'gy')), may hold values from -0.0234375 to 0.0234375
- gain_moment: float32 [1536], P(('gx', 'gy')), may hold values from -0.0234375 to 0.0234375
- bias_moment: float32 [7680], P(('gx', 'gy')), may hold values from -0.0234375 to 0.0234375
- qkv_average: float32 [768, 2304], P(('gx', 'gy')), may hold values from -0.21875 to 0.21875
- proj_average: float32 [768, 768], P(('gx', 'gy')), may hold values from -0.875 to 0.875
- up_average: float32 [768, 3072], P(('gx', 'gy')), may hold values from -0.21875 to 0.21875
- down_average: float32 [3072, 768], P(('gx', 'gy')), may hold values from -0.109375 to 0.109375
- gain_average: float32 [1536], P(('gx', 'gy')), may hold values from 0.5 to 1.5
- bias_average: float32 [7680], P(('gx', 'gy')), may hold values from -1.8 to 1.8
Outputs:
- layer_output: bfloat16 [65536, 768], P(('gx', 'gy'))
- input_grad: float32 [65536, 768], P(('gx', 'gy'))
- qkv_grad: float32 [768, 2304], P(('gx', 'gy'))
- proj_grad: float32 [768, 768], P(('gx', 'gy'))
- up_grad: float32 [768, 3072], P(('gx', 'gy'))
- down_grad: float32 [3072, 768], P(('gx', 'gy'))
- gain_grad: float32 [1536], P(('gx', 'gy'))
- bias_grad: float32 [7680], P(('gx', 'gy'))
- qkv_master_new: float32 [768, 2304], P(('gx', 'gy'))
- proj_master_new: float32 [768, 768], P(('gx', 'gy'))
- up_master_new: float32 [768, 3072], P(('gx', 'gy'))
- down_master_new: float32 [3072, 768], P(('gx', 'gy'))
- gain_master_step: float32 [1536], P(('gx', 'gy'))
- bias_master_new: float32 [7680], P(('gx', 'gy'))
- qkv_moment_new: float32 [768, 2304], P(('gx', 'gy'))
- proj_moment_new: float32 [768, 768], P(('gx', 'gy'))
- up_moment_new: float32 [768, 3072], P(('gx', 'gy'))
- down_moment_new: float32 [3072, 768], P(('gx', 'gy'))
- gain_moment_new: float32 [1536], P(('gx', 'gy'))
- bias_moment_new: float32 [7680], P(('gx', 'gy'))
- qkv_average_new: float32 [768, 2304], P(('gx', 'gy'))
- proj_average_new: float32 [768, 768], P(('gx', 'gy'))
- up_average_new: float32 [768, 3072], P(('gx', 'gy'))
- down_average_new: float32 [3072, 768], P(('gx', 'gy'))
- gain_average_step: float32 [1536], P(('gx', 'gy'))
- bias_average_new: float32 [7680], P(('gx', 'gy'))
Inputs may be any that keep to these rules, and one draw needn't show every extreme that they name: `segment_ids`: within each row of 512 tokens the pair numbers never fall, and each pair has 1 to 128 tokens. The last pad_counts[r] tokens of row r are padding.
All inputs are finite; a program needn't handle non-finite values.
Results may differ from a plain program's by a relative error of at most 0.013.
The roundings to bfloat16 on the way count: a program that leaves them out, or rounds other values in their place, can miss the bound.
Values may be sent and summed in bfloat16 or wider, within the bound.
A program may use at most 320 MiB of HBM per device.

v0:
```python
from functools import partial

import jax
import jax.numpy as jnp
from jax import lax
from jax.sharding import PartitionSpec as P

D = 768
HEADS = 12
HEAD_DIM = 64
FF = 3072


norm_eps = 1e-06
momentum_coef = 0.9
learn_rate = 4.0
average_keep = 0.9


def layer_norm(values, gain, shift):
    centre = jnp.mean(values, axis=-1, keepdims=True)
    centred = values - centre
    spread = jnp.mean(centred * centred, axis=-1, keepdims=True)
    return centred * lax.rsqrt(spread + norm_eps) * gain + shift


def outer_product(left, right):
    return lax.dot_general(
        left, right, (((0,), (0,)), ((), ())), preferred_element_type=jnp.float32
    )


def back_product(grads, weight):
    return lax.dot_general(
        grads, weight, (((1,), (1,)), ((), ())), preferred_element_type=jnp.float32
    )


def column_sum(values):
    return jnp.sum(values.astype(jnp.float32), axis=0)


def masked_scores(queries, key_heads, segments, padding):
    seq_len = segments.shape[1]
    position = jnp.arange(seq_len, dtype=jnp.int32)
    is_pad = position[None, :] >= (seq_len - padding)[:, None]
    allowed = (segments[:, :, None] == segments[:, None, :]) & (
        is_pad[:, :, None] == is_pad[:, None, :]
    )
    scores = jnp.einsum(
        "rqhd,rkhd->rhqk", queries, key_heads, preferred_element_type=jnp.float32
    ) * HEAD_DIM ** (-0.5)
    return jnp.where(allowed[:, None, :, :], scores, -1e30)


def update(grad, master, moment, average, tokens_all):
    mean_grad = grad / tokens_all
    moment_new = momentum_coef * moment + mean_grad
    step_size = -learn_rate * (mean_grad + momentum_coef * moment_new)
    master_new = master + step_size
    average_new = average_keep * average + (1.0 - average_keep) * master_new
    return (master_new, moment_new, average_new)


def update_steps(grad, master, moment, average, tokens_all):
    mean_grad = grad / tokens_all
    moment_new = momentum_coef * moment + mean_grad
    step_size = -learn_rate * (mean_grad + momentum_coef * moment_new)
    average_step = (1.0 - average_keep) * (master + step_size - average)
    return (step_size, moment_new, average_step)


def on_device(
    tokens,
    segment_ids,
    pad_counts,
    out_cotangent,
    qkv_master,
    proj_master,
    up_master,
    down_master,
    gain_master,
    bias_master,
    qkv_moment,
    proj_moment,
    up_moment,
    down_moment,
    gain_moment,
    bias_moment,
    qkv_average,
    proj_average,
    up_average,
    down_average,
    gain_average,
    bias_average,
):
    row_count = segment_ids.shape[0]
    seq_len = segment_ids.shape[1]
    token_count = row_count * seq_len
    tokens_all = token_count * lax.axis_size(("gx", "gy"))
    qkv_low = qkv_master.astype(jnp.bfloat16)
    proj_low = proj_master.astype(jnp.bfloat16)
    up_low = up_master.astype(jnp.bfloat16)
    down_low = down_master.astype(jnp.bfloat16)
    gain_low = gain_master.astype(jnp.bfloat16)
    bias_low = bias_master.astype(jnp.bfloat16)
    w_qkv, w_out, w_up, w_down, gain_all, bias_all = (
        lax.all_gather(qkv_low, ("gx", "gy"), axis=0, tiled=True),
        lax.all_gather(proj_low, ("gx", "gy"), axis=0, tiled=True),
        lax.all_gather(up_low, ("gx", "gy"), axis=0, tiled=True),
        lax.all_gather(down_low, ("gx", "gy"), axis=0, tiled=True),
        lax.all_gather(gain_low, ("gx", "gy"), axis=0, tiled=True),
        lax.all_gather(bias_low, ("gx", "gy"), axis=0, tiled=True),
    )
    bias_all = bias_all.astype(jnp.float32)
    gain_all = gain_all.astype(jnp.float32)
    bias_q = bias_all[0:D]
    bias_v = bias_all[D : 2 * D]
    bias_o = bias_all[2 * D : 3 * D]
    shift_one = bias_all[3 * D : 4 * D]
    bias_up = bias_all[4 * D : 4 * D + FF]
    bias_down = bias_all[4 * D + FF : 5 * D + FF]
    shift_two = bias_all[5 * D + FF : 6 * D + FF]
    gain_one = gain_all[0:D]
    gain_two = gain_all[D : 2 * D]
    inputs = tokens.astype(jnp.float32)
    key_zeros = jnp.zeros((D,), jnp.float32)
    projected = jnp.dot(tokens, w_qkv, preferred_element_type=jnp.float32) + jnp.concatenate(
        [bias_q, key_zeros, bias_v]
    )
    projected = projected.astype(jnp.bfloat16)
    queries = projected[:, 0:D].reshape(row_count, seq_len, HEADS, HEAD_DIM)
    key_heads = projected[:, D : 2 * D].reshape(row_count, seq_len, HEADS, HEAD_DIM)
    value_heads = projected[:, 2 * D : 3 * D].reshape(row_count, seq_len, HEADS, HEAD_DIM)
    masked = masked_scores(queries, key_heads, segment_ids, pad_counts)
    highest = jnp.max(masked, axis=-1, keepdims=True)
    summed = jnp.sum(jnp.exp(masked - highest), axis=-1, keepdims=True)
    log_total = highest + jnp.log(summed)
    probs_low = jnp.exp(masked - log_total).astype(jnp.bfloat16)
    context = jnp.einsum(
        "rhqk,rkhd->rqhd", probs_low, value_heads, preferred_element_type=jnp.float32
    )
    context = context.reshape(token_count, D).astype(jnp.bfloat16)
    branch = jnp.dot(context, w_out, preferred_element_type=jnp.float32) + bias_o
    normed, norm_one_back = jax.vjp(layer_norm, inputs + branch, gain_one, shift_one)
    normed_low = normed.astype(jnp.bfloat16)
    hidden = jnp.dot(normed_low, w_up, preferred_element_type=jnp.float32) + bias_up
    activated, gelu_back = jax.vjp(partial(jax.nn.gelu, approximate=False), hidden)
    activated_low = activated.astype(jnp.bfloat16)
    mixed = jnp.dot(activated_low, w_down, preferred_element_type=jnp.float32) + bias_down
    result, norm_two_back = jax.vjp(layer_norm, normed + mixed, gain_two, shift_two)
    layer_output = result.astype(jnp.bfloat16)
    w_qkv, w_out, w_up, w_down = (
        lax.all_gather(qkv_low, ("gx", "gy"), axis=0, tiled=True),
        lax.all_gather(proj_low, ("gx", "gy"), axis=0, tiled=True),
        lax.all_gather(up_low, ("gx", "gy"), axis=0, tiled=True),
        lax.all_gather(down_low, ("gx", "gy"), axis=0, tiled=True),
    )
    cotangent = out_cotangent.astype(jnp.float32)
    second_grad, gain_two_grad, shift_two_grad = norm_two_back(cotangent)
    mixed_grad = second_grad.astype(jnp.bfloat16)
    bias_down_grad = column_sum(mixed_grad)
    w_down_grad = outer_product(activated_low, mixed_grad)
    activated_grad = back_product(mixed_grad, w_down)
    hidden_grad = gelu_back(activated_grad)[0].astype(jnp.bfloat16)
    bias_up_grad = column_sum(hidden_grad)
    w_up_grad = outer_product(normed_low, hidden_grad)
    normed_grad = back_product(hidden_grad, w_up) + second_grad
    first_grad, gain_one_grad, shift_one_grad = norm_one_back(normed_grad)
    branch_grad = first_grad.astype(jnp.bfloat16)
    bias_o_grad = column_sum(branch_grad)
    w_out_grad = outer_product(context, branch_grad)
    context_grad = (
        back_product(branch_grad, w_out)
        .astype(jnp.bfloat16)
        .reshape(row_count, seq_len, HEADS, HEAD_DIM)
    )
    probs = jnp.exp(masked_scores(queries, key_heads, segment_ids, pad_counts) - log_total)
    probs_low = probs.astype(jnp.bfloat16)
    probs_grad = jnp.einsum(
        "rqhd,rkhd->rhqk", context_grad, value_heads, preferred_element_type=jnp.float32
    )
    value_grad = jnp.einsum(
        "rhqk,rqhd->rkhd", probs_low, context_grad, preferred_element_type=jnp.float32
    )
    weighted = jnp.sum(probs * probs_grad, axis=-1, keepdims=True)
    score_grad = (probs * (probs_grad - weighted)).astype(jnp.bfloat16)
    query_grad = jnp.einsum(
        "rhqk,rkhd->rqhd", score_grad, key_heads, preferred_element_type=jnp.float32
    ) * HEAD_DIM ** (-0.5)
    key_grad = jnp.einsum(
        "rhqk,rqhd->rkhd", score_grad, queries, preferred_element_type=jnp.float32
    ) * HEAD_DIM ** (-0.5)
    projected_grad = jnp.concatenate(
        [
            query_grad.reshape(token_count, D),
            key_grad.reshape(token_count, D),
            value_grad.reshape(token_count, D),
        ],
        axis=1,
    ).astype(jnp.bfloat16)
    bias_q_grad = column_sum(projected_grad[:, 0:D])
    bias_v_grad = column_sum(projected_grad[:, 2 * D : 3 * D])
    w_qkv_grad = outer_product(tokens, projected_grad)
    input_grad = first_grad + back_product(projected_grad, w_qkv)
    gain_terms = jnp.concatenate([gain_one_grad, gain_two_grad])
    bias_terms = jnp.concatenate(
        [
            bias_q_grad,
            bias_v_grad,
            bias_o_grad,
            shift_one_grad,
            bias_up_grad,
            bias_down_grad,
            shift_two_grad,
        ]
    )
    qkv_share, proj_share, up_share, down_share, gain_share, bias_share = (
        lax.psum_scatter(w_qkv_grad, ("gx", "gy"), scatter_dimension=0, tiled=True),
        lax.psum_scatter(w_out_grad, ("gx", "gy"), scatter_dimension=0, tiled=True),
        lax.psum_scatter(w_up_grad, ("gx", "gy"), scatter_dimension=0, tiled=True),
        lax.psum_scatter(w_down_grad, ("gx", "gy"), scatter_dimension=0, tiled=True),
        lax.psum_scatter(gain_terms, ("gx", "gy"), scatter_dimension=0, tiled=True),
        lax.psum_scatter(bias_terms, ("gx", "gy"), scatter_dimension=0, tiled=True),
    )
    qkv_new = update(qkv_share, qkv_master, qkv_moment, qkv_average, tokens_all)
    proj_new = update(proj_share, proj_master, proj_moment, proj_average, tokens_all)
    up_new = update(up_share, up_master, up_moment, up_average, tokens_all)
    down_new = update(down_share, down_master, down_moment, down_average, tokens_all)
    gain_new = update_steps(gain_share, gain_master, gain_moment, gain_average, tokens_all)
    bias_new = update(bias_share, bias_master, bias_moment, bias_average, tokens_all)
    return (
        layer_output,
        input_grad,
        qkv_share,
        proj_share,
        up_share,
        down_share,
        gain_share,
        bias_share,
        qkv_new[0],
        proj_new[0],
        up_new[0],
        down_new[0],
        gain_new[0],
        bias_new[0],
        qkv_new[1],
        proj_new[1],
        up_new[1],
        down_new[1],
        gain_new[1],
        bias_new[1],
        qkv_new[2],
        proj_new[2],
        up_new[2],
        down_new[2],
        gain_new[2],
        bias_new[2],
    )


def solution(mesh):
    in_specs = (
        P(("gx", "gy"), None),
        P(("gx", "gy"), None),
        P(("gx", "gy")),
        P(("gx", "gy"), None),
        P(("gx", "gy"), None),
        P(("gx", "gy"), None),
        P(("gx", "gy"), None),
        P(("gx", "gy"), None),
        P(("gx", "gy")),
        P(("gx", "gy")),
        P(("gx", "gy"), None),
        P(("gx", "gy"), None),
        P(("gx", "gy"), None),
        P(("gx", "gy"), None),
        P(("gx", "gy")),
        P(("gx", "gy")),
        P(("gx", "gy"), None),
        P(("gx", "gy"), None),
        P(("gx", "gy"), None),
        P(("gx", "gy"), None),
        P(("gx", "gy")),
        P(("gx", "gy")),
    )
    out_specs = (
        P(("gx", "gy"), None),
        P(("gx", "gy"), None),
        P(("gx", "gy"), None),
        P(("gx", "gy"), None),
        P(("gx", "gy"), None),
        P(("gx", "gy"), None),
        P(("gx", "gy")),
        P(("gx", "gy")),
        P(("gx", "gy"), None),
        P(("gx", "gy"), None),
        P(("gx", "gy"), None),
        P(("gx", "gy"), None),
        P(("gx", "gy")),
        P(("gx", "gy")),
        P(("gx", "gy"), None),
        P(("gx", "gy"), None),
        P(("gx", "gy"), None),
        P(("gx", "gy"), None),
        P(("gx", "gy")),
        P(("gx", "gy")),
        P(("gx", "gy"), None),
        P(("gx", "gy"), None),
        P(("gx", "gy"), None),
        P(("gx", "gy"), None),
        P(("gx", "gy")),
        P(("gx", "gy")),
    )
    return jax.shard_map(
        on_device, mesh=mesh, in_specs=in_specs, out_specs=out_specs, check_vma=False
    )
```

profile of v0, /device:TPU:0, one launch (start us, length us, event | category | flops | bytes accessed | tf_op | source)
XLA Modules:
  0.0 962.1 jit_solution(8887710263279011707)
XLA Ops:
  15.9 42.4 %all-reduce.5 = (bf16[7680]{0:T(1024)(128)(2,1)S(1)}, bf16[1536]{0:T(1024)(128)(2,1)S(1)}) all-reduce(bf16[7680]{0:T(1024)(128)(2,1)S(1)} %dynamic-update-slice, bf16[1536]{0:T(1024)(128)(2,1)S(1)} %dynamic-update-slice.1), channel_id=1, replica_groups=mesh['gx'=4,'gy'=8] {'gx','gy'}, use_global_device_ids=true, to_apply=%add | all-reduce | flops 9216 | bytes 36864
  74.7 9.9 %add_convert_fusion.1 = bf16[2048,2304]{1,0:T(8,128)(2,1)S(1)} fusion(bf16[2048,768]{1,0:T(8,128)(2,1)S(1)} %copy-done.11, bf16[768,2304]{1,0:T(8,128)(2,1)} %all-gather.5.cloned.1.call-done, f32[2304]{0:T(1024)S(1)} %pad_maximum_fusion), kind=kOutput, calls=%fused_computation.25 | convolution fusion | flops 7257194496 | bytes 16131072 | tf_op jit(solution)/shard_map/dot_general | solution.py:128
  117.8 22.4 %fusion = (f32[4,12,512]{2,1,0:T(8,128)S(1)}, f32[4,12,512,512]{2,3,1,0:T(8,128)}) fusion(pred[4,512,512]{1,2,0:T(8,128)(4,1)} %compare_and_fusion, bf16[4,512,12,64]{1,0,3,2:T(4,128)(2,1)} %reshape.199, bf16[4,512,12,64]{1,0,3,2:T(4,128)(2,1)S(1)} %reshape.198), kind=kOutput, calls=%fused_computation.5 | convolution fusion | flops 1648336896 | bytes 57769984 | tf_op jit(solution)/shard_map/rqhd,rkhd->rhqk/dot_general | solution.py:50
  140.2 21.4 %exponential_reduce_fusion = f32[4,12,512]{2,1,0:T(8,128)S(1)} fusion(f32[4,12,512,512]{2,3,1,0:T(8,128)} %get-tuple-element.185, f32[4,12,512]{2,1,0:T(8,128)S(1)} %get-tuple-element.184, pred[4,512,512]{1,2,0:T(8,128)(4,1)S(1)} %copy-done.6), kind=kLoop, calls=%fused_computation.3 | loop fusion | flops 50307072 | bytes 51576832 | tf_op jit(solution)/shard_map/reduce_sum | solution.py:137
  161.7 20.8 %convert_bitcast_fusion.1 = bf16[4,512,12,64]{1,3,2,0:T(8,128)(2,1)S(1)} fusion(bf16[4,512,12,64]{1,0,3,2:T(4,128)(2,1)S(1)} %copy-done.9, f32[4,12,512,512]{2,3,1,0:T(8,128)} %get-tuple-element.185, f32[4,12,512]{2,1,0:T(8,128)S(1)} %log_add_fusion, pred[4,512,512]{1,2,0:T(8,128)(4,1)S(1)} %copy-done.6), kind=kOutput, calls=%fused_computation.60 | convolution fusion | flops 1662517248 | bytes 57769984 | tf_op jit(solution)/shard_map/rhqk,rkhd->rqhd/dot_general | solution.py:140
  186.0 6.7 fusion.55
  197.5 70.2 %multiply_convert_fusion.1 = (bf16[2048,3072]{1,0:T(8,128)(2,1)}, f32[2048,3072]{1,0:T(8,128)}, f32[2048,3072]{1,0:T(8,128)}) fusion(f32[3072]{0:T(1024)S(1)} %slice.58, bf16[768,3072]{1,0:T(8,128)(2,1)} %all-gather.9.cloned.1.call-done, bf16[2048,768]{0,1:T(8,128)(2,1)S(1)} %fusion.48.clone.4), kind=kOutput, calls=%fused_computation.11 | convolution fusion | flops 10078912512 | bytes 70791168 | tf_op jit(solution)/shard_map/dot_general | solution.py:147
  267.8 18.1 %fusion.56 = (f32[2048]{0:T(1024)S(1)}, f32[2048,768]{0,1:T(8,128)}) fusion(f32[768]{0:T(1024)S(1)} %copy-done.45, bf16[2048,3072]{1,0:T(8,128)(2,1)} %get-tuple-element.168, bf16[3072,768]{1,0:T(8,128)(2,1)} %all-gather.11.cloned.1.call-done, f32[768]{0:T(1024)S(1)} %copy-done.38, f32[768]{0:T(1024)S(1)} %copy-done.31, f32[2048]{0:T(1024)S(1)} %copy-done.27, ...), kind=kOutput, calls=%fused_computation.130 | convolution fusion | flops 9674684416 | bytes 29918208 | tf_op jit(solution)/shard_map/dot_general | solution.py:150
  301.1 33.5 %convert_reduce_fusion = (f32[3072]{0:T(1024)}, bf16[2048,3072]{1,0:T(8,128)(2,1)}) fusion(f32[2048,3072]{1,0:T(8,128)} %get-tuple-element.169, bf16[2048,768]{0,1:T(8,128)(2,1)} %get-tuple-element.163, bf16[3072,768]{1,0:T(8,128)(2,1)} %all-gather.11.cloned.1.call-done, f32[2048,3072]{1,0:T(8,128)} %get-tuple-element.188, f32[3072]{0:T(1024)S(1)} %slice.58), kind=kOutput, calls=%fused_computation.9 | convolution fusion | flops 9770628096 | bytes 70803456 | tf_op jit(solution)/shard_map/dot_general | solution.py:34
  334.6 20.8 %multiply_reduce_fusion.1 = (f32[768]{0:T(1024)}, f32[2048]{0:T(1024)S(1)}, f32[768]{0:T(1024)}, f32[2048,768]{0,1:T(8,128)S(1)}) fusion(f32[2048,768]{0,1:T(8,128)} %copy-done, f32[2048]{0:T(1024)S(1)} %copy-done.27, f32[2048]{0:T(1024)S(1)} %copy-done.22, f32[768]{0:T(1024)S(1)} %copy-done.31, f32[2048]{0:T(1024)S(1)} %negate_multiply_fusion.2, ...), kind=kOutput, calls=%fused_computation.39 | convolution fusion | flops 9690411008 | bytes 39391232 | tf_op jit(solution)/shard_map/dot_general | solution.py:34
  384.1 23.1 %convert_bitcast_fusion = bf16[4,512,12,64]{1,3,2,0:T(8,128)(2,1)} fusion(bf16[4,512,12,64]{1,0,3,2:T(4,128)(2,1)} %reshape.200, f32[4,12,512,512]{2,3,1,0:T(8,128)} %get-tuple-element.185, f32[4,12,512]{2,1,0:T(8,128)S(1)} %copy-done.18, pred[4,512,512]{1,2,0:T(8,128)(4,1)S(1)} %copy-done.7), kind=kOutput, calls=%fused_computation.59 | convolution fusion | flops 1662517248 | bytes 57769984 | tf_op jit(solution)/shard_map/rhqk,rqhd->rkhd/dot_general | solution.py:183
  407.2 38.5 %multiply_reduce_fusion = (f32[4,12,512]{2,1,0:T(8,128)S(1)}, f32[4,12,512,512]{2,3,1,0:T(8,128)}) fusion(f32[4,12,512,512]{2,3,1,0:T(8,128)} %get-tuple-element.185, f32[4,12,512]{2,1,0:T(8,128)S(1)} %copy-done.18, pred[4,512,512]{1,2,0:T(8,128)(4,1)S(1)} %copy-done.7, bf16[4,512,12,64]{1,0,3,2:T(4,128)(2,1)} %reshape.197, ...), kind=kOutput, calls=%fused_computation.1 | convolution fusion | flops 1673502720 | bytes 108199936 | tf_op jit(solution)/shard_map/rqhd,rkhd->rhqk/dot_general | solution.py:180
  445.8 42.3 %multiply_convert_fusion = bf16[4,12,512,512]{2,3,1,0:T(8,128)(2,1)} fusion(f32[4,12,512,512]{2,3,1,0:T(8,128)} %get-tuple-element.193, f32[4,12,512,512]{2,3,1,0:T(8,128)} %get-tuple-element.185, f32[4,12,512]{2,1,0:T(8,128)S(1)} %get-tuple-element.192, f32[4,12,512]{2,1,0:T(8,128)S(1)} %copy-done.18, pred[4,512,512]{1,2,0:T(8,128)(4,1)} %compare_and_fusion), kind=kLoop, calls=%fused_computation | loop fusion | flops 75497472 | bytes 127074304 | tf_op jit(solution)/shard_map/convert_element_type | solution.py:187
  488.2 13.7 %fusion.14 = bf16[4,512,12,64]{1,3,2,0:T(8,128)(2,1)} fusion(bf16[4,12,512,512]{2,3,1,0:T(8,128)(2,1)} %multiply_convert_fusion, bf16[4,512,12,64]{1,0,3,2:T(4,128)(2,1)S(1)} %copy-done.4), kind=kOutput, calls=%fused_computation.58 | convolution fusion | flops 1613758464 | bytes 31457280 | tf_op jit(solution)/shard_map/rhqk,rqhd->rkhd/dot_general | solution.py:191
  501.9 13.5 %fusion.13 = bf16[4,512,12,64]{1,3,2,0:T(8,128)(2,1)S(1)} fusion(bf16[4,12,512,512]{2,3,1,0:T(8,128)(2,1)} %multiply_convert_fusion, bf16[4,512,12,64]{1,0,3,2:T(4,128)(2,1)} %reshape.199), kind=kOutput, calls=%fused_computation.57 | convolution fusion | flops 1613758464 | bytes 31457280 | tf_op jit(solution)/shard_map/rhqk,rkhd->rqhd/dot_general | solution.py:188
  530.7 9.6 convolution_bitcast_fusion
  540.3 8.0 copy.173
  548.4 16.2 %fusion.58 = f32[3072,768]{1,0:T(8,128)} fusion(bf16[2048,3072]{1,0:T(8,128)(2,1)} %get-tuple-element.168, bf16[2048,768]{0,1:T(8,128)(2,1)} %get-tuple-element.163), kind=kOutput, calls=%fused_computation.132 | convolution fusion | flops 9663676416 | bytes 25165824 | tf_op jit(solution)/shard_map/dot_general | solution.py:28
  565.3 17.7 %fusion.45 = f32[768,3072]{1,0:T(8,128)} fusion(bf16[2048,3072]{1,0:T(8,128)(2,1)} %get-tuple-element.195, f32[2048,768]{0,1:T(8,128)} %copy-done, f32[768]{0:T(1024)S(1)} %copy-done.39, f32[768]{0:T(1024)S(1)} %copy-done.32, f32[2048]{0:T(1024)S(1)} %copy-done.28, f32[2048]{0:T(1024)S(1)} %copy-done.23), kind=kOutput, calls=%fused_computation.122 | convolution fusion | flops 9671540736 | bytes 28334080 | tf_op jit(solution)/shard_map/dot_general | solution.py:28
  587.8 14.2 %add_add_fusion.4 = f32[2048,768]{0,1:T(8,128)} fusion(f32[2048,768]{0,1:T(8,128)} %copy-done.8, bf16[768,2304]{1,0:T(8,128)(2,1)} %all-gather.5.cloned.1.call-done, bf16[2048,2304]{0,1:T(8,128)(2,1)} %copy-done.19, f32[2048]{0:T(1024)S(1)} %copy-done.35), kind=kOutput, calls=%fused_computation.49 | convolution fusion | flops 7250903040 | bytes 25567232 | tf_op jit(solution)/shard_map/dot_general | solution.py:34
  611.9 40.4 %all-reduce.4 = (f32[1536]{0:T(1024)S(1)}, f32[7680]{0:T(1024)S(1)}) all-reduce(f32[1536]{0:T(1024)S(1)} %pad_maximum_fusion.1, f32[7680]{0:T(1024)S(1)} %constant_dynamic-update-slice_fusion.6), channel_id=6, replica_groups=mesh['gx'=4,'gy'=8] {'gx','gy'}, use_global_device_ids=true, to_apply=%region_17.18.clone | all-reduce | flops 9216 | bytes 73728
  656.7 12.6 %reduce-scatter.13.cloned.1.call-done = f32[24,2304]{1,0:T(8,128)} async-done(((f32[768,2304]{1,0:T(8,128)}), f32[24,2304]{1,0:T(8,128)}) %reduce-scatter.13.cloned.1.call-update) | async-done | bytes 221200
  671.4 139.0 %reduce-scatter.11.cloned.1.call-done = f32[96,768]{1,0:T(8,128)} async-done(((f32[3072,768]{1,0:T(8,128)}), f32[96,768]{1,0:T(8,128)}) %reduce-scatter.11.cloned.1.call-update) | async-done | bytes 294928 | tf_op jit(solution)/shard_map/reduce_scatter | solution.py:222
  812.5 140.1 %reduce-scatter.9.cloned.1.call-done = f32[24,3072]{1,0:T(8,128)} async-done(((f32[768,3072]{1,0:T(8,128)}), f32[24,3072]{1,0:T(8,128)}) %reduce-scatter.9.cloned.1.call-update) | async-done | bytes 294928 | tf_op jit(solution)/shard_map/reduce_scatter | solution.py:221
  (197 shorter events, 151.6 us)
Async XLA Ops:
  7.2 57.7 %copy-start.11 = (bf16[2048,768]{1,0:T(8,128)(2,1)S(1)}, bf16[2048,768]{1,0:T(8,128)(2,1)}, u32[]{:S(2)}) copy-start(bf16[2048,768]{1,0:T(8,128)(2,1)} %param.22) | copy-start | bytes 9437188
  7.2 67.4 %all-gather.5.cloned.1.call-start = ((), (), s32[]{:S(2)}) async-start(), calls=%async_computation.4 | async-start | bytes 3649536 | tf_op jit(solution)/shard_map/all_gather | solution.py:108
  9.0 177.0 %all-gather.7.cloned.1.call-start = ((), (), s32[]{:S(2)}) async-start(), calls=%async_computation.5 | async-start | bytes 1216512 | tf_op jit(solution)/shard_map/all_gather | solution.py:109
  10.6 186.9 %all-gather.9.cloned.1.call-start = ((), (), s32[]{:S(2)}) async-start(), calls=%async_computation.6 | async-start | bytes 4866048 | tf_op jit(solution)/shard_map/all_gather | solution.py:110
  12.3 255.4 %all-gather.11.cloned.1.call-start = ((), (), s32[]{:S(2)}) async-start(), calls=%async_computation.7 | async-start | bytes 4866048 | tf_op jit(solution)/shard_map/all_gather | solution.py:111
  14.0 640.9 %reduce-scatter.7.cloned.1.call-start = ((), (), s32[]{:S(2)}) async-start(), calls=%async_computation.8 | async-start | bytes 2433024 | tf_op jit(solution)/shard_map/reduce_scatter | solution.py:220
  58.9 135.6 %copy-start.37 = (f32[768]{0:T(1024)}, f32[768]{0:T(1024)S(1)}, u32[]{:S(2)}) copy-start(f32[768]{0:T(1024)S(1)} %get-tuple-element.176) | copy-start | bytes 9220
  60.2 134.3 %copy-start.30 = (f32[768]{0:T(1024)}, f32[768]{0:T(1024)S(1)}, u32[]{:S(2)}) copy-start(f32[768]{0:T(1024)S(1)} %get-tuple-element.183) | copy-start | bytes 9220
  95.4 22.5 %copy-start.3 = (bf16[4,512,12,64]{1,0,3,2:T(4,128)(2,1)}, bf16[4,512,12,64]{1,0,3,2:T(4,128)(2,1)S(1)}, u32[]{:S(2)}) copy-start(bf16[4,512,12,64]{1,0,3,2:T(4,128)(2,1)S(1)} %reshape.198) | copy-start | bytes 9437188
  117.8 22.4 %copy-start.6 = (pred[4,512,512]{1,2,0:T(8,128)(4,1)S(1)}, pred[4,512,512]{1,2,0:T(8,128)(4,1)}, u32[]{:S(2)}) copy-start(pred[4,512,512]{1,2,0:T(8,128)(4,1)} %compare_and_fusion) | copy-start | bytes 3145732
  140.2 21.5 %copy-start.9 = (bf16[4,512,12,64]{1,0,3,2:T(4,128)(2,1)S(1)}, bf16[4,512,12,64]{1,0,3,2:T(4,128)(2,1)}, u32[]{:S(2)}) copy-start(bf16[4,512,12,64]{1,0,3,2:T(4,128)(2,1)} %reshape.197) | copy-start | bytes 9437188
  197.5 70.2 %copy-start.22 = (f32[2048]{0:T(1024)S(1)}, f32[2048]{0:T(1024)}, u32[]{:S(2)}) copy-start(f32[2048]{0:T(1024)} %copy-done.21) | copy-start | bytes 24580
  197.5 70.2 %copy-start.27 = (f32[2048]{0:T(1024)S(1)}, f32[2048]{0:T(1024)}, u32[]{:S(2)}) copy-start(f32[2048]{0:T(1024)} %copy-done.26) | copy-start | bytes 24580
  197.5 70.2 %copy-start.31 = (f32[768]{0:T(1024)S(1)}, f32[768]{0:T(1024)}, u32[]{:S(2)}) copy-start(f32[768]{0:T(1024)} %copy-done.30) | copy-start | bytes 9220
  197.5 70.2 %copy-start.38 = (f32[768]{0:T(1024)S(1)}, f32[768]{0:T(1024)}, u32[]{:S(2)}) copy-start(f32[768]{0:T(1024)} %copy-done.37) | copy-start | bytes 9220
  197.5 70.3 %copy-start.45 = (f32[768]{0:T(1024)S(1)}, f32[768]{0:T(1024)}, u32[]{:S(2)}) copy-start(f32[768]{0:T(1024)} %get-tuple-element.175) | copy-start | bytes 9220
  445.8 223.4 %reduce-scatter.13.cloned.1.call-start = ((), (), s32[]{:S(2)}) async-start(), calls=%async_computation.11 | async-start | bytes 7299072
  445.8 42.3 %copy-start.4 = (bf16[4,512,12,64]{1,0,3,2:T(4,128)(2,1)S(1)}, bf16[4,512,12,64]{1,0,3,2:T(4,128)(2,1)}, u32[]{:S(2)}) copy-start(bf16[4,512,12,64]{1,0,3,2:T(4,128)(2,1)} %copy-done.3) | copy-start | bytes 9437188
  548.3 262.1 %reduce-scatter.11.cloned.1.call-start = ((), (), s32[]{:S(2)}) async-start(), calls=%async_computation.10 | async-start | bytes 9732096 | tf_op jit(solution)/shard_map/reduce_scatter | solution.py:222
  564.6 388.0 %reduce-scatter.9.cloned.1.call-start = ((), (), s32[]{:S(2)}) async-start(), calls=%async_computation.9 | async-start | bytes 9732096 | tf_op jit(solution)/shard_map/reduce_scatter | solution.py:221
  608.7 44.9 %copy-start.48 = (f32[240]{0:T(256)S(1)}, f32[240]{0:T(256)}, u32[]{:S(2)}) copy-start(f32[240]{0:T(256)} %param.31) | copy-start | bytes 2884
  608.8 44.9 %copy-start.49 = (f32[240]{0:T(256)S(1)}, f32[240]{0:T(256)}, u32[]{:S(2)}) copy-start(f32[240]{0:T(256)} %param.43) | copy-start | bytes 2884
  608.8 46.2 %copy-start.20 = (f32[24,768]{1,0:T(8,128)S(1)}, f32[24,768]{1,0:T(8,128)}, u32[]{:S(2)}) copy-start(f32[24,768]{1,0:T(8,128)} %param.27) | copy-start | bytes 221188
  608.8 201.6 %copy-start.16 = (f32[96,768]{1,0:T(8,128)S(1)}, f32[96,768]{1,0:T(8,128)}, u32[]{:S(2)}) copy-start(f32[96,768]{1,0:T(8,128)} %param.29) | copy-start | bytes 884740
  (34 other events, 202.4 us)
Sparse Core Ops, SparseCore 0:
  11.6 62.9 all-gather.4
  78.2 52.9 all-gather.6
  134.9 62.5 all-gather.8
  200.9 62.4 all-gather.10
  445.9 97.8 reduce-scatter.6
  550.9 118.3 reduce-scatter.12
  675.7 134.6 reduce-scatter.10
  817.9 134.7 reduce-scatter.8
where the time goes:
time: 973 us; the launch traced here: 962 us
  matrix products  358 us (37%)
  waiting for transfers between devices  298 us (31%)
  other arithmetic  110 us (11%)
  local copies, waits for them, and re-layouts  97.5 us (10%)
  blocking collectives  82.8 us (9%)
  between operations  15.3 us (2%)
    reduce_scatter x1, waiting for transfers between devices, on_device(): lax.psum_scatter(w_up_grad, ('gx', 'gy'), scatter_dimension=0, tiled=True)  140 us
    reduce_scatter x1, waiting for transfers between devices, on_device(): lax.psum_scatter(w_down_grad, ('gx', 'gy'), scatter_dimension=0, tiled=True)  139 us
    unnamed x2, blocking collectives  82.8 us
    dot_general x4, matrix products, back_product(): lax.dot_general(grads, weight, (((1,), (1,)), ((), ())), preferred_elemen...  73.8 us
    dot_general x1, matrix products, on_device(): jnp.dot(normed_low, w_up, preferred_element_type=jnp.float32) + bias_up  70.2 us
    dot_general x4, matrix products, outer_product(): lax.dot_general(left, right, (((0,), (0,)), ((), ())), preferred_element_...  47.6 us
    convert_element_type x1, other arithmetic, on_device(): score_grad = (probs * (probs_grad - weighted)).astype(jnp.bfloat16)  42.3 us
    unnamed x121, local copies, waits for them, and re-layouts  41.8 us
  transfers between devices with their start and end apart: 8, of which 5 were waited for; matrix products, arithmetic and copies ran while one was open for 39% of the time, Pallas kernels for 0%

commit v1 on v0

v1 whole, which is shorter than its diff:
```python
from functools import partial

import jax
import jax.numpy as jnp
from jax import lax
from jax.experimental import pallas as pl
from jax.experimental.pallas import tpu as pltpu
from jax.sharding import PartitionSpec as P

D = 768
HEADS = 12
HEAD_DIM = 64
FF = 3072
SEQ = 512
BAND = 128
PACK = 4
GROUPS = HEADS // PACK
WIDE = PACK * HEAD_DIM
VMEM = 60 * 1024 * 1024

norm_eps = 1e-06
momentum_coef = 0.9
learn_rate = 4.0
average_keep = 0.9

G1, G2, BQ, BV, BO, C1, B1, B2, C2 = (
    0, 768, 1536, 2304, 3072, 3840, 4608, 7680, 8448,
)
VEC = 9216

f32 = jnp.float32
bf16 = jnp.bfloat16

LOG2E = 1.4426950408889634
SCORE = HEAD_DIM ** (-0.5) * LOG2E


def nn(a, b):
    return lax.dot_general(a, b, (((1,), (0,)), ((), ())), preferred_element_type=f32)


def nt(a, b):
    return lax.dot_general(a, b, (((1,), (1,)), ((), ())), preferred_element_type=f32)


def tn(a, b):
    return lax.dot_general(a, b, (((0,), (0,)), ((), ())), preferred_element_type=f32)


def normal_cdf(u):
    t = 1.0 / (1.0 + 0.28 * jnp.abs(u))
    gauss = jnp.exp2(u * u * (-0.5 * LOG2E))
    q = -0.10568755
    for k in (0.38938334, -0.23620046, 0.26827342, 0.0677507, 0.11648054):
        q = q * t + k
    tail = q * t * gauss
    return jnp.where(u >= 0, 1.0 - tail, tail), gauss


def windows():
    for b in range(SEQ // BAND):
        first = max(0, (b - 1) * BAND)
        last = min(SEQ, (b + 2) * BAND)
        yield b, first, last - first


def head_masks():
    lane = lax.broadcasted_iota(jnp.int32, (BAND, WIDE), 1) // HEAD_DIM
    return [jnp.where(lane == h, 1.0, 0.0).astype(bf16) for h in range(PACK)]


def spread_heads(block, masks):
    return jnp.concatenate([block * m for m in masks], axis=0)


def pick_heads(wide):
    return jnp.concatenate(
        [
            wide[h * HEAD_DIM : (h + 1) * HEAD_DIM, h * BAND : (h + 1) * BAND]
            for h in range(PACK)
        ],
        axis=0,
    )


def mask_bias(col, row, b, first, width):
    keys = col[first : first + width, :]
    queries = row[0:1, b * BAND : (b + 1) * BAND]
    bias = jnp.where(keys == queries, 0.0, -1e30)
    return jnp.concatenate([bias] * PACK, axis=1)


def norm_stats(y):
    centre = jnp.mean(y, axis=-1, keepdims=True)
    centred = y - centre
    spread = jnp.mean(centred * centred, axis=-1, keepdims=True)
    r = lax.rsqrt(spread + norm_eps)
    return centred * r, r


def norm_back(dz, z, r):
    return r * (
        dz
        - jnp.mean(dz, axis=-1, keepdims=True)
        - z * jnp.mean(dz * z, axis=-1, keepdims=True)
    )


def fold_rows(v):
    n = v.shape[0]
    return jnp.sum(v.reshape(n // 8, 8, v.shape[1]), axis=0)


def front_kernel(
    x_ref, row_ref, col_ref, vec_ref, wqkv_ref, wo_ref, w1_ref,
    q_ref, k_ref, v_ref, lse_ref, c_ref, y1_ref, n1_ref, g_ref, gp_ref,
    c_all,
):
    s = pl.program_id(0)

    @pl.when(s < GROUPS * 4)
    def _():
        hg = s // 4
        r = s % 4
        rows = pl.multiple_of(r * SEQ, SEQ)
        lanes = pl.multiple_of(hg * WIDE, WIDE)
        xr = x_ref[pl.ds(rows, SEQ), :]
        q = nn(xr, wqkv_ref[hg, :, 0:WIDE]) + vec_ref[0:1, pl.ds(BQ + lanes, WIDE)]
        q = q.astype(bf16)
        k = nn(xr, wqkv_ref[hg, :, WIDE : 2 * WIDE]).astype(bf16)
        v = nn(xr, wqkv_ref[hg, :, 2 * WIDE :]) + vec_ref[0:1, pl.ds(BV + lanes, WIDE)]
        v = v.astype(bf16)
        q_ref[...] = q
        k_ref[...] = k
        v_ref[...] = v
        vt = v.T
        masks = head_masks()
        for b, first, width in windows():
            qc = spread_heads(q[b * BAND : (b + 1) * BAND, :], masks)
            t = nt(k[first : first + width, :], qc) * SCORE
            t = t + mask_bias(col_ref.at[0], row_ref.at[0], b, first, width)
            m = jnp.max(t, axis=0, keepdims=True)
            e = jnp.exp2(t - m)
            l = jnp.sum(e, axis=0, keepdims=True)
            p = (e * (1.0 / l)).astype(bf16)
            lse_ref[0, b : b + 1, :] = m + jnp.log2(l)
            ot = nn(vt[:, first : first + width], p)
            c = pick_heads(ot).T.astype(bf16)
            c_all[pl.ds(rows + b * BAND, BAND), pl.ds(lanes, WIDE)] = c

    @pl.when(s >= GROUPS * 4)
    def _():
        r = s - GROUPS * 4
        rows = pl.multiple_of(r * SEQ, SEQ)
        c = c_all[pl.ds(rows, SEQ), :]
        c_ref[...] = c
        y1 = x_ref[pl.ds(rows, SEQ), :].astype(f32) + (
            nn(c, wo_ref[...]) + vec_ref[0:1, BO : BO + D]
        )
        y1_ref[...] = y1
        z1, _ = norm_stats(y1)
        n1 = (z1 * vec_ref[0:1, G1 : G1 + D] + vec_ref[0:1, C1 : C1 + D]).astype(bf16)
        n1_ref[...] = n1
        step = 768
        for f in range(0, FF, step):
            u = nn(n1, w1_ref[:, f : f + step]) + vec_ref[0:1, B1 + f : B1 + f + step]
            cdf, gauss = normal_cdf(u)
            g_ref[:, f : f + step] = (u * cdf).astype(bf16)
            gp_ref[:, f : f + step] = (cdf + u * (gauss * 0.3989422804014327)).astype(bf16)


def front(x, row_codes, col_codes, vec, wqkv, wo, w1):
    tokens = x.shape[0]
    rows = tokens // SEQ
    steps = GROUPS * rows + rows
    assert rows == 4
    att = GROUPS * rows

    def one(shape):
        return pl.BlockSpec(shape, lambda s: (0,) * len(shape), pipeline_mode=pl.Buffered(1))

    def code_at(s):
        return (jnp.where(s < att, s % rows, rows - 1), 0, 0)

    def head_at(s):
        return (jnp.where(s < att, s % rows, rows - 1), jnp.minimum(s // rows, GROUPS - 1))

    def lse_at(s):
        return (jnp.minimum(s, att - 1), 0, 0)

    def tile_at(s):
        return (jnp.maximum(s - att, 0), 0)

    return pl.pallas_call(
        front_kernel,
        grid=(steps,),
        in_specs=[
            one((tokens, D)),
            pl.BlockSpec((1, 8, SEQ), code_at),
            pl.BlockSpec((1, SEQ, BAND), code_at),
            one((1, VEC)),
            one((GROUPS, D, 3 * WIDE)),
            one((D, D)),
            one((D, FF)),
        ],
        out_specs=[
            pl.BlockSpec((SEQ, WIDE), head_at),
            pl.BlockSpec((SEQ, WIDE), head_at),
            pl.BlockSpec((SEQ, WIDE), head_at),
            pl.BlockSpec((1, 8, PACK * BAND), lse_at),
            pl.BlockSpec((SEQ, D), tile_at),
            pl.BlockSpec((SEQ, D), tile_at),
            pl.BlockSpec((SEQ, D), tile_at),
            pl.BlockSpec((SEQ, FF), tile_at),
            pl.BlockSpec((SEQ, FF), tile_at),
        ],
        out_shape=[
            jax.ShapeDtypeStruct((tokens, D), bf16),
            jax.ShapeDtypeStruct((tokens, D), bf16),
            jax.ShapeDtypeStruct((tokens, D), bf16),
            jax.ShapeDtypeStruct((att, 8, PACK * BAND), f32),
            jax.ShapeDtypeStruct((tokens, D), bf16),
            jax.ShapeDtypeStruct((tokens, D), f32),
            jax.ShapeDtypeStruct((tokens, D), bf16),
            jax.ShapeDtypeStruct((tokens, FF), bf16),
            jax.ShapeDtypeStruct((tokens, FF), bf16),
        ],
        scratch_shapes=[pltpu.VMEM((tokens, D), bf16)],
        compiler_params=pltpu.CompilerParams(vmem_limit_bytes=VMEM),
        name="front",
    )(x, row_codes, col_codes, vec, wqkv, wo, w1)


def middle_kernel(
    y1_ref, g_ref, gp_ref, cot_ref, vec_ref, wo_ref, w1_ref, w2_ref,
    out_ref, df_ref, du_ref, dy1_ref, da_ref, dc_ref, sums_ref, ups_ref,
):
    s = pl.program_id(0)

    @pl.when(s == 0)
    def _():
        sums_ref[...] = jnp.zeros_like(sums_ref)
        ups_ref[...] = jnp.zeros_like(ups_ref)

    z1, r1 = norm_stats(y1_ref[...])
    gain1 = vec_ref[0:1, G1 : G1 + D]
    gain2 = vec_ref[0:1, G2 : G2 + D]
    n1 = z1 * gain1 + vec_ref[0:1, C1 : C1 + D]
    y2 = n1 + (nn(g_ref[...], w2_ref[...]) + vec_ref[0:1, B2 : B2 + D])
    z2, r2 = norm_stats(y2)
    out_ref[...] = (z2 * gain2 + vec_ref[0:1, C2 : C2 + D]).astype(bf16)
    e = cot_ref[...].astype(f32)
    sums_ref[0] += fold_rows(e * z2)
    sums_ref[1] += fold_rows(e)
    dy2 = norm_back(e * gain2, z2, r2)
    df = dy2.astype(bf16)
    df_ref[...] = df
    sums_ref[2] += fold_rows(df.astype(f32))
    step = 768
    for f in range(0, FF, step):
        dg = nt(df, w2_ref[f : f + step, :])
        du = (dg * gp_ref[:, f : f + step].astype(f32)).astype(bf16)
        du_ref[:, f : f + step] = du
        ups_ref[:, f : f + step] += fold_rows(du.astype(f32))
    dn1 = nt(du_ref[...], w1_ref[...]) + dy2
    sums_ref[3] += fold_rows(dn1 * z1)
    sums_ref[4] += fold_rows(dn1)
    dy1 = norm_back(dn1 * gain1, z1, r1)
    dy1_ref[...] = dy1
    da = dy1.astype(bf16)
    da_ref[...] = da
    sums_ref[5] += fold_rows(da.astype(f32))
    dc_ref[...] = nt(da, wo_ref[...]).astype(bf16)


def middle(y1, g, gp, cot, vec, wo, w1, w2):
    tokens = y1.shape[0]
    tile = SEQ

    def one(shape):
        return pl.BlockSpec(shape, lambda s: (0,) * len(shape), pipeline_mode=pl.Buffered(1))

    narrow = pl.BlockSpec((tile, D), lambda s: (s, 0))
    wide = pl.BlockSpec((tile, FF), lambda s: (s, 0))
    wide_out = pl.BlockSpec((tile, FF), lambda s: (s, 0))
    return pl.pallas_call(
        middle_kernel,
        grid=(tokens // tile,),
        in_specs=[
            narrow, wide, wide, narrow, one((1, VEC)), one((D, D)), one((D, FF)), one((FF, D)),
        ],
        out_specs=[
            narrow, narrow, wide_out, narrow, narrow, narrow,
            pl.BlockSpec((6, 8, D), lambda s: (0, 0, 0)),
            pl.BlockSpec((8, FF), lambda s: (0, 0)),
        ],
        out_shape=[
            jax.ShapeDtypeStruct((tokens, D), bf16),
            jax.ShapeDtypeStruct((tokens, D), bf16),
            jax.ShapeDtypeStruct((tokens, FF), bf16),
            jax.ShapeDtypeStruct((tokens, D), f32),
            jax.ShapeDtypeStruct((tokens, D), bf16),
            jax.ShapeDtypeStruct((tokens, D), bf16),
            jax.ShapeDtypeStruct((6, 8, D), f32),
            jax.ShapeDtypeStruct((8, FF), f32),
        ],
        compiler_params=pltpu.CompilerParams(vmem_limit_bytes=VMEM),
        name="middle",
    )(y1, g, gp, cot, vec, wo, w1, w2)


def outer_kernel(a_ref, b_ref, o_ref):
    o_ref[...] = tn(a_ref[...], b_ref[...]).astype(o_ref.dtype)


def outer(a, b, dtype, side):
    tokens, m = a.shape
    n = b.shape[1]
    step = 768
    if side == 0:
        grid, a_at, b_at, o_at = m // step, (lambda i: (0, i)), (lambda i: (0, 0)), (lambda i: (i, 0))
    else:
        grid, a_at, b_at, o_at = n // step, (lambda i: (0, 0)), (lambda i: (0, i)), (lambda i: (0, i))
    return pl.pallas_call(
        outer_kernel,
        grid=(grid,),
        in_specs=[pl.BlockSpec((tokens, step), a_at), pl.BlockSpec((tokens, step), b_at)],
        out_specs=pl.BlockSpec((step, step), o_at),
        out_shape=jax.ShapeDtypeStruct((m, n), dtype),
        compiler_params=pltpu.CompilerParams(vmem_limit_bytes=VMEM),
        name="outer",
    )(a, b)


def back_kernel(
    x_ref, row_ref, col_ref, wqkv_ref, q_ref, k_ref, v_ref, dc_ref, lse_ref, dy1_ref,
    dw_ref, dx_ref, sums_ref,
    dqkv, dk_sum, dv_sum,
):
    s = pl.program_id(0)
    att = GROUPS * 4

    @pl.when(s < att)
    def _():
        hg = s // 4
        r = s % 4
        rows = pl.multiple_of(r * SEQ, SEQ)
        kt = k_ref[...].T
        dk_sum[...] = jnp.zeros_like(dk_sum)
        dv_sum[...] = jnp.zeros_like(dv_sum)
        masks = head_masks()

        @pl.when(r == 0)
        def _():
            sums_ref[...] = jnp.zeros_like(sums_ref)

        for b, first, width in windows():
            block = slice(b * BAND, (b + 1) * BAND)
            span = slice(first, first + width)
            qc = spread_heads(q_ref[block, :], masks)
            dcc = spread_heads(dc_ref[block, :], masks)
            t = nt(k_ref[span, :], qc) * SCORE
            t = t + mask_bias(col_ref.at[0], row_ref.at[0], b, first, width)
            p = jnp.exp2(t - lse_ref[0, b : b + 1, :])
            dp = nt(v_ref[span, :], dcc)
            dv_sum[span, :] += nn(p.astype(bf16), dcc)
            pdp = p * dp
            weighted = jnp.sum(pdp, axis=0, keepdims=True)
            ds = (pdp - p * weighted).astype(bf16)
            dk_sum[span, :] += nn(ds, qc)
            dqt = nn(kt[:, span], ds)
            dq = (pick_heads(dqt).T * HEAD_DIM ** (-0.5)).astype(bf16)
            dqkv[hg, pl.ds(rows + b * BAND, BAND), 0:WIDE] = dq
            sums_ref[0, 0] += fold_rows(dq.astype(f32))
        dk = (dk_sum[...] * HEAD_DIM ** (-0.5)).astype(bf16)
        dv = dv_sum[...].astype(bf16)
        dqkv[hg, pl.ds(rows, SEQ), WIDE : 2 * WIDE] = dk
        dqkv[hg, pl.ds(rows, SEQ), 2 * WIDE :] = dv
        sums_ref[0, 1] += fold_rows(dv.astype(f32))

        @pl.when(r == 3)
        def _():
            dw_ref[0] = tn(x_ref[...], dqkv[hg]).astype(dw_ref.dtype)

    @pl.when(s >= att)
    def _():
        rows = pl.multiple_of((s - att) * SEQ, SEQ)
        total = dy1_ref[...]
        for hg in range(GROUPS):
            total = total + nt(dqkv[hg, pl.ds(rows, SEQ), :], wqkv_ref[hg])
        dx_ref[...] = total


def back(x, row_codes, col_codes, wqkv, q, k, v, dc, lse, dy1, dtype):
    tokens = x.shape[0]
    rows = tokens // SEQ
    att = GROUPS * rows
    assert rows == 4

    def one(shape):
        return pl.BlockSpec(shape, lambda s: (0,) * len(shape), pipeline_mode=pl.Buffered(1))

    def code_at(s):
        return (jnp.where(s < att, s % rows, rows - 1), 0, 0)

    def head_at(s):
        return (jnp.where(s < att, s % rows, rows - 1), jnp.minimum(s // rows, GROUPS - 1))

    def group_at(s):
        return (jnp.minimum(s // rows, GROUPS - 1), 0, 0)

    def tile_at(s):
        return (jnp.maximum(s - att, 0), 0)

    head = pl.BlockSpec((SEQ, WIDE), head_at)
    return pl.pallas_call(
        back_kernel,
        grid=(att + rows,),
        in_specs=[
            one((tokens, D)),
            pl.BlockSpec((1, 8, SEQ), code_at),
            pl.BlockSpec((1, SEQ, BAND), code_at),
            one((GROUPS, D, 3 * WIDE)),
            head, head, head, head,
            pl.BlockSpec((1, 8, PACK * BAND), lambda s: (jnp.minimum(s, att - 1), 0, 0)),
            pl.BlockSpec((SEQ, D), tile_at),
        ],
        out_specs=[
            pl.BlockSpec((1, D, 3 * WIDE), group_at),
            pl.BlockSpec((SEQ, D), tile_at),
            pl.BlockSpec((1, 2, 8, WIDE), lambda s: (jnp.minimum(s // rows, GROUPS - 1), 0, 0, 0)),
        ],
        out_shape=[
            jax.ShapeDtypeStruct((GROUPS, D, 3 * WIDE), dtype),
            jax.ShapeDtypeStruct((tokens, D), f32),
            jax.ShapeDtypeStruct((GROUPS, 2, 8, WIDE), f32),
        ],
        scratch_shapes=[
            pltpu.VMEM((GROUPS, tokens, 3 * WIDE), bf16),
            pltpu.VMEM((SEQ, WIDE), f32),
            pltpu.VMEM((SEQ, WIDE), f32),
        ],
        compiler_params=pltpu.CompilerParams(vmem_limit_bytes=VMEM),
        name="back",
    )(x, row_codes, col_codes, wqkv, q, k, v, dc, lse, dy1)


def group_columns(w):
    n = w.shape[0]
    return w.reshape(n, 3, GROUPS, WIDE).transpose(2, 0, 1, 3).reshape(GROUPS, n, 3 * WIDE)


def ungroup_columns(w):
    n = w.shape[1]
    return w.reshape(GROUPS, n, 3, WIDE).transpose(1, 2, 0, 3).reshape(n, 3 * D)


def update(grad, master, moment, average, tokens_all):
    mean_grad = grad / tokens_all
    moment_new = momentum_coef * moment + mean_grad
    step_size = -learn_rate * (mean_grad + momentum_coef * moment_new)
    master_new = master + step_size
    average_new = average_keep * average + (1.0 - average_keep) * master_new
    return (master_new, moment_new, average_new)


def update_steps(grad, master, moment, average, tokens_all):
    mean_grad = grad / tokens_all
    moment_new = momentum_coef * moment + mean_grad
    step_size = -learn_rate * (mean_grad + momentum_coef * moment_new)
    average_step = (1.0 - average_keep) * (master + step_size - average)
    return (step_size, moment_new, average_step)


def on_device(
    tokens, segment_ids, pad_counts, out_cotangent,
    qkv_master, proj_master, up_master, down_master, gain_master, bias_master,
    qkv_moment, proj_moment, up_moment, down_moment, gain_moment, bias_moment,
    qkv_average, proj_average, up_average, down_average, gain_average, bias_average,
):
    axes = ("gx", "gy")
    seq_len = segment_ids.shape[1]
    tokens_all = tokens.shape[0] * lax.axis_size(axes)
    position = jnp.arange(seq_len, dtype=jnp.int32)
    is_pad = position[None, :] >= (seq_len - pad_counts)[:, None]
    codes = segment_ids * 2 + is_pad.astype(jnp.int32)
    row_codes = jnp.broadcast_to(codes[:, None, :], (codes.shape[0], 8, seq_len))
    col_codes = jnp.broadcast_to(codes[:, :, None], (codes.shape[0], seq_len, BAND))

    gather = partial(lax.all_gather, axis_name=axes, tiled=True)
    wqkv = group_columns(gather(qkv_master.astype(bf16), axis=0))
    wo = gather(proj_master.astype(bf16), axis=0)
    w1 = gather(up_master.astype(bf16), axis=0)
    w2 = gather(down_master.astype(bf16), axis=0)
    vec = jnp.concatenate(
        [gather(gain_master.astype(bf16), axis=0), gather(bias_master.astype(bf16), axis=0)]
    ).astype(f32)[None, :]

    q, k, v, lse, c, y1, n1, g, gp = front(tokens, row_codes, col_codes, vec, wqkv, wo, w1)
    layer_output, df, du, dy1, da, dc, sums, ups = middle(
        y1, g, gp, out_cotangent, vec, wo, w1, w2
    )
    dw2 = outer(g, df, f32, 0)
    dw1 = outer(n1, du, f32, 1)
    dwo = outer(c, da, f32, 0)
    dwqkv, input_grad, qv_sums = back(
        tokens, row_codes, col_codes, wqkv, q, k, v, dc, lse, dy1, f32
    )
    sums = jnp.sum(sums, axis=1)
    ups = jnp.sum(ups, axis=0)
    qv_sums = jnp.sum(qv_sums, axis=2)
    gain_terms = jnp.concatenate([sums[3], sums[0]])
    bias_terms = jnp.concatenate(
        [
            qv_sums[:, 0].reshape(D), qv_sums[:, 1].reshape(D),
            sums[5], sums[4], ups, sums[2], sums[1],
        ]
    )
    scatter = partial(lax.psum_scatter, axis_name=axes, scatter_dimension=0, tiled=True)
    qkv_share = scatter(ungroup_columns(dwqkv))
    proj_share = scatter(dwo)
    up_share = scatter(dw1)
    down_share = scatter(dw2)
    gain_share = scatter(gain_terms)
    bias_share = scatter(bias_terms)
    qkv_new = update(qkv_share, qkv_master, qkv_moment, qkv_average, tokens_all)
    proj_new = update(proj_share, proj_master, proj_moment, proj_average, tokens_all)
    up_new = update(up_share, up_master, up_moment, up_average, tokens_all)
    down_new = update(down_share, down_master, down_moment, down_average, tokens_all)
    gain_new = update_steps(gain_share, gain_master, gain_moment, gain_average, tokens_all)
    bias_new = update(bias_share, bias_master, bias_moment, bias_average, tokens_all)
    news = (qkv_new, proj_new, up_new, down_new, gain_new, bias_new)
    return (
        layer_output, input_grad,
        qkv_share, proj_share, up_share, down_share, gain_share, bias_share,
        *(n[0] for n in news), *(n[1] for n in news), *(n[2] for n in news),
    )


def solution(mesh):
    both = ("gx", "gy")
    two, one = P(both, None), P(both)
    weights = (two, two, two, two, one, one)
    in_specs = (two, two, one, two) + weights * 3
    out_specs = (two, two) + weights * 4
    return jax.shard_map(
        on_device, mesh=mesh, in_specs=in_specs, out_specs=out_specs, check_vma=False
    )
```

time: 973 us -> 858 us (0.88)
  matrix products: 358 us -> 0 us
  Pallas kernels: 0 us -> 224 us
  waiting for transfers between devices: 298 us -> 476 us
  other arithmetic: 110 us -> 18.5 us
  local copies, waits for them, and re-layouts: 97.5 us -> 38.4 us
    dot_general x18 -> x0, matrix products: 358 us -> none  [the longest x4 73.8 us: back_product(): lax.dot_general(grads, weight, (((1,), (1,)), ((), ())), preferred_elemen...]
    pallas_call x0 -> x6, Pallas kernels: none -> 224 us  [the longest x1 78 us: front(): pl.pallas_call(front_kernel, grid=(steps,), in_specs=[one((tokens, D)), p...]
    all_gather x4, waiting for transfers between devices: 5.69 us -> 125 us  [the longest x1 66.2 us: on_device(): w1 = gather(up_master.astype(bf16), axis=0)]
    unnamed x9, waiting for transfers between devices: 12.7 us -> 71.6 us
    reduce_sum x9 -> x3, other arithmetic: 45.2 us -> 0.1 us  [the longest x1 0.04 us: on_device(): sums = jnp.sum(sums, axis=1)]
    convert_element_type x8 -> x7, other arithmetic: 51.2 us -> 8.38 us  [the longest x1 1.64 us: on_device(): w2 = gather(down_master.astype(bf16), axis=0)]
    unnamed x121 -> x53, local copies, waits for them, and re-layouts: 41.8 us -> 9.22 us
    reshape x4 -> x1, local copies, waits for them, and re-layouts: 23.4 us -> 6.03 us  [group_columns(): w.reshape(n, 3, GROUPS, WIDE).transpose(2, 0, 1, 3)]
  transfers between devices with their start and end apart: 8 -> 8, of which waited for: 5 -> 6; matrix products, arithmetic and copies ran while one was open for 39% -> 6% of each run, Pallas kernels for 0% -> 19%
where the time goes in v1:
time: 858 us; the launch traced here: 854 us
  waiting for transfers between devices  476 us (55%)
  Pallas kernels  224 us (26%)
  blocking collectives  82.4 us (10%)
  local copies, waits for them, and re-layouts  38.4 us (4%)
  other arithmetic  18.5 us (2%)
  between operations  15 us (2%)
    reduce_scatter x1, waiting for transfers between devices, on_device(): up_share = scatter(dw1)  140 us
    reduce_scatter x1, waiting for transfers between devices, on_device(): down_share = scatter(dw2)  139 us
    unnamed x2, blocking collectives  82.4 us
    pallas_call x1, Pallas kernels, front(): pl.pallas_call(front_kernel, grid=(steps,), in_specs=[one((tokens, D)), p...  78 us
    unnamed x9, waiting for transfers between devices  71.6 us
    all_gather x1, waiting for transfers between devices, on_device(): w1 = gather(up_master.astype(bf16), axis=0)  66.2 us
    pallas_call x1, Pallas kernels, back(): pl.pallas_call(back_kernel, grid=(att + rows,), in_specs=[one((tokens, D)...  54.8 us
    pallas_call x1, Pallas kernels, middle(): pl.pallas_call(middle_kernel, grid=(tokens // tile,), in_specs=[narrow, w...  53.8 us
  transfers between devices with their start and end apart: 8, of which 6 were waited for; matrix products, arithmetic and copies ran while one was open for 6% of the time, Pallas kernels for 19%

profile of v1, /device:TPU:0, one launch (start us, length us, event | category | flops | bytes accessed | tf_op | source)
XLA Modules:
  0.0 854.2 jit_solution(13044204362277025174)
XLA Ops:
  12.2 1.6 convert_element_type.38
  15.7 42.4 %all-reduce.5 = (bf16[7680]{0:T(1024)(128)(2,1)S(1)}, bf16[1536]{0:T(1024)(128)(2,1)S(1)}) all-reduce(bf16[7680]{0:T(1024)(128)(2,1)S(1)} %dynamic-update-slice.1, bf16[1536]{0:T(1024)(128)(2,1)S(1)} %dynamic-update-slice), channel_id=1, replica_groups=mesh['gx'=4,'gy'=8] {'gx','gy'}, use_global_device_ids=true, to_apply=%add.1 | all-reduce | flops 9216 | bytes 36864
  60.2 14.5 %all-gather.5.cloned.1.call-done = bf16[768,2304]{1,0:T(8,128)(2,1)} async-done(((bf16[24,2304]{1,0:T(8,128)(2,1)}), bf16[768,2304]{1,0:T(8,128)(2,1)}) %all-gather.5.cloned.1.call-update) | async-done | bytes 3538960 | tf_op jit(solution)/shard_map/all_gather | solution.py:491
  74.7 4.5 copy.76
  79.2 2.1 copy.77
  81.3 6.0 copy.78.wqkv_ref
  87.3 44.0 %all-gather.7.cloned.1.call-done.wo_ref = bf16[768,768]{1,0:T(8,128)(2,1)} async-done(((bf16[24,768]{1,0:T(8,128)(2,1)}), bf16[768,768]{1,0:T(8,128)(2,1)}) %all-gather.7.cloned.1.call-update) | async-done | bytes 1179664 | tf_op jit(solution)/shard_map/all_gather | solution.py:492
  131.3 66.2 %all-gather.9.cloned.1.call-done.w1_ref = bf16[768,3072]{1,0:T(8,128)(2,1)} async-done(((bf16[24,3072]{1,0:T(8,128)(2,1)}), bf16[768,3072]{1,0:T(8,128)(2,1)}) %all-gather.9.cloned.1.call-update) | async-done | bytes 4718608 | tf_op jit(solution)/shard_map/all_gather | solution.py:493
  199.5 78.0 %front.1 = (bf16[2048,768]{1,0:T(8,128)(2,1)}, bf16[2048,768]{1,0:T(8,128)(2,1)}, bf16[2048,768]{1,0:T(8,128)(2,1)}, f32[12,8,512]{2,1,0:T(8,128)}, bf16[2048,76...) custom-call(bf16[2048,768]{1,0:T(8,128)(2,1)} %x_ref.3, ...), custom_call_target="tpu_custom_call" | custom-call | tf_op jit(solution)/shard_map/front/pallas_call | solution.py:194
  277.6 53.8 %middle.1 = (bf16[2048,768]{1,0:T(8,128)(2,1)}, bf16[2048,768]{1,0:T(8,128)(2,1)}, bf16[2048,3072]{1,0:T(8,128)(2,1)}, f32[2048,768]{1,0:T(8,128)}, bf16[2048,76...) custom-call(f32[2048,768]{1,0:T(8,128)} %get-tuple-element.46.y1_ref, ...), custom_call_target="tpu_custom_call" | custom-call | tf_op jit(solution)/shard_map/middle/pallas_call | solution.py:286
  331.3 6.9 outer.3
  338.3 54.8 %back.1 = (f32[3,768,768]{2,1,0:T(8,128)}, f32[2048,768]{1,0:T(8,128)}, f32[3,2,8,256]{3,2,1,0:T(8,128)}) custom-call(bf16[2048,768]{1,0:T(8,128)(2,1)} %x_ref.3, s32[4,8,512]{2,1,0:T(8,128)} %broadcast_in_dim.4.row_ref, s32[4,512,128]{2,1,0:T(8,128)} %broadcast_in_dim.5.col_ref, bf16[3,768,768]{2,1,0:T(8,128)(2,1)} %copy.78.wqkv_ref, ...), custom_call_target="tpu_custom_call" | custom-call | tf_op jit(solution)/shard_map/back/pallas_call | solution.py:416
  393.1 8.1 copy.80
  401.2 6.4 copy.81
  407.6 8.1 copy.84
  415.7 15.0 %outer.5 = f32[3072,768]{1,0:T(8,128)} custom-call(bf16[2048,3072]{1,0:T(8,128)(2,1)} %get-tuple-element.47.g_ref.a_ref, bf16[2048,768]{1,0:T(8,128)(2,1)} %get-tuple-element.62.b_ref), custom_call_target="tpu_custom_call" | custom-call | tf_op jit(solution)/shard_map/outer/pallas_call | solution.py:324
  430.8 15.2 %outer.4 = f32[768,3072]{1,0:T(8,128)} custom-call(bf16[2048,768]{1,0:T(8,128)(2,1)} %get-tuple-element.60.a_ref, bf16[2048,3072]{1,0:T(8,128)(2,1)} %get-tuple-element.61.b_ref), custom_call_target="tpu_custom_call" | custom-call | tf_op jit(solution)/shard_map/outer/pallas_call | solution.py:324
  447.1 40.0 %all-reduce.4 = (f32[1536]{0:T(1024)S(1)}, f32[7680]{0:T(1024)S(1)}) all-reduce(f32[1536]{0:T(1024)S(1)} %pad_maximum_fusion, f32[7680]{0:T(1024)S(1)} %constant_dynamic-update-slice_fusion), channel_id=6, replica_groups=mesh['gx'=4,'gy'=8] {'gx','gy'}, use_global_device_ids=true, to_apply=%region_5.0.clone | all-reduce | flops 9216 | bytes 73728
  490.1 71.4 %reduce-scatter.13.cloned.1.call-done = f32[24,2304]{1,0:T(8,128)} async-done(((f32[768,2304]{1,0:T(8,128)}), f32[24,2304]{1,0:T(8,128)}) %reduce-scatter.13.cloned.1.call-update) | async-done | bytes 221200
  561.5 1.8 multiply_add_fusion.6
  563.4 139.2 %reduce-scatter.11.cloned.1.call-done = f32[96,768]{1,0:T(8,128)} async-done(((f32[3072,768]{1,0:T(8,128)}), f32[96,768]{1,0:T(8,128)}) %reduce-scatter.11.cloned.1.call-update) | async-done | bytes 294928 | tf_op jit(solution)/shard_map/reduce_scatter | solution.py:523
  702.6 1.9 multiply_add_fusion
  704.5 140.4 %reduce-scatter.9.cloned.1.call-done = f32[24,3072]{1,0:T(8,128)} async-done(((f32[768,3072]{1,0:T(8,128)}), f32[24,3072]{1,0:T(8,128)}) %reduce-scatter.9.cloned.1.call-update) | async-done | bytes 294928 | tf_op jit(solution)/shard_map/reduce_scatter | solution.py:522
  844.9 1.9 multiply_add_fusion.1
  (95 shorter events, 14.9 us)
Async XLA Ops:
  7.2 67.5 %all-gather.5.cloned.1.call-start = ((), (), s32[]{:S(2)}) async-start(), calls=%async_computation.4 | async-start | bytes 3649536 | tf_op jit(solution)/shard_map/all_gather | solution.py:491
  8.9 122.4 %all-gather.7.cloned.1.call-start = ((), (), s32[]{:S(2)}) async-start(), calls=%async_computation.5 | async-start | bytes 1216512 | tf_op jit(solution)/shard_map/all_gather | solution.py:492
  10.4 187.1 %all-gather.9.cloned.1.call-start = ((), (), s32[]{:S(2)}) async-start(), calls=%async_computation.6 | async-start | bytes 4866048 | tf_op jit(solution)/shard_map/all_gather | solution.py:493
  12.2 265.4 %all-gather.11.cloned.1.call-start = ((), (), s32[]{:S(2)}) async-start(), calls=%async_computation.7 | async-start | bytes 4866048 | tf_op jit(solution)/shard_map/all_gather | solution.py:494
  13.9 474.6 %reduce-scatter.7.cloned.1.call-start = ((), (), s32[]{:S(2)}) async-start(), calls=%async_computation.8 | async-start | bytes 2433024 | tf_op jit(solution)/shard_map/reduce_scatter | solution.py:521
  338.3 223.3 %reduce-scatter.13.cloned.1.call-start = ((), (), s32[]{:S(2)}) async-start(), calls=%async_computation.11 | async-start | bytes 7299072
  415.6 286.9 %reduce-scatter.11.cloned.1.call-start = ((), (), s32[]{:S(2)}) async-start(), calls=%async_computation.10 | async-start | bytes 9732096 | tf_op jit(solution)/shard_map/reduce_scatter | solution.py:523
  430.7 414.2 %reduce-scatter.9.cloned.1.call-start = ((), (), s32[]{:S(2)}) async-start(), calls=%async_computation.9 | async-start | bytes 9732096 | tf_op jit(solution)/shard_map/reduce_scatter | solution.py:522
  446.0 41.2 %copy-start.18 = (f32[48]{0:T(128)S(1)}, f32[48]{0:T(128)}, u32[]{:S(2)}) copy-start(f32[48]{0:T(128)} %param.30) | copy-start | bytes 580
  446.0 41.8 %copy-start.15 = (f32[240]{0:T(256)S(1)}, f32[240]{0:T(256)}, u32[]{:S(2)}) copy-start(f32[240]{0:T(256)} %param.31) | copy-start | bytes 2884
  446.0 41.8 %copy-start.16 = (f32[240]{0:T(256)S(1)}, f32[240]{0:T(256)}, u32[]{:S(2)}) copy-start(f32[240]{0:T(256)} %param.43) | copy-start | bytes 2884
  446.0 41.8 %copy-start.17 = (f32[240]{0:T(256)S(1)}, f32[240]{0:T(256)}, u32[]{:S(2)}) copy-start(f32[240]{0:T(256)} %param.37) | copy-start | bytes 2884
  446.0 42.5 %copy-start.3 = (f32[24,768]{1,0:T(8,128)S(1)}, f32[24,768]{1,0:T(8,128)}, u32[]{:S(2)}) copy-start(f32[24,768]{1,0:T(8,128)} %param.27) | copy-start | bytes 221188
  446.0 42.5 %copy-start.12 = (f32[24,768]{1,0:T(8,128)S(1)}, f32[24,768]{1,0:T(8,128)}, u32[]{:S(2)}) copy-start(f32[24,768]{1,0:T(8,128)} %param.39) | copy-start | bytes 221188
  446.0 42.4 %copy-start.13 = (f32[24,768]{1,0:T(8,128)S(1)}, f32[24,768]{1,0:T(8,128)}, u32[]{:S(2)}) copy-start(f32[24,768]{1,0:T(8,128)} %param.33) | copy-start | bytes 221188
  446.1 115.5 %copy-start.2 = (f32[24,2304]{1,0:T(8,128)S(1)}, f32[24,2304]{1,0:T(8,128)}, u32[]{:S(2)}) copy-start(f32[24,2304]{1,0:T(8,128)} %param.26) | copy-start | bytes 663556
  446.1 115.4 %copy-start.8 = (f32[24,2304]{1,0:T(8,128)S(1)}, f32[24,2304]{1,0:T(8,128)}, u32[]{:S(2)}) copy-start(f32[24,2304]{1,0:T(8,128)} %param.38) | copy-start | bytes 663556
  446.1 115.4 %copy-start.9 = (f32[24,2304]{1,0:T(8,128)S(1)}, f32[24,2304]{1,0:T(8,128)}, u32[]{:S(2)}) copy-start(f32[24,2304]{1,0:T(8,128)} %param.32) | copy-start | bytes 663556
  446.1 256.5 %copy-start = (f32[96,768]{1,0:T(8,128)S(1)}, f32[96,768]{1,0:T(8,128)}, u32[]{:S(2)}) copy-start(f32[96,768]{1,0:T(8,128)} %param.29) | copy-start | bytes 884740
  446.1 256.5 %copy-start.4 = (f32[96,768]{1,0:T(8,128)S(1)}, f32[96,768]{1,0:T(8,128)}, u32[]{:S(2)}) copy-start(f32[96,768]{1,0:T(8,128)} %param.41) | copy-start | bytes 884740
  446.1 256.5 %copy-start.5 = (f32[96,768]{1,0:T(8,128)S(1)}, f32[96,768]{1,0:T(8,128)}, u32[]{:S(2)}) copy-start(f32[96,768]{1,0:T(8,128)} %param.35) | copy-start | bytes 884740
  446.2 398.8 %copy-start.1 = (f32[24,3072]{1,0:T(8,128)S(1)}, f32[24,3072]{1,0:T(8,128)}, u32[]{:S(2)}) copy-start(f32[24,3072]{1,0:T(8,128)} %param.28) | copy-start | bytes 884740
  446.2 398.8 %copy-start.6 = (f32[24,3072]{1,0:T(8,128)S(1)}, f32[24,3072]{1,0:T(8,128)}, u32[]{:S(2)}) copy-start(f32[24,3072]{1,0:T(8,128)} %param.40) | copy-start | bytes 884740
  446.2 398.8 %copy-start.7 = (f32[24,3072]{1,0:T(8,128)S(1)}, f32[24,3072]{1,0:T(8,128)}, u32[]{:S(2)}) copy-start(f32[24,3072]{1,0:T(8,128)} %param.34) | copy-start | bytes 884740
  (5 other events, 85.2 us)
Sparse Core Ops, SparseCore 0:
  11.6 63.0 all-gather.4
  78.3 52.9 all-gather.6
  134.9 62.5 all-gather.8
  201.0 62.4 all-gather.10
  338.4 97.8 reduce-scatter.6
  443.3 118.1 reduce-scatter.12
  568.0 134.5 reduce-scatter.10
  710.1 134.8 reduce-scatter.8

commit v2 on v1

v2 whole, which is shorter than its diff:
```python
from functools import partial

import jax
import jax.numpy as jnp
from jax import lax
from jax.experimental import pallas as pl
from jax.experimental.pallas import tpu as pltpu
from jax.sharding import PartitionSpec as P

D = 768
HEADS = 12
HEAD_DIM = 64
FF = 3072
SEQ = 512
BAND = 128
PACK = 4
GROUPS = HEADS // PACK
WIDE = PACK * HEAD_DIM
VMEM = 60 * 1024 * 1024

norm_eps = 1e-06
momentum_coef = 0.9
learn_rate = 4.0
average_keep = 0.9

G1, G2, BQ, BV, BO, C1, B1, B2, C2 = (0, 1, 2, 3, 4, 5, 6, 10, 11)
TABLE = 16
CHUNK = 768
CHUNKS = 12
HALF = CHUNK // 2
MESH = pl.DeviceIdType.MESH

f32 = jnp.float32
bf16 = jnp.bfloat16

LOG2E = 1.4426950408889634
SCORE = HEAD_DIM ** (-0.5) * LOG2E


def nn(a, b):
    return lax.dot_general(a, b, (((1,), (0,)), ((), ())), preferred_element_type=f32)


def nt(a, b):
    return lax.dot_general(a, b, (((1,), (1,)), ((), ())), preferred_element_type=f32)


def tn(a, b):
    return lax.dot_general(a, b, (((0,), (0,)), ((), ())), preferred_element_type=f32)


def normal_cdf(u):
    t = 1.0 / (1.0 + 0.28 * jnp.abs(u))
    gauss = jnp.exp2(u * u * (-0.5 * LOG2E))
    q = -0.10568755
    for k in (0.38938334, -0.23620046, 0.26827342, 0.0677507, 0.11648054):
        q = q * t + k
    tail = q * t * gauss
    return jnp.where(u >= 0, 1.0 - tail, tail), gauss


def windows():
    for b in range(SEQ // BAND):
        first = max(0, (b - 1) * BAND)
        last = min(SEQ, (b + 2) * BAND)
        yield b, first, last - first


def head_masks():
    lane = lax.broadcasted_iota(jnp.int32, (BAND, WIDE), 1) // HEAD_DIM
    return [jnp.where(lane == h, 1.0, 0.0).astype(bf16) for h in range(PACK)]


def spread_heads(block, masks):
    return jnp.concatenate([block * m for m in masks], axis=0)


def pick_heads(wide):
    return jnp.concatenate(
        [
            wide[h * HEAD_DIM : (h + 1) * HEAD_DIM, h * BAND : (h + 1) * BAND]
            for h in range(PACK)
        ],
        axis=0,
    )


def mask_bias(col, row, b, first, width):
    keys = col[first : first + width, :]
    queries = row[0:1, b * BAND : (b + 1) * BAND]
    bias = jnp.where(keys == queries, 0.0, -1e30)
    return jnp.concatenate([bias] * PACK, axis=1)


def norm_stats(y):
    centre = jnp.mean(y, axis=-1, keepdims=True)
    centred = y - centre
    spread = jnp.mean(centred * centred, axis=-1, keepdims=True)
    r = lax.rsqrt(spread + norm_eps)
    return centred * r, r


def norm_back(dz, z, r):
    return r * (
        dz
        - jnp.mean(dz, axis=-1, keepdims=True)
        - z * jnp.mean(dz * z, axis=-1, keepdims=True)
    )


def remote(src, dst, send, recv, device):
    return pltpu.make_async_remote_copy(
        src_ref=src, dst_ref=dst, send_sem=send, recv_sem=recv, device_id=device,
        device_id_type=MESH,
    )


class Place:
    def __init__(self, nz):
        gx = lax.axis_index("gx")
        gy = lax.axis_index("gy")
        self.nz = nz
        self.x, self.y = gx % 2, gx // 2
        self.z, self.c = gy // 2, gy % 2
        x, y, z, c = self.x, self.y, self.z, self.c
        self.other = (gx, z * 2 + 1 - c)
        ax, ay = x + (1 - c) * (1 - 2 * x), y + c * (1 - 2 * y)
        bx, by = x + c * (1 - 2 * x), y + (1 - c) * (1 - 2 * y)
        self.first = (ay * 2 + ax, gy)
        self.second = (by * 2 + bx, gy)
        self.quarter = gx
        self.quarter_first = ay * 2 + ax
        self.quarter_second = by * 2 + bx
        self.quarter_far = (1 - y) * 2 + 1 - x

    def along_z(self, j):
        return (self.quarter, (self.z + j) % self.nz * 2 + self.c)

    def barrier(self):
        sem = pltpu.get_barrier_semaphore()
        partners = [self.other, self.first, self.second]
        partners += [self.along_z(j) for j in range(1, self.nz)]
        for p in partners:
            pl.semaphore_signal(sem, inc=1, device_id=p, device_id_type=MESH)
        pl.semaphore_wait(sem, len(partners))


def fold_rows(v):
    n = v.shape[0]
    return jnp.sum(v.reshape(n // 8, 8, v.shape[1]), axis=0)


class Gather:
    def __init__(self, nz, wa, wb, held, stage, z_sem, s_sem, own_sem, load_sem):
        self.at = Place(nz)
        self.nz, self.wa, self.wb, self.held, self.stage = nz, wa, wb, held, stage
        self.z_sem, self.s_sem, self.own_sem, self.load_sem = z_sem, s_sem, own_sem, load_sem

    def step(self, j, k):
        if isinstance(k, int):
            self.act(j, k, k < 8)
            return
        pl.when((k >= 2) & (k < 8))(lambda: self.act(j, k, True))
        if j < 5:
            pl.when((k >= 8) & (k < CHUNKS))(lambda: self.act(j, k, False))

    def act(self, j, k, first):
        at, nz = self.at, self.nz
        mine = pl.ds(pl.multiple_of(at.c * HALF, HALF), HALF)
        others = pl.ds(pl.multiple_of((1 - at.c) * HALF, HALF), HALF)

        def spot(chip, lanes=mine):
            if first:
                return self.wa.at[k, chip, :, lanes]
            return self.wb.at[chip, k - 8, :, lanes]

        def quarter(q):
            return spot(pl.ds(q * nz, nz))

        def z_copy(i, chip):
            return remote(
                self.stage.at[k], spot(chip), self.z_sem.at[0, k, i - 1],
                self.z_sem.at[1, k, i - 1], at.along_z(i),
            )

        def s_copy(i, q, device):
            return remote(quarter(q), quarter(q), self.s_sem.at[0, k, i], self.s_sem.at[1, k, i], device)

        def c_copy(lanes):
            whole = spot(slice(None), lanes)
            return remote(whole, whole, self.s_sem.at[0, k, 3], self.s_sem.at[1, k, 3], at.other)

        chip = at.quarter * nz + at.z

        def own():
            return pltpu.make_async_copy(self.stage.at[k], spot(chip), self.own_sem.at[k])

        if j == 0:
            for i in range(1, nz):
                z_copy(i, chip).start()
            own().start()
        elif j == 1:
            for i in range(1, nz):
                z_copy(i, at.quarter * nz + (at.z - i + nz) % nz).wait_recv()
            own().wait()
            s_copy(0, at.quarter, at.first).start()
            s_copy(1, at.quarter, at.second).start()
        elif j == 2:
            s_copy(0, at.quarter_first, at.first).wait_recv()
            s_copy(2, at.quarter_first, at.second).start()
        elif j == 3:
            s_copy(1, at.quarter_second, at.second).wait_recv()
            s_copy(2, at.quarter_far, at.second).wait_recv()
            c_copy(mine).start()
        elif j == 4:
            c_copy(others).wait_recv()
            for i in range(1, nz):
                z_copy(i, chip).wait_send()
            s_copy(0, at.quarter, at.first).wait_send()
            s_copy(1, at.quarter, at.second).wait_send()
            s_copy(2, at.quarter_first, at.second).wait_send()
            c_copy(mine).wait_send()
            if first:
                self.load(k).start()
        elif first:
            self.load(k).wait()

    def load(self, k):
        return pltpu.make_async_copy(self.wa.at[k], self.held.at[k], self.load_sem.at[k])


def share_start(nz, part_ref, masters, sibs, stage, table_ref, sums, got, x_sem, v_sem, gather):
    at = gather.at
    at.barrier()
    swaps = [
        remote(m, o, x_sem.at[0, i], x_sem.at[1, i], at.other)
        for i, (m, o) in enumerate(zip(masters, sibs))
    ]
    swaps.insert(1, remote(part_ref, got.at[0], x_sem.at[0, 4], x_sem.at[1, 4], at.other))
    for swap in swaps:
        swap.start()
    mq, mo, m1, m2 = masters
    sq, so, s1, s2 = sibs
    even = at.c == 0

    def halves(own, sib):
        own = jnp.where(even, own[:, :HALF], own[:, HALF:])
        sib = jnp.where(even, sib[:, :HALF], sib[:, HALF:])
        top, low = jnp.where(even, own, sib), jnp.where(even, sib, own)
        return jnp.concatenate([top, low], axis=0).astype(bf16)

    def group(ref, hg):
        cols = [ref[:, i * D + hg * WIDE : i * D + (hg + 1) * WIDE] for i in range(3)]
        return jnp.concatenate(cols, axis=1)

    def vec_copy(i, src, device):
        return remote(src, got.at[i], v_sem.at[0, i], v_sem.at[1, i], device)

    swaps[0].wait()
    for hg in range(GROUPS):
        stage[hg] = halves(group(mq, hg), group(sq, hg))
        if hg < 2:
            gather.step(0, hg)
    swaps[1].wait()
    sums[0] = part_ref[...] + got[0]
    z_copies = [vec_copy(i, sums.at[0], at.along_z(i)) for i in range(1, nz)]
    for copy in z_copies:
        copy.start()
    for swap in swaps[2:]:
        swap.wait()
    stage[3] = halves(mo[...], so[...])
    for f in range(4):
        cols = slice(f * CHUNK, (f + 1) * CHUNK)
        stage[4 + f] = halves(m1[:, cols], s1[:, cols])
    step = stage.shape[1]
    for i in range(4):
        rows = slice(i % 2 * step, (i % 2 + 1) * step)
        block = jnp.where(at.c == i // 2, m2[rows, :], s2[rows, :])
        stage[8 + i] = jnp.where(even, block[:, :HALF], block[:, HALF:]).astype(bf16)
    gather.step(1, 0)
    gather.step(1, 1)
    for copy in z_copies:
        copy.wait()
    total = sums[0]
    for i in range(1, nz):
        total = total + got[i]
    sums[1] = total
    a_copy = vec_copy(nz, sums.at[1], at.first)
    a_copy.start()
    gather.step(2, 0)
    a_copy.wait()
    sums[2] = sums[1] + got[nz]
    b_copy = vec_copy(nz + 1, sums.at[2], at.second)
    b_copy.start()
    gather.step(2, 1)
    gather.step(3, 0)
    b_copy.wait()
    table_ref[...] = (sums[2] + got[nz + 1]).astype(f32)
    gather.step(4, 0)
    gather.step(3, 1)
    gather.step(5, 0)


def front_kernel(nz, *refs):
    refs = list(refs)
    x_ref, row_ref, col_ref, vec_ref = refs[:4]
    s = pl.program_id(0)
    att = GROUPS * 4
    if nz:
        masters, refs = refs[4:8], refs[8:]
    else:
        wa_ref, refs = refs[4], refs[5:]
    q_ref, k_ref, v_ref, lse_ref, c_ref, y1_ref, n1_ref, g_ref, gp_ref = refs[:9]
    refs = refs[9:]
    if nz:
        wa_ref, wb_ref, table_ref = refs[:3]
        c_all, held, stage, sq, so, s1, s2, sums, got = refs[3:12]
        z_sem, s_sem, own_sem, load_sem, x_sem, v_sem = refs[12:]
        gather = Gather(nz, wa_ref, wb_ref, held, stage, z_sem, s_sem, own_sem, load_sem)

        @pl.when(s == 0)
        def _():
            share_start(
                nz, vec_ref, masters, (sq, so, s1, s2), stage, table_ref, sums, got,
                x_sem, v_sem, gather,
            )

        for j in (5, 4, 3, 2, 1, 0):
            if j >= 4:
                pl.when(s == j - 4)(lambda: gather.step(j, 1))
            gather.step(j, s + 2 - j)
    else:
        c_all, held, load_sem = refs
        table_ref = vec_ref

        @pl.when(s == 0)
        def _():
            copy = pltpu.make_async_copy(wa_ref, held, load_sem)
            copy.start()
            copy.wait()

    def weight(k):
        return held[k].reshape(CHUNK, CHUNK)

    @pl.when(s < att)
    def _():
        hg = s // 4
        r = s % 4
        rows = pl.multiple_of(r * SEQ, SEQ)
        lanes = pl.multiple_of(hg * WIDE, WIDE)
        xr = x_ref[pl.ds(rows, SEQ), :]
        wqkv = weight(hg)
        q = nn(xr, wqkv[:, 0:WIDE]) + table_ref[BQ : BQ + 1, pl.ds(lanes, WIDE)]
        q = q.astype(bf16)
        k = nn(xr, wqkv[:, WIDE : 2 * WIDE]).astype(bf16)
        v = nn(xr, wqkv[:, 2 * WIDE :]) + table_ref[BV : BV + 1, pl.ds(lanes, WIDE)]
        v = v.astype(bf16)
        q_ref[...] = q
        k_ref[...] = k
        v_ref[...] = v
        vt = v.T
        masks = head_masks()
        for b, first, width in windows():
            qc = spread_heads(q[b * BAND : (b + 1) * BAND, :], masks)
            t = nt(k[first : first + width, :], qc) * SCORE
            t = t + mask_bias(col_ref.at[0], row_ref.at[0], b, first, width)
            m = jnp.max(t, axis=0, keepdims=True)
            e = jnp.exp2(t - m)
            l = jnp.sum(e, axis=0, keepdims=True)
            p = (e * (1.0 / l)).astype(bf16)
            lse_ref[0, b : b + 1, :] = m + jnp.log2(l)
            ot = nn(vt[:, first : first + width], p)
            c = pick_heads(ot).T.astype(bf16)
            c_all[pl.ds(rows + b * BAND, BAND), pl.ds(lanes, WIDE)] = c

    @pl.when(s >= att)
    def _():
        r = s - att
        rows = pl.multiple_of(r * SEQ, SEQ)
        c = c_all[pl.ds(rows, SEQ), :]
        c_ref[...] = c
        y1 = x_ref[pl.ds(rows, SEQ), :].astype(f32) + (
            nn(c, weight(3)) + table_ref[BO : BO + 1, :]
        )
        y1_ref[...] = y1
        z1, _ = norm_stats(y1)
        n1 = (z1 * table_ref[G1 : G1 + 1, :] + table_ref[C1 : C1 + 1, :]).astype(bf16)
        n1_ref[...] = n1
        for f in range(4):
            cols = slice(f * CHUNK, (f + 1) * CHUNK)
            u = nn(n1, weight(4 + f)) + table_ref[B1 + f : B1 + f + 1, :]
            cdf, gauss = normal_cdf(u)
            g_ref[:, cols] = (u * cdf).astype(bf16)
            gp_ref[:, cols] = (cdf + u * (gauss * 0.3989422804014327)).astype(bf16)


def constant(shape):
    return pl.BlockSpec(shape, lambda s: (0,) * len(shape), pipeline_mode=pl.Buffered(1))


def front(x, row_codes, col_codes, table, weights, chips=0):
    tokens = x.shape[0]
    rows = tokens // SEQ
    assert rows == 4
    att = GROUPS * rows
    nz = chips // 4

    def code_at(s):
        return (jnp.where(s < att, s % rows, rows - 1), 0, 0)

    def head_at(s):
        return (jnp.where(s < att, s % rows, rows - 1), jnp.minimum(s // rows, GROUPS - 1))

    def tile_at(s):
        return (jnp.maximum(s - att, 0), 0)

    anywhere = pl.BlockSpec(memory_space=pl.ANY)
    narrow = pl.BlockSpec((SEQ, D), tile_at)
    head = pl.BlockSpec((SEQ, WIDE), head_at)
    wide = pl.BlockSpec((SEQ, FF), tile_at)
    in_specs = [
        constant((tokens, D)),
        pl.BlockSpec((1, 8, SEQ), code_at),
        pl.BlockSpec((1, SEQ, BAND), code_at),
        constant((TABLE, CHUNK)),
    ]
    out_specs = [
        head, head, head,
        pl.BlockSpec((1, 8, PACK * BAND), lambda s: (jnp.minimum(s, att - 1), 0, 0)),
        narrow, narrow, narrow, wide, wide,
    ]
    low = jax.ShapeDtypeStruct((tokens, D), bf16)
    out_shape = [
        low, low, low,
        jax.ShapeDtypeStruct((att, 8, PACK * BAND), f32),
        low,
        jax.ShapeDtypeStruct((tokens, D), f32),
        low,
        jax.ShapeDtypeStruct((tokens, FF), bf16),
        jax.ShapeDtypeStruct((tokens, FF), bf16),
    ]
    if nz:
        step = CHUNK // chips
        in_specs += [constant(w.shape) for w in weights]
        out_specs += [anywhere, anywhere, pl.BlockSpec((TABLE, CHUNK), lambda s: (0, 0))]
        out_shape += [
            jax.ShapeDtypeStruct((8, chips, step, CHUNK), bf16),
            jax.ShapeDtypeStruct((chips, 4, step, CHUNK), bf16),
            jax.ShapeDtypeStruct((TABLE, CHUNK), f32),
        ]
        dma = pltpu.SemaphoreType.DMA
        scratch = [
            pltpu.VMEM((tokens, D), bf16),
            pltpu.VMEM((8, chips, step, CHUNK), bf16),
            pltpu.VMEM((CHUNKS, step, HALF), bf16),
            *(pltpu.VMEM(w.shape, f32) for w in weights),
            pltpu.VMEM((3, TABLE, CHUNK), bf16),
            pltpu.VMEM((nz + 2, TABLE, CHUNK), bf16),
            dma((2, CHUNKS, nz - 1)), dma((2, CHUNKS, 4)), dma((CHUNKS,)), dma((8,)),
            dma((2, 5)), dma((2, nz + 2)),
        ]
        params = pltpu.CompilerParams(
            vmem_limit_bytes=VMEM, collective_id=0, has_side_effects=True
        )
    else:
        in_specs.append(anywhere)
        scratch = [
            pltpu.VMEM((tokens, D), bf16),
            pltpu.VMEM(weights[0].shape, bf16),
            pltpu.SemaphoreType.DMA,
        ]
        params = pltpu.CompilerParams(vmem_limit_bytes=VMEM)
    return pl.pallas_call(
        partial(front_kernel, nz),
        grid=(att + rows,),
        in_specs=in_specs,
        out_specs=out_specs,
        out_shape=out_shape,
        scratch_shapes=scratch,
        compiler_params=params,
        name="front",
    )(x, row_codes, col_codes, table, *weights)


def middle_kernel(
    y1_ref, g_ref, gp_ref, cot_ref, vec_ref, wo_ref, w1_ref, w2_ref,
    out_ref, df_ref, du_ref, dy1_ref, da_ref, dc_ref, grads_ref, sums_ref, ups_ref,
):
    s = pl.program_id(0)

    @pl.when(s == 0)
    def _():
        sums_ref[...] = jnp.zeros_like(sums_ref)
        ups_ref[...] = jnp.zeros_like(ups_ref)

    z1, r1 = norm_stats(y1_ref[...])
    gain1 = vec_ref[G1 : G1 + 1, :]
    gain2 = vec_ref[G2 : G2 + 1, :]
    n1 = z1 * gain1 + vec_ref[C1 : C1 + 1, :]
    y2 = n1 + (nn(g_ref[...], w2_ref[...]) + vec_ref[B2 : B2 + 1, :])
    z2, r2 = norm_stats(y2)
    out_ref[...] = (z2 * gain2 + vec_ref[C2 : C2 + 1, :]).astype(bf16)
    e = cot_ref[...].astype(f32)
    sums_ref[0] += fold_rows(e * z2)
    sums_ref[1] += fold_rows(e)
    dy2 = norm_back(e * gain2, z2, r2)
    df = dy2.astype(bf16)
    df_ref[...] = df
    sums_ref[2] += fold_rows(df.astype(f32))
    step = 768
    for f in range(0, FF, step):
        dg = nt(df, w2_ref[f : f + step, :])
        du = (dg * gp_ref[:, f : f + step].astype(f32)).astype(bf16)
        du_ref[:, f : f + step] = du
        ups_ref[:, f : f + step] += fold_rows(du.astype(f32))
    dn1 = dy2
    for f in range(4):
        dn1 = dn1 + nt(du_ref[:, f * CHUNK : (f + 1) * CHUNK], w1_ref[f])
    sums_ref[3] += fold_rows(dn1 * z1)
    sums_ref[4] += fold_rows(dn1)
    dy1 = norm_back(dn1 * gain1, z1, r1)
    dy1_ref[...] = dy1
    da = dy1.astype(bf16)
    da_ref[...] = da
    sums_ref[5] += fold_rows(da.astype(f32))
    dc_ref[...] = nt(da, wo_ref[0]).astype(bf16)

    @pl.when(s == pl.num_programs(0) - 1)
    def _():
        grads_ref[...] = jnp.zeros_like(grads_ref)
        for i, row in enumerate((G2, C2, B2, G1, C1, BO)):
            grads_ref[row : row + 1, :] = jnp.sum(sums_ref[i], axis=0, keepdims=True)
        for f in range(4):
            cols = slice(f * CHUNK, (f + 1) * CHUNK)
            grads_ref[B1 + f : B1 + f + 1, :] = jnp.sum(ups_ref[:, cols], axis=0, keepdims=True)


def chunks_at(count, index):
    return pl.BlockSpec(
        (count, CHUNK, CHUNK), lambda s: (index, 0, 0), pipeline_mode=pl.Buffered(1)
    )


def middle(y1, g, gp, cot, table, wa, w2):
    tokens = y1.shape[0]
    tile = SEQ

    narrow = pl.BlockSpec((tile, D), lambda s: (s, 0))
    wide = pl.BlockSpec((tile, FF), lambda s: (s, 0))
    wide_out = pl.BlockSpec((tile, FF), lambda s: (s, 0))
    return pl.pallas_call(
        middle_kernel,
        grid=(tokens // tile,),
        in_specs=[
            narrow, wide, wide, narrow, constant((TABLE, CHUNK)),
            chunks_at(1, 3), chunks_at(4, 1), constant((FF, D)),
        ],
        out_specs=[
            narrow, narrow, wide_out, narrow, narrow, narrow,
            pl.BlockSpec((TABLE, CHUNK), lambda s: (0, 0)),
        ],
        out_shape=[
            jax.ShapeDtypeStruct((tokens, D), bf16),
            jax.ShapeDtypeStruct((tokens, D), bf16),
            jax.ShapeDtypeStruct((tokens, FF), bf16),
            jax.ShapeDtypeStruct((tokens, D), f32),
            jax.ShapeDtypeStruct((tokens, D), bf16),
            jax.ShapeDtypeStruct((tokens, D), bf16),
            jax.ShapeDtypeStruct((TABLE, CHUNK), f32),
        ],
        scratch_shapes=[pltpu.VMEM((6, 8, D), f32), pltpu.VMEM((8, FF), f32)],
        compiler_params=pltpu.CompilerParams(vmem_limit_bytes=VMEM),
        name="middle",
    )(y1, g, gp, cot, table, wa, wa, w2)


def outer_kernel(a_ref, b_ref, o_ref):
    o_ref[...] = tn(a_ref[...], b_ref[...]).astype(o_ref.dtype).reshape(o_ref.shape)


def outer(a, b, dtype, side):
    tokens, m = a.shape
    n = b.shape[1]
    if side == 0:
        grid, a_at, b_at = m // CHUNK, (lambda i: (0, i)), (lambda i: (0, 0))
    else:
        grid, a_at, b_at = n // CHUNK, (lambda i: (0, 0)), (lambda i: (0, i))
    return pl.pallas_call(
        outer_kernel,
        grid=(grid,),
        in_specs=[pl.BlockSpec((tokens, CHUNK), a_at), pl.BlockSpec((tokens, CHUNK), b_at)],
        out_specs=pl.BlockSpec((1, CHUNK, CHUNK), lambda i: (i, 0, 0)),
        out_shape=jax.ShapeDtypeStruct((grid, CHUNK, CHUNK), dtype),
        compiler_params=pltpu.CompilerParams(vmem_limit_bytes=VMEM),
        name="outer",
    )(a, b)


DOWN, UP, PROJ, QKV = 0, 4, 8, 9


class Reduce:
    def __init__(self, nz, grads, made, local, bufs, fin, outs, sems):
        self.at = Place(nz)
        self.nz, self.grads, self.made, self.local = nz, grads, made, local
        self.bufs, self.fin, self.outs = bufs, fin, outs
        self.c_sem, self.l_sem, self.q_sem, self.z_sem, self.f_sem = sems

    def step(self, j, r):
        if isinstance(r, int):
            self.act(j, r)
        else:
            pl.when((r >= 0) & (r < QKV))(lambda: self.act(j, r))

    def source(self, r, lanes, fn):
        g2, g1, go = self.grads
        if isinstance(r, int):
            assert r >= QKV
            fn(self.made.at[r - QKV, :, :, lanes])
            return
        pl.when(r < UP)(lambda: fn(g2.at[:, r, :, lanes]))
        pl.when((r >= UP) & (r < PROJ))(lambda: fn(g1.at[r - UP, :, :, lanes]))
        pl.when(r == PROJ)(lambda: fn(go.at[0, :, :, lanes]))

    def act(self, j, r):
        at, nz = self.at, self.nz
        r0, r1, r2, r3 = self.bufs
        fin, got = self.fin
        c, x, y, z = at.c, at.x, at.y, at.z
        half = [pl.ds(pl.multiple_of(i * HALF, HALF), HALF) for i in (c, 1 - c)]

        def c_copy(src):
            return remote(src, r0.at[r], self.c_sem.at[0, r], self.c_sem.at[1, r], at.other)

        def l_copy(src):
            return pltpu.make_async_copy(src, self.local.at[r % 2], self.l_sem.at[r % 2])

        def a_copy(i):
            q = (1 - c) * (2 * i + 1 - x) + c * (2 * (1 - y) + i)
            return remote(
                r0.at[r, pl.ds(q * nz, nz)], r1.at[r, i],
                self.q_sem.at[0, r, i], self.q_sem.at[1, r, i], at.first,
            )

        keep = (1 - c) * y + c * x

        def b_copy():
            return remote(
                r1.at[r, 1 - keep], r2.at[r],
                self.q_sem.at[0, r, 2], self.q_sem.at[1, r, 2], at.second,
            )

        def z_copy(i):
            return remote(
                r2.at[r, (z + i) % nz], r3.at[r, i - 1],
                self.z_sem.at[0, r, i - 1], self.z_sem.at[1, r, i - 1], at.along_z(i),
            )

        def f_copy():
            return remote(fin.at[r], got.at[r], self.f_sem.at[0, r], self.f_sem.at[1, r], at.other)

        rows = fin.shape[1] // 2
        if j == 0:
            self.source(r, half[1], lambda src: c_copy(src).start())
            if not isinstance(r, int):
                self.source(r, half[0], lambda src: l_copy(src).start())
        elif j == 1:
            if isinstance(r, int):
                c_copy(self.made.at[r - QKV, :, :, half[1]]).wait()
                mine = jnp.where(
                    c == 0, self.made[r - QKV, :, :, :HALF], self.made[r - QKV, :, :, HALF:]
                )
            else:
                self.source(r, half[1], lambda src: c_copy(src).wait())
                self.source(r, half[0], lambda src: l_copy(src).wait())
                mine = self.local[r % 2]
            r0[r] = r0[r] + mine
            a_copy(0).start()
            a_copy(1).start()
        elif j == 2:
            for i in (0, 1):
                a_copy(i).wait()
                q = (1 - c) * (2 * i + x) + c * (2 * y + i)
                r1[r, i] = r1[r, i] + r0[r, pl.ds(q * nz, nz)]
            b_copy().start()
        elif j == 3:
            b_copy().wait()
            r2[r] = r2[r] + r1[r, keep]
            for i in range(1, nz):
                z_copy(i).start()
        elif j == 4:
            total = r2[r, z].astype(f32)
            for i in range(1, nz):
                z_copy(i).wait()
                total = total + r3[r, i - 1].astype(f32)
            fin[r] = total
            f_copy().start()
        else:
            f_copy().wait()
            self.finish(r, rows)

    def finish(self, r, rows):
        c = self.at.c
        fin, got = self.fin
        out, out_down = self.outs
        even = c == 0

        def sides(own, other):
            return jnp.concatenate(
                [jnp.where(even, own, other), jnp.where(even, other, own)], axis=1
            )

        def down():
            @pl.when(c == r // 2)
            def _():
                out_down[r % 2] = sides(fin[r], got[r])

        def rest():
            own = jnp.where(even, fin[r, :rows, :], fin[r, rows:, :])
            other = jnp.where(even, got[r, :rows, :], got[r, rows:, :])
            out[r - UP] = sides(own, other)

        if isinstance(r, int):
            rest()
        else:
            pl.when(r < UP)(down)
            pl.when(r >= UP)(rest)


def back_kernel(nz, *refs):
    x_ref, row_ref, col_ref, wqkv_ref, q_ref, k_ref, v_ref, dc_ref, lse_ref, dy1_ref = refs[:10]
    refs = refs[10:]
    s = pl.program_id(0)
    att = GROUPS * 4
    if nz:
        table_ref, g2, g1, go, out, out_down, total_ref, dx_ref = refs[:8]
        dqkv, dk_sum, dv_sum, qv_sum, made, local, r0, r1, r2, r3, fin, got = refs[8:20]
        mine, came = refs[20:22]
        sems, v_sem = refs[22:27], refs[27]
        reduce = Reduce(
            nz, (g2, g1, go), made, local, (r0, r1, r2, r3), (fin, got), (out, out_down), sems
        )
        at = reduce.at

        @pl.when(s == 0)
        def _():
            at.barrier()

        for j in (5, 4, 3, 2, 1, 0):
            reduce.step(j, s - j)
            for hg in range(GROUPS - 1):
                pl.when(s == (hg + 1) * 4 + j)(lambda: reduce.step(j, QKV + hg))
    else:
        dw_ref, dx_ref, total_ref, dqkv, dk_sum, dv_sum, qv_sum = refs

    @pl.when(s == 0)
    def _():
        qv_sum[...] = jnp.zeros_like(qv_sum)

    @pl.when(s < att)
    def _():
        hg = s // 4
        r = s % 4
        rows = pl.multiple_of(r * SEQ, SEQ)
        lanes = pl.ds(pl.multiple_of(hg * WIDE, WIDE), WIDE)
        kt = k_ref[...].T
        dk_sum[...] = jnp.zeros_like(dk_sum)
        dv_sum[...] = jnp.zeros_like(dv_sum)
        masks = head_masks()
        for b, first, width in windows():
            block = slice(b * BAND, (b + 1) * BAND)
            span = slice(first, first + width)
            qc = spread_heads(q_ref[block, :], masks)
            dcc = spread_heads(dc_ref[block, :], masks)
            t = nt(k_ref[span, :], qc) * SCORE
            t = t + mask_bias(col_ref.at[0], row_ref.at[0], b, first, width)
            p = jnp.exp2(t - lse_ref[0, b : b + 1, :])
            dp = nt(v_ref[span, :], dcc)
            dv_sum[span, :] += nn(p.astype(bf16), dcc)
            pdp = p * dp
            weighted = jnp.sum(pdp, axis=0, keepdims=True)
            ds = (pdp - p * weighted).astype(bf16)
            dk_sum[span, :] += nn(ds, qc)
            dqt = nn(kt[:, span], ds)
            dq = (pick_heads(dqt).T * HEAD_DIM ** (-0.5)).astype(bf16)
            dqkv[hg, pl.ds(rows + b * BAND, BAND), 0:WIDE] = dq
            qv_sum[0, :, lanes] += fold_rows(dq.astype(f32))
        dk = (dk_sum[...] * HEAD_DIM ** (-0.5)).astype(bf16)
        dv = dv_sum[...].astype(bf16)
        dqkv[hg, pl.ds(rows, SEQ), WIDE : 2 * WIDE] = dk
        dqkv[hg, pl.ds(rows, SEQ), 2 * WIDE :] = dv
        qv_sum[1, :, lanes] += fold_rows(dv.astype(f32))

        @pl.when(r == 3)
        def _():
            dw = tn(x_ref[...], dqkv[hg])
            if nz:
                made[hg] = dw.astype(bf16).reshape(made.shape[1:])
            else:
                dw_ref[0] = dw

    if nz:
        def vec_copy(i, src, device):
            return remote(src, came.at[i], v_sem.at[0, i], v_sem.at[1, i], device)

        c_copy = vec_copy(0, mine.at[0], at.other)
        z_copies = [vec_copy(i, mine.at[1], at.along_z(i)) for i in range(1, nz)]
        a_copy = vec_copy(nz, mine.at[2], at.first)
        b_copy = vec_copy(nz + 1, mine.at[3], at.second)

        @pl.when(s == att - 1)
        def _():
            reduce.step(0, QKV + GROUPS - 1)
            mine[0] = table_ref[...]
            mine[0, BQ : BQ + 1, :] = jnp.sum(qv_sum[0], axis=0, keepdims=True)
            mine[0, BV : BV + 1, :] = jnp.sum(qv_sum[1], axis=0, keepdims=True)
            c_copy.start()

        @pl.when(s == att)
        def _():
            reduce.step(1, QKV + GROUPS - 1)
            c_copy.wait()
            mine[1] = mine[0] + came[0]
            for copy in z_copies:
                copy.start()

        @pl.when(s == att + 1)
        def _():
            reduce.step(2, QKV + GROUPS - 1)
            total = mine[1]
            for i in range(1, nz):
                z_copies[i - 1].wait()
                total = total + came[i]
            mine[2] = total
            a_copy.start()

        @pl.when(s == att + 2)
        def _():
            reduce.step(3, QKV + GROUPS - 1)
            a_copy.wait()
            mine[3] = mine[2] + came[nz]
            b_copy.start()

        @pl.when(s == att + 3)
        def _():
            reduce.step(4, QKV + GROUPS - 1)

    @pl.when(s >= att)
    def _():
        rows = pl.multiple_of((s - att) * SEQ, SEQ)
        total = dy1_ref[...]
        for hg in range(GROUPS):
            total = total + nt(dqkv[hg, pl.ds(rows, SEQ), :], wqkv_ref[hg])
        dx_ref[...] = total

    @pl.when(s == att + 3)
    def _():
        if nz:
            b_copy.wait()
            total_ref[...] = mine[3] + came[nz + 1]
            reduce.step(5, QKV + GROUPS - 1)
        else:
            total_ref[...] = jnp.zeros_like(total_ref)
            total_ref[BQ : BQ + 1, :] = jnp.sum(qv_sum[0], axis=0, keepdims=True)
            total_ref[BV : BV + 1, :] = jnp.sum(qv_sum[1], axis=0, keepdims=True)


def back(x, row_codes, col_codes, wa, q, k, v, dc, lse, dy1, table=None, grads=None, chips=0):
    tokens = x.shape[0]
    rows = tokens // SEQ
    att = GROUPS * rows
    assert rows == 4
    nz = chips // 4

    def code_at(s):
        return (jnp.where(s < att, s % rows, rows - 1), 0, 0)

    def head_at(s):
        return (jnp.where(s < att, s % rows, rows - 1), jnp.minimum(s // rows, GROUPS - 1))

    def tile_at(s):
        return (jnp.maximum(s - att, 0), 0)

    anywhere = pl.BlockSpec(memory_space=pl.ANY)
    whole_table = pl.BlockSpec((TABLE, CHUNK), lambda s: (0, 0))
    head = pl.BlockSpec((SEQ, WIDE), head_at)
    tile = pl.BlockSpec((SEQ, D), tile_at)
    dx = jax.ShapeDtypeStruct((tokens, D), f32)
    total = jax.ShapeDtypeStruct((TABLE, CHUNK), f32)
    in_specs = [
        constant((tokens, D)),
        pl.BlockSpec((1, 8, SEQ), code_at),
        pl.BlockSpec((1, SEQ, BAND), code_at),
        chunks_at(3, 0),
        head, head, head, head,
        pl.BlockSpec((1, 8, PACK * BAND), lambda s: (jnp.minimum(s, att - 1), 0, 0)),
        tile,
    ]
    scratch = [
        pltpu.VMEM((GROUPS, tokens, 3 * WIDE), bf16),
        pltpu.VMEM((SEQ, WIDE), f32),
        pltpu.VMEM((SEQ, WIDE), f32),
        pltpu.VMEM((2, 8, D), f32),
    ]
    args = [x, row_codes, col_codes, wa, q, k, v, dc, lse, dy1]
    if nz:
        step = CHUNK // chips
        dma = pltpu.SemaphoreType.DMA
        g2, g1, go = grads
        args += [
            table,
            g2.reshape(chips, 4, step, CHUNK),
            g1.reshape(4, chips, step, CHUNK),
            go.reshape(1, chips, step, CHUNK),
        ]
        in_specs += [whole_table, anywhere, anywhere, anywhere]
        out_specs = [
            pl.BlockSpec((8, step // 2, CHUNK), lambda s: (0, 0, 0)),
            pl.BlockSpec((2, step, CHUNK), lambda s: (0, 0, 0)),
            whole_table, tile,
        ]
        out_shape = [
            jax.ShapeDtypeStruct((8, step // 2, CHUNK), f32),
            jax.ShapeDtypeStruct((2, step, CHUNK), f32),
            total, dx,
        ]
        scratch += [
            pltpu.VMEM((GROUPS, chips, step, CHUNK), bf16),
            pltpu.VMEM((2, chips, step, HALF), bf16),
            pltpu.VMEM((CHUNKS, chips, step, HALF), bf16),
            pltpu.VMEM((CHUNKS, 2, nz, step, HALF), bf16),
            pltpu.VMEM((CHUNKS, nz, step, HALF), bf16),
            pltpu.VMEM((CHUNKS, nz - 1, step, HALF), bf16),
            pltpu.VMEM((CHUNKS, step, HALF), f32),
            pltpu.VMEM((CHUNKS, step, HALF), f32),
            pltpu.VMEM((4, TABLE, CHUNK), f32),
            pltpu.VMEM((nz + 2, TABLE, CHUNK), f32),
            dma((2, CHUNKS)), dma((2,)), dma((2, CHUNKS, 3)), dma((2, CHUNKS, nz - 1)),
            dma((2, CHUNKS)), dma((2, nz + 2)),
        ]
        params = pltpu.CompilerParams(
            vmem_limit_bytes=VMEM, collective_id=1, has_side_effects=True
        )
    else:
        out_specs = [
            pl.BlockSpec((1, D, 3 * WIDE), lambda s: (jnp.minimum(s // rows, GROUPS - 1), 0, 0)),
            tile, whole_table,
        ]
        out_shape = [jax.ShapeDtypeStruct((GROUPS, D, 3 * WIDE), f32), dx, total]
        params = pltpu.CompilerParams(vmem_limit_bytes=VMEM)
    return pl.pallas_call(
        partial(back_kernel, nz),
        grid=(att + rows,),
        in_specs=in_specs,
        out_specs=out_specs,
        out_shape=out_shape,
        scratch_shapes=scratch,
        compiler_params=params,
        name="back",
    )(*args)


def update(grad, master, moment, average, tokens_all):
    mean_grad = grad / tokens_all
    moment_new = momentum_coef * moment + mean_grad
    step_size = -learn_rate * (mean_grad + momentum_coef * moment_new)
    master_new = master + step_size
    average_new = average_keep * average + (1.0 - average_keep) * master_new
    return (master_new, moment_new, average_new)


def update_steps(grad, master, moment, average, tokens_all):
    mean_grad = grad / tokens_all
    moment_new = momentum_coef * moment + mean_grad
    step_size = -learn_rate * (mean_grad + momentum_coef * moment_new)
    average_step = (1.0 - average_keep) * (master + step_size - average)
    return (step_size, moment_new, average_step)


def update_kernel(tokens_all, *refs):
    grad_ref, down_ref = refs[:2]
    states, outs = refs[2:14], refs[14:]

    def one(i, index, grad):
        master, moment, average = (states[i + 4 * j][index] for j in range(3))
        outs[i][index] = grad
        new = update(grad, master, moment, average, tokens_all)
        for j in range(3):
            outs[i + 4 * (j + 1)][index] = new[j]

    rows = grad_ref.shape[1]
    for hg in range(GROUPS):
        for i in range(3):
            cols = slice(i * D + hg * WIDE, i * D + (hg + 1) * WIDE)
            one(0, (slice(None), cols), grad_ref[5 + hg, :, i * WIDE : (i + 1) * WIDE])
    one(1, (slice(None), slice(None)), grad_ref[4])
    for f in range(4):
        one(2, (slice(None), slice(f * CHUNK, (f + 1) * CHUNK)), grad_ref[f])
    for i in range(2):
        one(3, (slice(2 * rows * i, 2 * rows * (i + 1)), slice(None)), down_ref[i])


def update_weights(grads, grads_down, states, tokens_all):
    whole = pl.BlockSpec(memory_space=pltpu.VMEM)
    shapes = [jax.ShapeDtypeStruct(w.shape, f32) for w in states[:4]]
    return pl.pallas_call(
        partial(update_kernel, tokens_all),
        in_specs=[whole] * 14,
        out_specs=[whole] * 16,
        out_shape=shapes * 4,
        compiler_params=pltpu.CompilerParams(vmem_limit_bytes=VMEM),
        name="update",
    )(grads, grads_down, *states)


def group_columns(w):
    n = w.shape[0]
    return w.reshape(n, 3, GROUPS, WIDE).transpose(2, 0, 1, 3).reshape(GROUPS, n, 3 * WIDE)


def ungroup_columns(w):
    n = w.shape[1]
    return w.reshape(GROUPS, n, 3, WIDE).transpose(1, 2, 0, 3).reshape(n, 3 * D)


def table_of(gains, biases):
    flat = jnp.concatenate([gains, biases, jnp.zeros((TABLE * CHUNK - 9216,), gains.dtype)])
    return flat.reshape(TABLE, CHUNK)


def on_device(
    tokens, segment_ids, pad_counts, out_cotangent,
    qkv_master, proj_master, up_master, down_master, gain_master, bias_master,
    qkv_moment, proj_moment, up_moment, down_moment, gain_moment, bias_moment,
    qkv_average, proj_average, up_average, down_average, gain_average, bias_average,
):
    axes = ("gx", "gy")
    devices = lax.axis_size(axes)
    seq_len = segment_ids.shape[1]
    tokens_all = tokens.shape[0] * devices
    position = jnp.arange(seq_len, dtype=jnp.int32)
    is_pad = position[None, :] >= (seq_len - pad_counts)[:, None]
    codes = segment_ids * 2 + is_pad.astype(jnp.int32)
    row_codes = jnp.broadcast_to(codes[:, None, :], (codes.shape[0], 8, seq_len))
    col_codes = jnp.broadcast_to(codes[:, :, None], (codes.shape[0], seq_len, BAND))
    gain_len, bias_len = gain_master.shape[0], bias_master.shape[0]
    gains = gain_len * devices
    place = lax.axis_index(axes)

    fine = lax.axis_size("gx") == 4 and (2 * D // devices) % 16 == 0
    if fine:
        chips = devices // 2
        part = jnp.zeros((TABLE * CHUNK,), bf16)
        part = lax.dynamic_update_slice(part, gain_master.astype(bf16), (place * gain_len,))
        part = lax.dynamic_update_slice(
            part, bias_master.astype(bf16), (gains + place * bias_len,)
        ).reshape(TABLE, CHUNK)
        q, k, v, lse, c, y1, n1, g, gp, wa, w2, table = front(
            tokens, row_codes, col_codes, part,
            (qkv_master, proj_master, up_master, down_master), chips,
        )
        wa = wa.reshape(8, CHUNK, CHUNK)
        w2 = w2.reshape(FF, D)
    else:
        gather = partial(lax.all_gather, axis_name=axes, axis=0, tiled=True)
        w1 = gather(up_master.astype(bf16))
        wa = jnp.concatenate(
            [
                group_columns(gather(qkv_master.astype(bf16))),
                gather(proj_master.astype(bf16))[None],
                w1.reshape(D, 4, CHUNK).transpose(1, 0, 2),
            ]
        )
        w2 = gather(down_master.astype(bf16))
        table = table_of(
            gather(gain_master.astype(bf16)), gather(bias_master.astype(bf16))
        ).astype(f32)
        q, k, v, lse, c, y1, n1, g, gp = front(
            tokens, row_codes, col_codes, table, (wa.reshape(8, 16, CHUNK // 16, CHUNK),)
        )
    layer_output, df, du, dy1, da, dc, terms = middle(y1, g, gp, out_cotangent, table, wa, w2)
    kept = bf16 if fine else f32
    dw2 = outer(g, df, kept, 0)
    dw1 = outer(n1, du, kept, 1)
    dwo = outer(c, da, kept, 0)
    scatter = partial(lax.psum_scatter, axis_name=axes, scatter_dimension=0, tiled=True)
    states = (
        qkv_master, proj_master, up_master, down_master,
        qkv_moment, proj_moment, up_moment, down_moment,
        qkv_average, proj_average, up_average, down_average,
    )
    if fine:
        grads, grads_down, terms, input_grad = back(
            tokens, row_codes, col_codes, wa, q, k, v, dc, lse, dy1, terms,
            (dw2, dw1, dwo), chips,
        )
        new = update_weights(grads, grads_down, states, tokens_all)
        shares, masters, moments, averages = new[:4], new[4:8], new[8:12], new[12:]
        terms = terms.reshape(-1)
        gain_share = lax.dynamic_slice(terms, (place * gain_len,), (gain_len,))
        bias_share = lax.dynamic_slice(terms, (gains + place * bias_len,), (bias_len,))
    else:
        dwqkv, input_grad, more = back(
            tokens, row_codes, col_codes, wa, q, k, v, dc, lse, dy1
        )
        terms = (terms + more).reshape(-1)
        shares = (
            scatter(ungroup_columns(dwqkv)),
            scatter(dwo[0]),
            scatter(dw1.transpose(1, 0, 2).reshape(D, FF)),
            scatter(dw2.reshape(FF, D)),
        )
        news = [
            update(shares[i], states[i], states[4 + i], states[8 + i], tokens_all)
            for i in range(4)
        ]
        masters, moments, averages = zip(*news)
        gain_share = scatter(terms[:gains])
        bias_share = scatter(terms[gains : gains + bias_len * devices])
    gain_new = update_steps(gain_share, gain_master, gain_moment, gain_average, tokens_all)
    bias_new = update(bias_share, bias_master, bias_moment, bias_average, tokens_all)
    return (
        layer_output, input_grad, *shares, gain_share, bias_share,
        *masters, gain_new[0], bias_new[0],
        *moments, gain_new[1], bias_new[1],
        *averages, gain_new[2], bias_new[2],
    )


def solution(mesh):
    both = ("gx", "gy")
    two, one = P(both, None), P(both)
    weights = (two, two, two, two, one, one)
    in_specs = (two, two, one, two) + weights * 3
    out_specs = (two, two) + weights * 4
    return jax.shard_map(
        on_device, mesh=mesh, in_specs=in_specs, out_specs=out_specs, check_vma=False
    )
```

time: 858 us -> 353 us (0.41)
  waiting for transfers between devices: 476 us -> 0 us
  Pallas kernels: 224 us -> 338 us
  blocking collectives: 82.4 us -> 0 us
  local copies, waits for them, and re-layouts: 38.4 us -> 9.79 us
  other arithmetic: 18.5 us -> 4.03 us
  between operations: 15 us -> 0.75 us
    reduce_scatter x3 -> x0, waiting for transfers between devices: 280 us -> none  [the longest x1 140 us: on_device(): up_share = scatter(dw1)]
    all_gather x4 -> x0, waiting for transfers between devices: 125 us -> none  [the longest x1 66.2 us: on_device(): w1 = gather(up_master.astype(bf16), axis=0)]
    pallas_call x2 -> x3, Pallas kernels: 133 us -> 248 us  [the longest x1 137 us: front(): pl.pallas_call(partial(front_kernel, nz), grid=(att + rows,), in_specs=in...]
    unnamed x2 -> x0, blocking collectives: 82.4 us -> none
    unnamed x9 -> x0, waiting for transfers between devices: 71.6 us -> none
  transfers between devices with their start and end apart: 8 -> 0, of which waited for: 6 -> 0; matrix products, arithmetic and copies ran while one was open for 6% -> 0% of each run, Pallas kernels for 19% -> 0%
where the time goes in v2:
time: 353 us
  Pallas kernels  338 us (96%)
  local copies, waits for them, and re-layouts  9.79 us (3%)
  other arithmetic  4.03 us (1%)
    pallas_call x1, Pallas kernels, front(): pl.pallas_call(partial(front_kernel, nz), grid=(att + rows,), in_specs=in...  137 us
    pallas_call x1, Pallas kernels, back(): pl.pallas_call(partial(back_kernel, nz), grid=(att + rows,), in_specs=in_...  106 us
    pallas_call x1, Pallas kernels, middle(): pl.pallas_call(middle_kernel, grid=(tokens // tile,), in_specs=[narrow, w...  55 us
    pallas_call x3, Pallas kernels, outer(): pl.pallas_call(outer_kernel, grid=(grid,), in_specs=[pl.BlockSpec((tokens...  35.6 us

profile of v2, /device:TPU:0, one launch (start us, length us, event | category | flops | bytes accessed | tf_op | source)
XLA Modules:
  0.0 352.7 jit_solution(15931385559152081002)
XLA Ops:
  0.7 0.7 broadcast_subtract_fusion
  1.3 0.7 convert_element_type.10
  2.0 0.7 convert_element_type.11
  2.7 0.8 convert_add_fusion
  3.4 0.2 dynamic_update_slice.6
  3.7 0.2 dynamic_update_slice.7
  3.9 0.7 reshape.76.refs_3_
  4.5 0.6 broadcast_in_dim.6.refs_1_
  5.2 1.4 broadcast_in_dim.7.refs_2_
  6.5 137.3 %front.1 = (bf16[2048,768]{1,0:T(8,128)(2,1)}, bf16[2048,768]{1,0:T(8,128)(2,1)}, bf16[2048,768]{1,0:T(8,128)(2,1)}, f32[12,8,512]{2,1,0:T(8,128)}, bf16[2048,76...) custom-call(bf16[2048,768]{1,0:T(8,128)(2,1)} %refs_0_.3, ...), custom_call_target="tpu_custom_call" | custom-call | tf_op jit(solution)/shard_map/front/pallas_call | solution.py:473
  143.8 55.0 %middle.1 = (bf16[2048,768]{1,0:T(8,128)(2,1)}, bf16[2048,768]{1,0:T(8,128)(2,1)}, bf16[2048,3072]{1,0:T(8,128)(2,1)}, f32[2048,768]{1,0:T(8,128)}, bf16[2048,76...) custom-call(f32[2048,768]{1,0:T(8,128)} %get-tuple-element.65.y1_ref, ...), custom_call_target="tpu_custom_call" | custom-call | tf_op jit(solution)/shard_map/middle/pallas_call | solution.py:551
  198.8 6.5 %outer.5 = bf16[1,768,768]{2,1,0:T(8,128)(2,1)} custom-call(bf16[2048,768]{1,0:T(8,128)(2,1)} %get-tuple-element.82.a_ref, bf16[2048,768]{1,0:T(8,128)(2,1)} %get-tuple-element.83.b_ref), custom_call_target="tpu_custom_call" | custom-call | tf_op jit(solution)/shard_map/outer/pallas_call | solution.py:588
  205.3 14.5 %outer.3 = bf16[4,768,768]{2,1,0:T(8,128)(2,1)} custom-call(bf16[2048,3072]{1,0:T(8,128)(2,1)} %get-tuple-element.66.g_ref.a_ref, bf16[2048,768]{1,0:T(8,128)(2,1)} %get-tuple-element.79.b_ref), custom_call_target="tpu_custom_call" | custom-call | tf_op jit(solution)/shard_map/outer/pallas_call | solution.py:588
  219.8 14.5 %outer.4 = bf16[4,768,768]{2,1,0:T(8,128)(2,1)} custom-call(bf16[2048,768]{1,0:T(8,128)(2,1)} %get-tuple-element.80.a_ref, bf16[2048,3072]{1,0:T(8,128)(2,1)} %get-tuple-element.81.b_ref), custom_call_target="tpu_custom_call" | custom-call | tf_op jit(solution)/shard_map/outer/pallas_call | solution.py:588
  234.3 0.0 copy-start
  234.3 0.0 copy-start.1
  234.4 0.0 copy-start.2
  234.4 106.5 %back.1 = (f32[8,24,768]{2,1,0:T(8,128)}, f32[2,48,768]{2,1,0:T(8,128)}, f32[16,768]{1,0:T(8,128)}, f32[2048,768]{1,0:T(8,128)}) custom-call(bf16[2048,768]{1,0:T(8,128)(2,1)} %refs_0_.3, s32[4,8,512]{2,1,0:T(8,128)} %broadcast_in_dim.6.refs_1_, s32[4,512,128]{2,1,0:T(8,128)} %broadcast_in_dim.7.refs_2_, bf16[8,768,768]{2,1,0:T(8,128)(2,1)} %bitcast.7, ...), custom_call_target="tpu_custom_call" | custom-call | tf_op jit(solution)/shard_map/back/pallas_call | solution.py:951
  340.9 0.8 reshape.82
  341.7 0.0 copy-done.3
  341.7 0.6 subtract_multiply_fusion
  342.3 0.7 multiply_add_fusion
  343.0 3.8 %update.1 = (f32[24,2304]{1,0:T(8,128)}, f32[24,768]{1,0:T(8,128)}, f32[24,3072]{1,0:T(8,128)}, f32[96,768]{1,0:T(8,128)}, f32[24,2304]{1,0:T(8,128)}, /*index=5...) custom-call(f32[8,24,768]{2,1,0:T(8,128)} %get-tuple-element.85.refs, ...), custom_call_target="tpu_custom_call" | custom-call | tf_op jit(solution)/shard_map/update/pallas_call | solution.py:1006
  346.8 5.9 %copy.51 = f32[2048,768]{1,0:T(8,128)} copy(f32[2048,768]{1,0:T(8,128)} %get-tuple-element.139) | data formatting | bytes 12582912
  (9 shorter events, 0.0 us)
Async XLA Ops:
  234.3 107.4 %copy-start.3 = (f32[48]{0:T(128)S(1)}, f32[48]{0:T(128)}, u32[]{:S(2)}) copy-start(f32[48]{0:T(128)} %param.30) | copy-start | bytes 580
  234.3 107.4 %copy-start.4 = (f32[48]{0:T(128)S(1)}, f32[48]{0:T(128)}, u32[]{:S(2)}) copy-start(f32[48]{0:T(128)} %param.42) | copy-start | bytes 580
  234.3 107.4 %copy-start.5 = (f32[48]{0:T(128)S(1)}, f32[48]{0:T(128)}, u32[]{:S(2)}) copy-start(f32[48]{0:T(128)} %param.36) | copy-start | bytes 580
  234.3 108.0 %copy-start = (f32[240]{0:T(256)S(1)}, f32[240]{0:T(256)}, u32[]{:S(2)}) copy-start(f32[240]{0:T(256)} %param.31) | copy-start | bytes 2884
  234.3 108.0 %copy-start.1 = (f32[240]{0:T(256)S(1)}, f32[240]{0:T(256)}, u32[]{:S(2)}) copy-start(f32[240]{0:T(256)} %param.43) | copy-start | bytes 2884
  234.4 107.9 %copy-start.2 = (f32[240]{0:T(256)S(1)}, f32[240]{0:T(256)}, u32[]{:S(2)}) copy-start(f32[240]{0:T(256)} %param.37) | copy-start | bytes 2884

commit v3 on v2

--- a/solution.py
+++ b/solution.py
@@ -50,13 +50,8 @@
 
 
 def normal_cdf(u):
-    t = 1.0 / (1.0 + 0.28 * jnp.abs(u))
     gauss = jnp.exp2(u * u * (-0.5 * LOG2E))
-    q = -0.10568755
-    for k in (0.38938334, -0.23620046, 0.26827342, 0.0677507, 0.11648054):
-        q = q * t + k
-    tail = q * t * gauss
-    return jnp.where(u >= 0, 1.0 - tail, tail), gauss
+    return 0.5 + 0.5 * lax.erf(u * 0.7071067811865476), gauss
 
 
 def windows():
@@ -128,6 +123,7 @@
         bx, by = x + c * (1 - 2 * x), y + (1 - c) * (1 - 2 * y)
         self.first = (ay * 2 + ax, gy)
         self.second = (by * 2 + bx, gy)
+        self.far = ((1 - y) * 2 + 1 - x, gy)
         self.quarter = gx
         self.quarter_first = ay * 2 + ax
         self.quarter_second = by * 2 + bx
@@ -136,13 +132,15 @@
     def along_z(self, j):
         return (self.quarter, (self.z + j) % self.nz * 2 + self.c)
 
-    def barrier(self):
+    def greet(self):
         sem = pltpu.get_barrier_semaphore()
-        partners = [self.other, self.first, self.second]
+        partners = [self.other, self.first, self.second, self.far]
         partners += [self.along_z(j) for j in range(1, self.nz)]
         for p in partners:
             pl.semaphore_signal(sem, inc=1, device_id=p, device_id_type=MESH)
-        pl.semaphore_wait(sem, len(partners))
+
+    def meet(self):
+        pl.semaphore_wait(pltpu.get_barrier_semaphore(), 4 + self.nz - 1)
 
 
 def fold_rows(v):
@@ -151,28 +149,27 @@
 
 
 class Gather:
-    def __init__(self, nz, wa, wb, held, stage, z_sem, s_sem, own_sem, load_sem):
+    TURNS = (0, 4, 7, 10, 12, 13)
+
+    def __init__(self, nz, wa, wb, held, stage, z_sem, s_sem, own_sem, out_sem):
         self.at = Place(nz)
         self.nz, self.wa, self.wb, self.held, self.stage = nz, wa, wb, held, stage
-        self.z_sem, self.s_sem, self.own_sem, self.load_sem = z_sem, s_sem, own_sem, load_sem
-
-    def step(self, j, k):
-        if isinstance(k, int):
-            self.act(j, k, k < 8)
-            return
-        pl.when((k >= 2) & (k < 8))(lambda: self.act(j, k, True))
-        if j < 5:
-            pl.when((k >= 8) & (k < CHUNKS))(lambda: self.act(j, k, False))
-
-    def act(self, j, k, first):
+        self.z_sem, self.s_sem, self.own_sem, self.out_sem = z_sem, s_sem, own_sem, out_sem
+
+    def pump(self, s, half):
+        for j in (5, 4, 3, 2, 1, 0):
+            if self.TURNS[j] % 2 == half:
+                k = s + 2 + (half - self.TURNS[j]) // 2
+                pl.when((k >= 2) & (k < CHUNKS))(partial(self.act, j, k))
+
+    def act(self, j, k):
         at, nz = self.at, self.nz
+        direct = isinstance(k, int) and k == 0
         mine = pl.ds(pl.multiple_of(at.c * HALF, HALF), HALF)
         others = pl.ds(pl.multiple_of((1 - at.c) * HALF, HALF), HALF)
 
         def spot(chip, lanes=mine):
-            if first:
-                return self.wa.at[k, chip, :, lanes]
-            return self.wb.at[chip, k - 8, :, lanes]
+            return self.held.at[k, chip, :, lanes]
 
         def quarter(q):
             return spot(pl.ds(q * nz, nz))
@@ -184,17 +181,25 @@
             )
 
         def s_copy(i, q, device):
-            return remote(quarter(q), quarter(q), self.s_sem.at[0, k, i], self.s_sem.at[1, k, i], device)
+            return remote(
+                quarter(q), quarter(q), self.s_sem.at[0, k, i], self.s_sem.at[1, k, i], device
+            )
+
+        def far_copy(q):
+            if direct:
+                return s_copy(2, at.quarter if q is None else q, at.far)
+            return s_copy(2, at.quarter_first if q is None else q, at.second)
 
         def c_copy(lanes):
             whole = spot(slice(None), lanes)
-            return remote(whole, whole, self.s_sem.at[0, k, 3], self.s_sem.at[1, k, 3], at.other)
-
-        chip = at.quarter * nz + at.z
+            return remote(
+                whole, whole, self.s_sem.at[0, k, 3], self.s_sem.at[1, k, 3], at.other
+            )
 
         def own():
             return pltpu.make_async_copy(self.stage.at[k], spot(chip), self.own_sem.at[k])
 
+        chip = at.quarter * nz + at.z
         if j == 0:
             for i in range(1, nz):
                 z_copy(i, chip).start()
@@ -205,12 +210,15 @@
             own().wait()
             s_copy(0, at.quarter, at.first).start()
             s_copy(1, at.quarter, at.second).start()
+            if direct:
+                far_copy(None).start()
         elif j == 2:
             s_copy(0, at.quarter_first, at.first).wait_recv()
-            s_copy(2, at.quarter_first, at.second).start()
+            if not direct:
+                far_copy(None).start()
         elif j == 3:
             s_copy(1, at.quarter_second, at.second).wait_recv()
-            s_copy(2, at.quarter_far, at.second).wait_recv()
+            far_copy(at.quarter_far).wait_recv()
             c_copy(mine).start()
         elif j == 4:
             c_copy(others).wait_recv()
@@ -218,20 +226,30 @@
                 z_copy(i, chip).wait_send()
             s_copy(0, at.quarter, at.first).wait_send()
             s_copy(1, at.quarter, at.second).wait_send()
-            s_copy(2, at.quarter_first, at.second).wait_send()
+            far_copy(None).wait_send()
             c_copy(mine).wait_send()
-            if first:
-                self.load(k).start()
-        elif first:
-            self.load(k).wait()
-
-    def load(self, k):
-        return pltpu.make_async_copy(self.wa.at[k], self.held.at[k], self.load_sem.at[k])
+            self.keep(k, lambda copy: copy.start())
+        else:
+            self.keep(k, lambda copy: copy.wait())
+
+    def keep(self, k, fn):
+        def early():
+            fn(pltpu.make_async_copy(self.held.at[k], self.wa.at[k], self.out_sem.at[k]))
+
+        def late():
+            fn(pltpu.make_async_copy(self.held.at[k], self.wb.at[:, k - 8], self.out_sem.at[k]))
+
+        if isinstance(k, int):
+            early()
+        else:
+            pl.when(k < 8)(early)
+            pl.when(k >= 8)(late)
 
 
 def share_start(nz, part_ref, masters, sibs, stage, table_ref, sums, got, x_sem, v_sem, gather):
     at = gather.at
-    at.barrier()
+    at.greet()
+    at.meet()
     swaps = [
         remote(m, o, x_sem.at[0, i], x_sem.at[1, i], at.other)
         for i, (m, o) in enumerate(zip(masters, sibs))
@@ -260,7 +278,7 @@
     for hg in range(GROUPS):
         stage[hg] = halves(group(mq, hg), group(sq, hg))
         if hg < 2:
-            gather.step(0, hg)
+            gather.act(0, hg)
     swaps[1].wait()
     sums[0] = part_ref[...] + got[0]
     z_copies = [vec_copy(i, sums.at[0], at.along_z(i)) for i in range(1, nz)]
@@ -277,28 +295,25 @@
         rows = slice(i % 2 * step, (i % 2 + 1) * step)
         block = jnp.where(at.c == i // 2, m2[rows, :], s2[rows, :])
         stage[8 + i] = jnp.where(even, block[:, :HALF], block[:, HALF:]).astype(bf16)
-    gather.step(1, 0)
-    gather.step(1, 1)
     for copy in z_copies:
         copy.wait()
     total = sums[0]
     for i in range(1, nz):
         total = total + got[i]
     sums[1] = total
-    a_copy = vec_copy(nz, sums.at[1], at.first)
-    a_copy.start()
-    gather.step(2, 0)
-    a_copy.wait()
-    sums[2] = sums[1] + got[nz]
-    b_copy = vec_copy(nz + 1, sums.at[2], at.second)
-    b_copy.start()
-    gather.step(2, 1)
-    gather.step(3, 0)
-    b_copy.wait()
-    table_ref[...] = (sums[2] + got[nz + 1]).astype(f32)
-    gather.step(4, 0)
-    gather.step(3, 1)
-    gather.step(5, 0)
+    near = [
+        vec_copy(nz + i, sums.at[1], device)
+        for i, device in enumerate((at.first, at.second, at.far))
+    ]
+    gather.act(1, 0)
+    for copy in near:
+        copy.start()
+    gather.act(2, 0)
+    gather.act(3, 0)
+    for copy in near:
+        copy.wait()
+    table_ref[...] = (sums[1] + got[nz] + got[nz + 1] + got[nz + 2]).astype(f32)
+    gather.act(4, 0)
 
 
 def front_kernel(nz, *refs):
@@ -315,8 +330,8 @@
     if nz:
         wa_ref, wb_ref, table_ref = refs[:3]
         c_all, held, stage, sq, so, s1, s2, sums, got = refs[3:12]
-        z_sem, s_sem, own_sem, load_sem, x_sem, v_sem = refs[12:]
-        gather = Gather(nz, wa_ref, wb_ref, held, stage, z_sem, s_sem, own_sem, load_sem)
+        z_sem, s_sem, own_sem, out_sem, x_sem, v_sem = refs[12:]
+        gather = Gather(nz, wa_ref, wb_ref, held, stage, z_sem, s_sem, own_sem, out_sem)
 
         @pl.when(s == 0)
         def _():
@@ -325,10 +340,10 @@
                 x_sem, v_sem, gather,
             )
 
-        for j in (5, 4, 3, 2, 1, 0):
-            if j >= 4:
-                pl.when(s == j - 4)(lambda: gather.step(j, 1))
-            gather.step(j, s + 2 - j)
+        for j in (1, 2, 3, 4, 5):
+            pl.when(s == j - 1)(partial(gather.act, j, 1))
+        pl.when(s == 2)(partial(gather.act, 5, 0))
+        gather.pump(s, 0)
     else:
         c_all, held, load_sem = refs
         table_ref = vec_ref
@@ -361,6 +376,8 @@
         vt = v.T
         masks = head_masks()
         for b, first, width in windows():
+            if nz and b == 2:
+                gather.pump(s, 1)
             qc = spread_heads(q[b * BAND : (b + 1) * BAND, :], masks)
             t = nt(k[first : first + width, :], qc) * SCORE
             t = t + mask_bias(col_ref.at[0], row_ref.at[0], b, first, width)
@@ -387,6 +404,8 @@
         n1 = (z1 * table_ref[G1 : G1 + 1, :] + table_ref[C1 : C1 + 1, :]).astype(bf16)
         n1_ref[...] = n1
         for f in range(4):
+            if nz and f == 2:
+                gather.pump(s, 1)
             cols = slice(f * CHUNK, (f + 1) * CHUNK)
             u = nn(n1, weight(4 + f)) + table_ref[B1 + f : B1 + f + 1, :]
             cdf, gauss = normal_cdf(u)
@@ -451,13 +470,13 @@
         dma = pltpu.SemaphoreType.DMA
         scratch = [
             pltpu.VMEM((tokens, D), bf16),
-            pltpu.VMEM((8, chips, step, CHUNK), bf16),
+            pltpu.VMEM((CHUNKS, chips, step, CHUNK), bf16),
             pltpu.VMEM((CHUNKS, step, HALF), bf16),
             *(pltpu.VMEM(w.shape, f32) for w in weights),
-            pltpu.VMEM((3, TABLE, CHUNK), bf16),
-            pltpu.VMEM((nz + 2, TABLE, CHUNK), bf16),
-            dma((2, CHUNKS, nz - 1)), dma((2, CHUNKS, 4)), dma((CHUNKS,)), dma((8,)),
-            dma((2, 5)), dma((2, nz + 2)),
+            pltpu.VMEM((2, TABLE, CHUNK), bf16),
+            pltpu.VMEM((nz + 3, TABLE, CHUNK), bf16),
+            dma((2, CHUNKS, nz - 1)), dma((2, CHUNKS, 4)), dma((CHUNKS,)), dma((CHUNKS,)),
+            dma((2, 5)), dma((2, nz + 3)),
         ]
         params = pltpu.CompilerParams(
             vmem_limit_bytes=VMEM, collective_id=0, has_side_effects=True
@@ -574,29 +593,8 @@
     )(y1, g, gp, cot, table, wa, wa, w2)
 
 
-def outer_kernel(a_ref, b_ref, o_ref):
-    o_ref[...] = tn(a_ref[...], b_ref[...]).astype(o_ref.dtype).reshape(o_ref.shape)
-
-
-def outer(a, b, dtype, side):
-    tokens, m = a.shape
-    n = b.shape[1]
-    if side == 0:
-        grid, a_at, b_at = m // CHUNK, (lambda i: (0, i)), (lambda i: (0, 0))
-    else:
-        grid, a_at, b_at = n // CHUNK, (lambda i: (0, 0)), (lambda i: (0, i))
-    return pl.pallas_call(
-        outer_kernel,
-        grid=(grid,),
-        in_specs=[pl.BlockSpec((tokens, CHUNK), a_at), pl.BlockSpec((tokens, CHUNK), b_at)],
-        out_specs=pl.BlockSpec((1, CHUNK, CHUNK), lambda i: (i, 0, 0)),
-        out_shape=jax.ShapeDtypeStruct((grid, CHUNK, CHUNK), dtype),
-        compiler_params=pltpu.CompilerParams(vmem_limit_bytes=VMEM),
-        name="outer",
-    )(a, b)
-
-
 DOWN, UP, PROJ, QKV = 0, 4, 8, 9
+OUTERS = 9
 
 
 class Reduce:
@@ -606,21 +604,30 @@
         self.bufs, self.fin, self.outs = bufs, fin, outs
         self.c_sem, self.l_sem, self.q_sem, self.z_sem, self.f_sem = sems
 
-    def step(self, j, r):
+    TURNS = (0, 2, 6, 10, 15, 17)
+    LATE_TURNS = (0, 2, 5, 8, 12, 14)
+
+    def pump(self, s, half):
+        for j in (5, 4, 3, 2, 1, 0):
+            if self.TURNS[j] % 2 != half:
+                r = s + (half - 9 - self.TURNS[j]) // 2
+                pl.when((r >= 0) & (r < QKV))(partial(self.act, j, r))
+
+        @pl.when(s >= 13)
+        def _():
+            for hg, start, turns in ((0, 27, self.TURNS), (1, 35, self.LATE_TURNS)):
+                for j in range(6):
+                    turn = start + turns[j]
+                    if turn % 2 == half:
+                        pl.when(s == turn // 2)(partial(self.act, j, QKV + hg))
+
+    def source(self, r, lanes, fn):
+        g2, g19 = self.grads
         if isinstance(r, int):
-            self.act(j, r)
-        else:
-            pl.when((r >= 0) & (r < QKV))(lambda: self.act(j, r))
-
-    def source(self, r, lanes, fn):
-        g2, g1, go = self.grads
-        if isinstance(r, int):
-            assert r >= QKV
-            fn(self.made.at[r - QKV, :, :, lanes])
+            fn(self.made.at[r - QKV, :, :, :, lanes])
             return
-        pl.when(r < UP)(lambda: fn(g2.at[:, r, :, lanes]))
-        pl.when((r >= UP) & (r < PROJ))(lambda: fn(g1.at[r - UP, :, :, lanes]))
-        pl.when(r == PROJ)(lambda: fn(go.at[0, :, :, lanes]))
+        pl.when(r < UP)(lambda: fn(g2.at[:, :, r, :, lanes]))
+        pl.when(r >= UP)(lambda: fn(g19.at[r - UP, :, :, :, lanes]))
 
     def act(self, j, r):
         at, nz = self.at, self.nz
@@ -638,7 +645,7 @@
         def a_copy(i):
             q = (1 - c) * (2 * i + 1 - x) + c * (2 * (1 - y) + i)
             return remote(
-                r0.at[r, pl.ds(q * nz, nz)], r1.at[r, i],
+                r0.at[r, q], r1.at[r, i],
                 self.q_sem.at[0, r, i], self.q_sem.at[1, r, i], at.first,
             )
 
@@ -666,10 +673,9 @@
                 self.source(r, half[0], lambda src: l_copy(src).start())
         elif j == 1:
             if isinstance(r, int):
-                c_copy(self.made.at[r - QKV, :, :, half[1]]).wait()
-                mine = jnp.where(
-                    c == 0, self.made[r - QKV, :, :, :HALF], self.made[r - QKV, :, :, HALF:]
-                )
+                c_copy(self.made.at[r - QKV, :, :, :, half[1]]).wait()
+                own = self.made.at[r - QKV]
+                mine = jnp.where(c == 0, own[:, :, :, :HALF], own[:, :, :, HALF:])
             else:
                 self.source(r, half[1], lambda src: c_copy(src).wait())
                 self.source(r, half[0], lambda src: l_copy(src).wait())
@@ -681,7 +687,7 @@
             for i in (0, 1):
                 a_copy(i).wait()
                 q = (1 - c) * (2 * i + x) + c * (2 * y + i)
-                r1[r, i] = r1[r, i] + r0[r, pl.ds(q * nz, nz)]
+                r1[r, i] = r1[r, i] + r0[r, q]
             b_copy().start()
         elif j == 3:
             b_copy().wait()
@@ -727,40 +733,110 @@
             pl.when(r >= UP)(rest)
 
 
-def back_kernel(nz, *refs):
-    x_ref, row_ref, col_ref, wqkv_ref, q_ref, k_ref, v_ref, dc_ref, lse_ref, dy1_ref = refs[:10]
-    refs = refs[10:]
+def back_kernel(comm, nz, *refs):
+    (
+        x_hbm, row_ref, col_ref, wa_hbm, q_ref, k_ref, v_ref, dc_ref, lse_ref, dy1_ref, table_ref,
+        g_hbm, df_hbm, n1_hbm, du_hbm, c_hbm, da_hbm,
+        g2_hbm, g19_hbm, out, out_down, total_ref, dx_ref,
+        x_ref, wqkv_ref, work, res, made, dk_sum, dv_sum, qv_sum, in_sem, res_sem,
+    ) = refs[:33]
     s = pl.program_id(0)
     att = GROUPS * 4
-    if nz:
-        table_ref, g2, g1, go, out, out_down, total_ref, dx_ref = refs[:8]
-        dqkv, dk_sum, dv_sum, qv_sum, made, local, r0, r1, r2, r3, fin, got = refs[8:20]
-        mine, came = refs[20:22]
-        sems, v_sem = refs[22:27], refs[27]
+    end = OUTERS + att
+    if comm:
+        local, r0, r1, r2, r3, fin, got, mine, came = refs[33:42]
+        sems, v_sem = refs[42:47], refs[47]
         reduce = Reduce(
-            nz, (g2, g1, go), made, local, (r0, r1, r2, r3), (fin, got), (out, out_down), sems
+            nz, (g2_hbm, g19_hbm), made, local, (r0, r1, r2, r3), (fin, got), (out, out_down), sems
         )
         at = reduce.at
 
-        @pl.when(s == 0)
-        def _():
-            at.barrier()
-
-        for j in (5, 4, 3, 2, 1, 0):
-            reduce.step(j, s - j)
-            for hg in range(GROUPS - 1):
-                pl.when(s == (hg + 1) * 4 + j)(lambda: reduce.step(j, QKV + hg))
-    else:
-        dw_ref, dx_ref, total_ref, dqkv, dk_sum, dv_sum, qv_sum = refs
+        pl.when(s == 0)(at.greet)
+        pl.when(s == 4)(at.meet)
+
+    def pump(half):
+        if half == 1:
+            pl.when((s >= 1) & (s <= OUTERS))(lambda: store(s - 1, lambda copy: copy.wait()))
+        if comm:
+            reduce.pump(s, half)
+
+    def bring(src, dst, i):
+        return pltpu.make_async_copy(src, dst, in_sem.at[i])
+
+    def stream(i, fn):
+        cols = pl.ds(pl.multiple_of(i % 4 * CHUNK, CHUNK), CHUNK)
+        slot = i % 2
+        pl.when(i < 4)(lambda: fn(bring(g_hbm.at[:, cols], work.at[slot], slot)))
+        pl.when((i >= 4) & (i < 8))(lambda: fn(bring(du_hbm.at[:, cols], work.at[slot], slot)))
+        pl.when(i == 8)(lambda: fn(bring(c_hbm, work.at[slot], slot)))
+
+    def store(i, fn):
+        slot = i % 2
+        pl.when(i < 4)(
+            lambda: fn(pltpu.make_async_copy(res.at[slot], g2_hbm.at[i], res_sem.at[slot]))
+        )
+        pl.when(i >= 4)(
+            lambda: fn(pltpu.make_async_copy(res.at[slot], g19_hbm.at[i - 4], res_sem.at[slot]))
+        )
+
+    whole_df, whole_da = bring(df_hbm, work.at[2], 2), bring(da_hbm, work.at[2], 2)
+    whole_n1 = bring(n1_hbm, work.at[3], 3)
+    whole_x = bring(x_hbm, x_ref, 4)
+    whole_w = bring(wa_hbm.at[0:GROUPS], wqkv_ref, 5)
 
     @pl.when(s == 0)
     def _():
+        stream(s, lambda copy: copy.start())
+        whole_df.start()
+        stream(s + 1, lambda copy: copy.start())
+        whole_n1.start()
+        whole_df.wait()
         qv_sum[...] = jnp.zeros_like(qv_sum)
 
-    @pl.when(s < att)
+    pump(0)
+
+    @pl.when(s < OUTERS)
     def _():
-        hg = s // 4
-        r = s % 4
+        stream(s, lambda copy: copy.wait())
+        pl.when(s == 4)(lambda: whole_n1.wait())
+        pl.when(s == 8)(lambda: whole_da.wait())
+        part = CHUNK // 2
+
+        def piece(h):
+            @pl.when((s < 4) | (s == 8))
+            def _():
+                left = work[s % 2, :, h * part : (h + 1) * part]
+                put(h, tn(left, work[2]))
+
+            @pl.when((s >= 4) & (s < 8))
+            def _():
+                put(h, tn(work[3, :, h * part : (h + 1) * part], work[s % 2]))
+
+        def put(h, product):
+            shape = (2, *res.shape[2:])
+            res[s % 2, 2 * h : 2 * h + 2] = product.astype(bf16).reshape(shape)
+
+        piece(0)
+        pump(1)
+        piece(1)
+        store(s, lambda copy: copy.start())
+        pl.when(s < OUTERS - 2)(lambda: stream(s + 2, lambda copy: copy.start()))
+        pl.when(s == 3)(lambda: whole_da.start())
+
+        @pl.when(s == 2)
+        def _():
+            whole_x.start()
+            whole_w.start()
+
+        @pl.when(s == OUTERS - 1)
+        def _():
+            whole_x.wait()
+            whole_w.wait()
+
+    @pl.when((s >= OUTERS) & (s < end))
+    def _():
+        hg = (s - OUTERS) // 4
+        r = (s - OUTERS) % 4
         rows = pl.multiple_of(r * SEQ, SEQ)
         lanes = pl.ds(pl.multiple_of(hg * WIDE, WIDE), WIDE)
         kt = k_ref[...].T
@@ -768,6 +844,8 @@
         dv_sum[...] = jnp.zeros_like(dv_sum)
         masks = head_masks()
         for b, first, width in windows():
+            if b == 2:
+                pump(1)
             block = slice(b * BAND, (b + 1) * BAND)
             span = slice(first, first + width)
             qc = spread_heads(q_ref[block, :], masks)
@@ -783,181 +861,189 @@
             dk_sum[span, :] += nn(ds, qc)
             dqt = nn(kt[:, span], ds)
             dq = (pick_heads(dqt).T * HEAD_DIM ** (-0.5)).astype(bf16)
-            dqkv[hg, pl.ds(rows + b * BAND, BAND), 0:WIDE] = dq
+            work[hg, pl.ds(rows + b * BAND, BAND), 0:WIDE] = dq
             qv_sum[0, :, lanes] += fold_rows(dq.astype(f32))
         dk = (dk_sum[...] * HEAD_DIM ** (-0.5)).astype(bf16)
         dv = dv_sum[...].astype(bf16)
-        dqkv[hg, pl.ds(rows, SEQ), WIDE : 2 * WIDE] = dk
-        dqkv[hg, pl.ds(rows, SEQ), 2 * WIDE :] = dv
+        work[hg, pl.ds(rows, SEQ), WIDE : 2 * WIDE] = dk
+        work[hg, pl.ds(rows, SEQ), 2 * WIDE :] = dv
         qv_sum[1, :, lanes] += fold_rows(dv.astype(f32))
 
         @pl.when(r == 3)
         def _():
-            dw = tn(x_ref[...], dqkv[hg])
-            if nz:
-                made[hg] = dw.astype(bf16).reshape(made.shape[1:])
-            else:
-                dw_ref[0] = dw
-
-    if nz:
+            made[hg] = tn(x_ref[...], work[hg]).astype(bf16).reshape(made.shape[1:])
+
+    last = QKV + GROUPS - 1
+    if comm:
         def vec_copy(i, src, device):
             return remote(src, came.at[i], v_sem.at[0, i], v_sem.at[1, i], device)
 
         c_copy = vec_copy(0, mine.at[0], at.other)
         z_copies = [vec_copy(i, mine.at[1], at.along_z(i)) for i in range(1, nz)]
-        a_copy = vec_copy(nz, mine.at[2], at.first)
-        b_copy = vec_copy(nz + 1, mine.at[3], at.second)
-
-        @pl.when(s == att - 1)
+        near = [
+            vec_copy(nz + i, mine.at[2], device)
+            for i, device in enumerate((at.first, at.second, at.far))
+        ]
+
+        @pl.when(s == end - 1)
         def _():
-            reduce.step(0, QKV + GROUPS - 1)
+            reduce.act(0, last)
             mine[0] = table_ref[...]
             mine[0, BQ : BQ + 1, :] = jnp.sum(qv_sum[0], axis=0, keepdims=True)
             mine[0, BV : BV + 1, :] = jnp.sum(qv_sum[1], axis=0, keepdims=True)
             c_copy.start()
 
-        @pl.when(s == att)
+        @pl.when(s == end)
         def _():
-            reduce.step(1, QKV + GROUPS - 1)
+            reduce.act(1, last)
             c_copy.wait()
             mine[1] = mine[0] + came[0]
             for copy in z_copies:
                 copy.start()
 
-        @pl.when(s == att + 1)
+        @pl.when(s == end + 1)
         def _():
-            reduce.step(2, QKV + GROUPS - 1)
+            reduce.act(3, last)
             total = mine[1]
             for i in range(1, nz):
                 z_copies[i - 1].wait()
                 total = total + came[i]
             mine[2] = total
-            a_copy.start()
-
-        @pl.when(s == att + 2)
-        def _():
-            reduce.step(3, QKV + GROUPS - 1)
-            a_copy.wait()
-            mine[3] = mine[2] + came[nz]
-            b_copy.start()
-
-        @pl.when(s == att + 3)
-        def _():
-            reduce.step(4, QKV + GROUPS - 1)
-
-    @pl.when(s >= att)
+            for copy in near:
+                copy.start()
+
+    @pl.when(s >= end)
     def _():
-        rows = pl.multiple_of((s - att) * SEQ, SEQ)
-        total = dy1_ref[...]
-        for hg in range(GROUPS):
-            total = total + nt(dqkv[hg, pl.ds(rows, SEQ), :], wqkv_ref[hg])
-        dx_ref[...] = total
-
-    @pl.when(s == att + 3)
+        half = SEQ // 2
+        for h in range(2):
+            if h == 1:
+                pump(1)
+                if comm:
+                    pl.when(s == end)(lambda: reduce.act(2, last))
+                    pl.when(s == end + 1)(lambda: reduce.act(4, last))
+            rows = pl.ds(pl.multiple_of((s - end) * SEQ + h * half, half), half)
+            total = dy1_ref[h * half : (h + 1) * half, :]
+            for hg in range(GROUPS):
+                total = total + nt(work[hg, rows, :], wqkv_ref[hg].reshape(CHUNK, CHUNK))
+            dx_ref[h * half : (h + 1) * half, :] = total
+
+    @pl.when(s == end + 3)
     def _():
-        if nz:
-            b_copy.wait()
-            total_ref[...] = mine[3] + came[nz + 1]
-            reduce.step(5, QKV + GROUPS - 1)
+        if comm:
+            for copy in near:
+                copy.wait()
+            total_ref[...] = mine[2] + came[nz] + came[nz + 1] + came[nz + 2]
+            reduce.act(5, last)
         else:
-            total_ref[...] = jnp.zeros_like(total_ref)
+            total_ref[...] = table_ref[...]
             total_ref[BQ : BQ + 1, :] = jnp.sum(qv_sum[0], axis=0, keepdims=True)
             total_ref[BV : BV + 1, :] = jnp.sum(qv_sum[1], axis=0, keepdims=True)
-
-
-def back(x, row_codes, col_codes, wa, q, k, v, dc, lse, dy1, table=None, grads=None, chips=0):
+            out[...] = jnp.zeros_like(out)
+            out_down[...] = jnp.zeros_like(out_down)
+
+
+def back(x, row_codes, col_codes, wa, q, k, v, dc, lse, dy1, table, pairs, chips, comm):
     tokens = x.shape[0]
     rows = tokens // SEQ
     att = GROUPS * rows
+    end = OUTERS + att
     assert rows == 4
     nz = chips // 4
+    step = CHUNK // chips
+
+    def turn(s):
+        return jnp.clip(s - OUTERS, 0, att - 1)
 
     def code_at(s):
-        return (jnp.where(s < att, s % rows, rows - 1), 0, 0)
+        return (turn(s) % rows, 0, 0)
 
     def head_at(s):
-        return (jnp.where(s < att, s % rows, rows - 1), jnp.minimum(s // rows, GROUPS - 1))
+        return (turn(s) % rows, turn(s) // rows)
 
     def tile_at(s):
-        return (jnp.maximum(s - att, 0), 0)
+        return (jnp.maximum(s - end, 0), 0)
 
     anywhere = pl.BlockSpec(memory_space=pl.ANY)
     whole_table = pl.BlockSpec((TABLE, CHUNK), lambda s: (0, 0))
     head = pl.BlockSpec((SEQ, WIDE), head_at)
     tile = pl.BlockSpec((SEQ, D), tile_at)
-    dx = jax.ShapeDtypeStruct((tokens, D), f32)
-    total = jax.ShapeDtypeStruct((TABLE, CHUNK), f32)
-    in_specs = [
-        constant((tokens, D)),
-        pl.BlockSpec((1, 8, SEQ), code_at),
-        pl.BlockSpec((1, SEQ, BAND), code_at),
-        chunks_at(3, 0),
-        head, head, head, head,
-        pl.BlockSpec((1, 8, PACK * BAND), lambda s: (jnp.minimum(s, att - 1), 0, 0)),
-        tile,
+    made_shape = (GROUPS, 4, nz, step, CHUNK)
+    dma = pltpu.SemaphoreType.DMA
+    scratch = [
+        pltpu.VMEM((tokens, D), bf16),
+        pltpu.VMEM((GROUPS, *wa.shape[1:]), bf16),
+        pltpu.VMEM((4, tokens, CHUNK), bf16),
+        pltpu.VMEM((2, 4, nz, step, CHUNK), bf16),
     ]
-    scratch = [
-        pltpu.VMEM((GROUPS, tokens, 3 * WIDE), bf16),
+    if comm:
+        scratch.append(pltpu.VMEM(made_shape, bf16))
+    scratch += [
         pltpu.VMEM((SEQ, WIDE), f32),
         pltpu.VMEM((SEQ, WIDE), f32),
         pltpu.VMEM((2, 8, D), f32),
+        dma((6,)), dma((2,)),
     ]
-    args = [x, row_codes, col_codes, wa, q, k, v, dc, lse, dy1]
-    if nz:
-        step = CHUNK // chips
-        dma = pltpu.SemaphoreType.DMA
-        g2, g1, go = grads
-        args += [
-            table,
-            g2.reshape(chips, 4, step, CHUNK),
-            g1.reshape(4, chips, step, CHUNK),
-            go.reshape(1, chips, step, CHUNK),
-        ]
-        in_specs += [whole_table, anywhere, anywhere, anywhere]
-        out_specs = [
-            pl.BlockSpec((8, step // 2, CHUNK), lambda s: (0, 0, 0)),
-            pl.BlockSpec((2, step, CHUNK), lambda s: (0, 0, 0)),
-            whole_table, tile,
-        ]
-        out_shape = [
-            jax.ShapeDtypeStruct((8, step // 2, CHUNK), f32),
-            jax.ShapeDtypeStruct((2, step, CHUNK), f32),
-            total, dx,
-        ]
+    out_specs = [
+        anywhere, anywhere,
+        pl.BlockSpec((8, step // 2, CHUNK), lambda s: (0, 0, 0)),
+        pl.BlockSpec((2, step, CHUNK), lambda s: (0, 0, 0)),
+        whole_table, tile,
+    ]
+    out_shape = [
+        jax.ShapeDtypeStruct((4, nz, 4, step, CHUNK), bf16),
+        jax.ShapeDtypeStruct((5, 4, nz, step, CHUNK), bf16),
+        jax.ShapeDtypeStruct((8, step // 2, CHUNK), f32),
+        jax.ShapeDtypeStruct((2, step, CHUNK), f32),
+        jax.ShapeDtypeStruct((TABLE, CHUNK), f32),
+        jax.ShapeDtypeStruct((tokens, D), f32),
+    ]
+    kernel = partial(back_kernel, comm, nz)
+    if comm:
         scratch += [
-            pltpu.VMEM((GROUPS, chips, step, CHUNK), bf16),
-            pltpu.VMEM((2, chips, step, HALF), bf16),
-            pltpu.VMEM((CHUNKS, chips, step, HALF), bf16),
+            pltpu.VMEM((2, 4, nz, step, HALF), bf16),
+            pltpu.VMEM((CHUNKS, 4, nz, step, HALF), bf16),
             pltpu.VMEM((CHUNKS, 2, nz, step, HALF), bf16),
             pltpu.VMEM((CHUNKS, nz, step, HALF), bf16),
             pltpu.VMEM((CHUNKS, nz - 1, step, HALF), bf16),
             pltpu.VMEM((CHUNKS, step, HALF), f32),
             pltpu.VMEM((CHUNKS, step, HALF), f32),
-            pltpu.VMEM((4, TABLE, CHUNK), f32),
-            pltpu.VMEM((nz + 2, TABLE, CHUNK), f32),
+            pltpu.VMEM((3, TABLE, CHUNK), f32),
+            pltpu.VMEM((nz + 3, TABLE, CHUNK), f32),
             dma((2, CHUNKS)), dma((2,)), dma((2, CHUNKS, 3)), dma((2, CHUNKS, nz - 1)),
-            dma((2, CHUNKS)), dma((2, nz + 2)),
+            dma((2, CHUNKS)), dma((2, nz + 3)),
         ]
         params = pltpu.CompilerParams(
             vmem_limit_bytes=VMEM, collective_id=1, has_side_effects=True
         )
     else:
-        out_specs = [
-            pl.BlockSpec((1, D, 3 * WIDE), lambda s: (jnp.minimum(s // rows, GROUPS - 1), 0, 0)),
-            tile, whole_table,
-        ]
-        out_shape = [jax.ShapeDtypeStruct((GROUPS, D, 3 * WIDE), f32), dx, total]
+        def kernel(*refs):
+            refs = list(refs)
+            made = refs.pop(23)
+            refs.insert(27, made)
+            back_kernel(comm, nz, *refs)
+
+        out_specs.append(pl.BlockSpec(made_shape, lambda s: (0,) * 5, pipeline_mode=pl.Buffered(1)))
+        out_shape.append(jax.ShapeDtypeStruct(made_shape, bf16))
         params = pltpu.CompilerParams(vmem_limit_bytes=VMEM)
     return pl.pallas_call(
-        partial(back_kernel, nz),
-        grid=(att + rows,),
-        in_specs=in_specs,
+        kernel,
+        grid=(end + rows,),
+        in_specs=[
+            anywhere,
+            pl.BlockSpec((1, 8, SEQ), code_at),
+            pl.BlockSpec((1, SEQ, BAND), code_at),
+            anywhere,
+            head, head, head, head,
+            pl.BlockSpec((1, 8, PACK * BAND), lambda s: (turn(s), 0, 0)),
+            tile, whole_table,
+            *(anywhere for _ in pairs),
+        ],
         out_specs=out_specs,
         out_shape=out_shape,
         scratch_shapes=scratch,
         compiler_params=params,
         name="back",
-    )(*args)
+    )(x, row_codes, col_codes, wa, q, k, v, dc, lse, dy1, table, *pairs)
 
 
 def update(grad, master, moment, average, tokens_all):
@@ -1047,7 +1133,7 @@
     gains = gain_len * devices
     place = lax.axis_index(axes)
 
-    fine = lax.axis_size("gx") == 4 and (2 * D // devices) % 16 == 0
+    fine = lax.axis_size("gx") == 4 and lax.axis_size("gy") == 8
     if fine:
         chips = devices // 2
         part = jnp.zeros((TABLE * CHUNK,), bf16)
@@ -1059,7 +1145,6 @@
             tokens, row_codes, col_codes, part,
             (qkv_master, proj_master, up_master, down_master), chips,
         )
-        wa = wa.reshape(8, CHUNK, CHUNK)
         w2 = w2.reshape(FF, D)
     else:
         gather = partial(lax.all_gather, axis_name=axes, axis=0, tiled=True)
@@ -1070,19 +1155,22 @@
                 gather(proj_master.astype(bf16))[None],
                 w1.reshape(D, 4, CHUNK).transpose(1, 0, 2),
             ]
-        )
+        ).reshape(8, 16, CHUNK // 16, CHUNK)
         w2 = gather(down_master.astype(bf16))
         table = table_of(
             gather(gain_master.astype(bf16)), gather(bias_master.astype(bf16))
         ).astype(f32)
         q, k, v, lse, c, y1, n1, g, gp = front(
-            tokens, row_codes, col_codes, table, (wa.reshape(8, 16, CHUNK // 16, CHUNK),)
+            tokens, row_codes, col_codes, table, (wa,)
         )
-    layer_output, df, du, dy1, da, dc, terms = middle(y1, g, gp, out_cotangent, table, wa, w2)
-    kept = bf16 if fine else f32
-    dw2 = outer(g, df, kept, 0)
-    dw1 = outer(n1, du, kept, 1)
-    dwo = outer(c, da, kept, 0)
+    layer_output, df, du, dy1, da, dc, terms = middle(
+        y1, g, gp, out_cotangent, table, wa.reshape(8, CHUNK, CHUNK), w2
+    )
+    results = back(
+        tokens, row_codes, col_codes, wa, q, k, v, dc, lse, dy1, terms,
+        (g, df, n1, du, c, da), chips if fine else 16, fine,
+    )
+    input_grad = results[5]
     scatter = partial(lax.psum_scatter, axis_name=axes, scatter_dimension=0, tiled=True)
     states = (
         qkv_master, proj_master, up_master, down_master,
@@ -1090,25 +1178,21 @@
         qkv_average, proj_average, up_average, down_average,
     )
     if fine:
-        grads, grads_down, terms, input_grad = back(
-            tokens, row_codes, col_codes, wa, q, k, v, dc, lse, dy1, terms,
-            (dw2, dw1, dwo), chips,
-        )
+        grads, grads_down, terms = results[2:5]
         new = update_weights(grads, grads_down, states, tokens_all)
         shares, masters, moments, averages = new[:4], new[4:8], new[8:12], new[12:]
         terms = terms.reshape(-1)
         gain_share = lax.dynamic_slice(terms, (place * gain_len,), (gain_len,))
         bias_share = lax.dynamic_slice(terms, (gains + place * bias_len,), (bias_len,))
     else:
-        dwqkv, input_grad, more = back(
-            tokens, row_codes, col_codes, wa, q, k, v, dc, lse, dy1
-        )
-        terms = (terms + more).reshape(-1)
+        down_part, rest, terms, dwqkv = (results[i].astype(f32) for i in (0, 1, 4, 6))
+        rest = rest.reshape(5, CHUNK, CHUNK)
+        terms = terms.reshape(-1)
         shares = (
-            scatter(ungroup_columns(dwqkv)),
-            scatter(dwo[0]),
-            scatter(dw1.transpose(1, 0, 2).reshape(D, FF)),
-            scatter(dw2.reshape(FF, D)),
+            scatter(ungroup_columns(dwqkv.reshape(GROUPS, CHUNK, CHUNK))),
+            scatter(rest[4]),
+            scatter(rest[:4].transpose(1, 0, 2).reshape(D, FF)),
+            scatter(down_part.reshape(FF, D)),
         )
         news = [
             update(shares[i], states[i], states[4 + i], states[8 + i], tokens_all)

time: 353 us -> 310 us (0.88)
  Pallas kernels: 338 us -> 295 us
    pallas_call x1, Pallas kernels: 137 us -> 114 us  [front(): pl.pallas_call(partial(front_kernel, nz), grid=(att + rows,), in_specs=in...]
    pallas_call x4 -> x1, Pallas kernels: 142 us -> 122 us  [back(): pl.pallas_call(kernel, grid=(end + rows,), in_specs=[anywhere, pl.BlockSp...]
where the time goes in v3:
time: 310 us; the launch traced here: 309 us
  Pallas kernels  295 us (95%)
  local copies, waits for them, and re-layouts  9.8 us (3%)
  other arithmetic  4.03 us (1%)
    pallas_call x1, Pallas kernels, back(): pl.pallas_call(kernel, grid=(end + rows,), in_specs=[anywhere, pl.BlockSp...  122 us
    pallas_call x1, Pallas kernels, front(): pl.pallas_call(partial(front_kernel, nz), grid=(att + rows,), in_specs=in...  114 us
    pallas_call x1, Pallas kernels, middle(): pl.pallas_call(middle_kernel, grid=(tokens // tile,), in_specs=[narrow, w...  55.2 us

profile of v3, /device:TPU:0, one launch (start us, length us, event | category | flops | bytes accessed | tf_op | source)
XLA Modules:
  0.0 309.2 jit_solution(2686814605289346825)
XLA Ops:
  0.7 0.7 broadcast_subtract_fusion
  1.3 0.7 convert_element_type.10
  2.0 0.7 convert_element_type.11
  2.7 0.8 convert_add_fusion
  3.4 0.2 dynamic_update_slice.6
  3.7 0.2 dynamic_update_slice.7
  3.9 0.7 reshape.67.refs_3_
  4.5 0.6 broadcast_in_dim.6.refs_1_
  5.2 1.4 broadcast_in_dim.7.refs_2_
  6.5 113.8 %front.1 = (bf16[2048,768]{1,0:T(8,128)(2,1)}, bf16[2048,768]{1,0:T(8,128)(2,1)}, bf16[2048,768]{1,0:T(8,128)(2,1)}, f32[12,8,512]{2,1,0:T(8,128)}, bf16[2048,76...) custom-call(bf16[2048,768]{1,0:T(8,128)(2,1)} %refs_0_.3, ...), custom_call_target="tpu_custom_call" | custom-call | tf_op jit(solution)/shard_map/front/pallas_call | solution.py:492
  120.3 55.2 %middle.1 = (bf16[2048,768]{1,0:T(8,128)(2,1)}, bf16[2048,768]{1,0:T(8,128)(2,1)}, bf16[2048,3072]{1,0:T(8,128)(2,1)}, f32[2048,768]{1,0:T(8,128)}, bf16[2048,76...) custom-call(f32[2048,768]{1,0:T(8,128)} %get-tuple-element.65.y1_ref, ...), custom_call_target="tpu_custom_call" | custom-call | tf_op jit(solution)/shard_map/middle/pallas_call | solution.py:570
  175.5 0.0 copy-start.3
  175.5 0.0 copy-start.4
  175.5 0.0 copy-start.5
  175.5 0.0 copy-start
  175.5 0.0 copy-start.1
  175.5 0.0 copy-start.2
  175.5 121.8 %back.1 = (bf16[4,4,4,48,768]{4,3,2,1,0:T(8,128)(2,1)}, bf16[5,4,4,48,768]{4,3,2,1,0:T(8,128)(2,1)}, f32[8,24,768]{2,1,0:T(8,128)}, f32[2,48,768]{2,1,0:T(8,128)...) custom-call(bf16[2048,768]{1,0:T(8,128)(2,1)} %refs_0_.3, s32[4,8,512]{2,1,0:T(8,128)} %broadcast_in_dim.6.refs_1_, ...), custom_call_target="tpu_custom_call" | custom-call | tf_op jit(solution)/shard_map/back/pallas_call | solution.py:1028
  297.4 0.8 reshape.70
  298.2 0.0 copy-done.5
  298.2 0.6 subtract_multiply_fusion
  298.8 0.7 multiply_add_fusion
  299.5 3.8 %update.1 = (f32[24,2304]{1,0:T(8,128)}, f32[24,768]{1,0:T(8,128)}, f32[24,3072]{1,0:T(8,128)}, f32[96,768]{1,0:T(8,128)}, f32[24,2304]{1,0:T(8,128)}, /*index=5...) custom-call(f32[8,24,768]{2,1,0:T(8,128)} %get-tuple-element.85.refs, ...), custom_call_target="tpu_custom_call" | custom-call | tf_op jit(solution)/shard_map/update/pallas_call | solution.py:1092
  303.3 5.9 %copy.51 = f32[2048,768]{1,0:T(8,128)} copy(f32[2048,768]{1,0:T(8,128)} %get-tuple-element.139) | data formatting | bytes 12582912
  (6 shorter events, 0.0 us)
Async XLA Ops:
  175.5 122.7 %copy-start.3 = (f32[48]{0:T(128)S(1)}, f32[48]{0:T(128)}, u32[]{:S(2)}) copy-start(f32[48]{0:T(128)} %param.30) | copy-start | bytes 580
  175.5 122.7 %copy-start.4 = (f32[48]{0:T(128)S(1)}, f32[48]{0:T(128)}, u32[]{:S(2)}) copy-start(f32[48]{0:T(128)} %param.42) | copy-start | bytes 580
  175.5 122.7 %copy-start.5 = (f32[48]{0:T(128)S(1)}, f32[48]{0:T(128)}, u32[]{:S(2)}) copy-start(f32[48]{0:T(128)} %param.36) | copy-start | bytes 580
  175.5 123.3 %copy-start = (f32[240]{0:T(256)S(1)}, f32[240]{0:T(256)}, u32[]{:S(2)}) copy-start(f32[240]{0:T(256)} %param.31) | copy-start | bytes 2884
  175.5 123.3 %copy-start.1 = (f32[240]{0:T(256)S(1)}, f32[240]{0:T(256)}, u32[]{:S(2)}) copy-start(f32[240]{0:T(256)} %param.43) | copy-start | bytes 2884
  175.5 123.3 %copy-start.2 = (f32[240]{0:T(256)S(1)}, f32[240]{0:T(256)}, u32[]{:S(2)}) copy-start(f32[240]{0:T(256)} %param.37) | copy-start | bytes 2884

commit v4 on v3

--- a/solution.py
+++ b/solution.py
@@ -149,18 +149,17 @@
 
 
 class Gather:
-    TURNS = (0, 4, 7, 10, 12, 13)
+    TURNS = (0, 2, 4, 6, 7, 8)
 
     def __init__(self, nz, wa, wb, held, stage, z_sem, s_sem, own_sem, out_sem):
         self.at = Place(nz)
         self.nz, self.wa, self.wb, self.held, self.stage = nz, wa, wb, held, stage
         self.z_sem, self.s_sem, self.own_sem, self.out_sem = z_sem, s_sem, own_sem, out_sem
 
-    def pump(self, s, half):
+    def pump(self, s):
         for j in (5, 4, 3, 2, 1, 0):
-            if self.TURNS[j] % 2 == half:
-                k = s + 2 + (half - self.TURNS[j]) // 2
-                pl.when((k >= 2) & (k < CHUNKS))(partial(self.act, j, k))
+            k = s + 3 - self.TURNS[j]
+            pl.when((k >= (2 if j else 3)) & (k < CHUNKS))(partial(self.act, j, k))
 
     def act(self, j, k):
         at, nz = self.at, self.nz
@@ -239,8 +238,10 @@
         def late():
             fn(pltpu.make_async_copy(self.held.at[k], self.wb.at[:, k - 8], self.out_sem.at[k]))
 
-        if isinstance(k, int):
+        if isinstance(k, int) and k < 8:
             early()
+        elif isinstance(k, int):
+            late()
         else:
             pl.when(k < 8)(early)
             pl.when(k >= 8)(late)
@@ -277,7 +278,7 @@
     swaps[0].wait()
     for hg in range(GROUPS):
         stage[hg] = halves(group(mq, hg), group(sq, hg))
-        if hg < 2:
+        if hg == 0:
             gather.act(0, hg)
     swaps[1].wait()
     sums[0] = part_ref[...] + got[0]
@@ -308,6 +309,8 @@
     gather.act(1, 0)
     for copy in near:
         copy.start()
+    gather.act(0, 1)
+    gather.act(0, 2)
     gather.act(2, 0)
     gather.act(3, 0)
     for copy in near:
@@ -343,7 +346,7 @@
         for j in (1, 2, 3, 4, 5):
             pl.when(s == j - 1)(partial(gather.act, j, 1))
         pl.when(s == 2)(partial(gather.act, 5, 0))
-        gather.pump(s, 0)
+        gather.pump(s)
     else:
         c_all, held, load_sem = refs
         table_ref = vec_ref
@@ -375,12 +378,18 @@
         v_ref[...] = v
         vt = v.T
         masks = head_masks()
-        for b, first, width in windows():
-            if nz and b == 2:
-                gather.pump(s, 1)
+        places = list(windows())
+
+        def begin(b, first, width):
             qc = spread_heads(q[b * BAND : (b + 1) * BAND, :], masks)
-            t = nt(k[first : first + width, :], qc) * SCORE
-            t = t + mask_bias(col_ref.at[0], row_ref.at[0], b, first, width)
+            return nt(k[first : first + width, :], qc)
+
+        ahead = begin(*places[0])
+        for b, first, width in places:
+            t = ahead
+            if b + 1 < len(places):
+                ahead = begin(*places[b + 1])
+            t = t * SCORE + mask_bias(col_ref.at[0], row_ref.at[0], b, first, width)
             m = jnp.max(t, axis=0, keepdims=True)
             e = jnp.exp2(t - m)
             l = jnp.sum(e, axis=0, keepdims=True)
@@ -404,13 +413,13 @@
         n1 = (z1 * table_ref[G1 : G1 + 1, :] + table_ref[C1 : C1 + 1, :]).astype(bf16)
         n1_ref[...] = n1
         for f in range(4):
-            if nz and f == 2:
-                gather.pump(s, 1)
             cols = slice(f * CHUNK, (f + 1) * CHUNK)
             u = nn(n1, weight(4 + f)) + table_ref[B1 + f : B1 + f + 1, :]
             cdf, gauss = normal_cdf(u)
             g_ref[:, cols] = (u * cdf).astype(bf16)
             gp_ref[:, cols] = (cdf + u * (gauss * 0.3989422804014327)).astype(bf16)
+        if nz:
+            pl.when(s == att + 3)(partial(gather.act, 5, CHUNKS - 1))
 
 
 def constant(shape):
@@ -512,37 +521,63 @@
         sums_ref[...] = jnp.zeros_like(sums_ref)
         ups_ref[...] = jnp.zeros_like(ups_ref)
 
-    z1, r1 = norm_stats(y1_ref[...])
     gain1 = vec_ref[G1 : G1 + 1, :]
     gain2 = vec_ref[G2 : G2 + 1, :]
-    n1 = z1 * gain1 + vec_ref[C1 : C1 + 1, :]
-    y2 = n1 + (nn(g_ref[...], w2_ref[...]) + vec_ref[B2 : B2 + 1, :])
-    z2, r2 = norm_stats(y2)
-    out_ref[...] = (z2 * gain2 + vec_ref[C2 : C2 + 1, :]).astype(bf16)
-    e = cot_ref[...].astype(f32)
-    sums_ref[0] += fold_rows(e * z2)
-    sums_ref[1] += fold_rows(e)
-    dy2 = norm_back(e * gain2, z2, r2)
-    df = dy2.astype(bf16)
-    df_ref[...] = df
-    sums_ref[2] += fold_rows(df.astype(f32))
-    step = 768
-    for f in range(0, FF, step):
-        dg = nt(df, w2_ref[f : f + step, :])
-        du = (dg * gp_ref[:, f : f + step].astype(f32)).astype(bf16)
-        du_ref[:, f : f + step] = du
-        ups_ref[:, f : f + step] += fold_rows(du.astype(f32))
-    dn1 = dy2
-    for f in range(4):
-        dn1 = dn1 + nt(du_ref[:, f * CHUNK : (f + 1) * CHUNK], w1_ref[f])
-    sums_ref[3] += fold_rows(dn1 * z1)
-    sums_ref[4] += fold_rows(dn1)
-    dy1 = norm_back(dn1 * gain1, z1, r1)
-    dy1_ref[...] = dy1
-    da = dy1.astype(bf16)
-    da_ref[...] = da
-    sums_ref[5] += fold_rows(da.astype(f32))
-    dc_ref[...] = nt(da, wo_ref[0]).astype(bf16)
+    part = y1_ref.shape[0] // 2
+    kept = [{}, {}]
+
+    def down(h):
+        rows = slice(h * part, (h + 1) * part)
+        kept[h]["f"] = nn(g_ref[rows, :], w2_ref[...])
+
+    def norm_two(h):
+        rows = slice(h * part, (h + 1) * part)
+        z1, r1 = norm_stats(y1_ref[rows, :])
+        n1 = z1 * gain1 + vec_ref[C1 : C1 + 1, :]
+        y2 = n1 + (kept[h]["f"] + vec_ref[B2 : B2 + 1, :])
+        z2, r2 = norm_stats(y2)
+        out_ref[rows, :] = (z2 * gain2 + vec_ref[C2 : C2 + 1, :]).astype(bf16)
+        e = cot_ref[rows, :].astype(f32)
+        sums_ref[0] += fold_rows(e * z2)
+        sums_ref[1] += fold_rows(e)
+        dy2 = norm_back(e * gain2, z2, r2)
+        df = dy2.astype(bf16)
+        df_ref[rows, :] = df
+        sums_ref[2] += fold_rows(df.astype(f32))
+        kept[h].update(dy2=dy2, df=df)
+
+    def up_grad(h):
+        rows = slice(h * part, (h + 1) * part)
+        for f in range(4):
+            cols = slice(f * CHUNK, (f + 1) * CHUNK)
+            dg = nt(kept[h]["df"], w2_ref[cols, :])
+            du = (dg * gp_ref[rows, cols].astype(f32)).astype(bf16)
+            du_ref[rows, cols] = du
+            ups_ref[:, cols] += fold_rows(du.astype(f32))
+
+    def up_back(h):
+        rows = slice(h * part, (h + 1) * part)
+        dn1 = kept[h]["dy2"]
+        for f in range(4):
+            dn1 = dn1 + nt(du_ref[rows, f * CHUNK : (f + 1) * CHUNK], w1_ref[f])
+        kept[h]["dn1"] = dn1
+
+    def norm_one(h):
+        rows = slice(h * part, (h + 1) * part)
+        z1, r1 = norm_stats(y1_ref[rows, :])
+        dn1 = kept[h]["dn1"]
+        sums_ref[3] += fold_rows(dn1 * z1)
+        sums_ref[4] += fold_rows(dn1)
+        dy1 = norm_back(dn1 * gain1, z1, r1)
+        dy1_ref[rows, :] = dy1
+        da = dy1.astype(bf16)
+        da_ref[rows, :] = da
+        sums_ref[5] += fold_rows(da.astype(f32))
+        dc_ref[rows, :] = nt(da, wo_ref[0]).astype(bf16)
+
+    for stage in (down, norm_two, up_grad, up_back, norm_one):
+        for h in range(2):
+            stage(h)
 
     @pl.when(s == pl.num_programs(0) - 1)
     def _():
@@ -604,22 +639,19 @@
         self.bufs, self.fin, self.outs = bufs, fin, outs
         self.c_sem, self.l_sem, self.q_sem, self.z_sem, self.f_sem = sems
 
-    TURNS = (0, 2, 6, 10, 15, 17)
-    LATE_TURNS = (0, 2, 5, 8, 12, 14)
-
-    def pump(self, s, half):
+    TURNS = (0, 1, 3, 5, 7, 8)
+    LATE_TURNS = (0, 1, 3, 4, 6, 7)
+
+    def pump(self, s):
         for j in (5, 4, 3, 2, 1, 0):
-            if self.TURNS[j] % 2 != half:
-                r = s + (half - 9 - self.TURNS[j]) // 2
-                pl.when((r >= 0) & (r < QKV))(partial(self.act, j, r))
-
-        @pl.when(s >= 13)
+            r = s - 5 - self.TURNS[j]
+            pl.when((r >= 0) & (r < QKV))(partial(self.act, j, r))
+
+        @pl.when(s >= 5 + QKV)
         def _():
-            for hg, start, turns in ((0, 27, self.TURNS), (1, 35, self.LATE_TURNS)):
+            for hg, start, turns in ((0, 5 + QKV, self.TURNS), (1, 17, self.LATE_TURNS)):
                 for j in range(6):
-                    turn = start + turns[j]
-                    if turn % 2 == half:
-                        pl.when(s == turn // 2)(partial(self.act, j, QKV + hg))
+                    pl.when(s == start + turns[j])(partial(self.act, j, QKV + hg))
 
     def source(self, r, lanes, fn):
         g2, g19 = self.grads
@@ -752,13 +784,7 @@
         at = reduce.at
 
         pl.when(s == 0)(at.greet)
-        pl.when(s == 4)(at.meet)
-
-    def pump(half):
-        if half == 1:
-            pl.when((s >= 1) & (s <= OUTERS))(lambda: store(s - 1, lambda copy: copy.wait()))
-        if comm:
-            reduce.pump(s, half)
+        pl.when(s == 5)(at.meet)
 
     def bring(src, dst, i):
         return pltpu.make_async_copy(src, dst, in_sem.at[i])
@@ -793,32 +819,26 @@
         whole_df.wait()
         qv_sum[...] = jnp.zeros_like(qv_sum)
 
-    pump(0)
+    pl.when((s >= 2) & (s < OUTERS + 2))(lambda: store(s - 2, lambda copy: copy.wait()))
+    if comm:
+        reduce.pump(s)
 
     @pl.when(s < OUTERS)
     def _():
         stream(s, lambda copy: copy.wait())
         pl.when(s == 4)(lambda: whole_n1.wait())
         pl.when(s == 8)(lambda: whole_da.wait())
-        part = CHUNK // 2
-
-        def piece(h):
-            @pl.when((s < 4) | (s == 8))
-            def _():
-                left = work[s % 2, :, h * part : (h + 1) * part]
-                put(h, tn(left, work[2]))
-
-            @pl.when((s >= 4) & (s < 8))
-            def _():
-                put(h, tn(work[3, :, h * part : (h + 1) * part], work[s % 2]))
-
-        def put(h, product):
-            shape = (2, *res.shape[2:])
-            res[s % 2, 2 * h : 2 * h + 2] = product.astype(bf16).reshape(shape)
-
-        piece(0)
-        pump(1)
-        piece(1)
+        def put(product):
+            res[s % 2] = product.astype(bf16).reshape(res.shape[1:])
+
+        @pl.when((s < 4) | (s == 8))
+        def _():
+            put(tn(work[s % 2], work[2]))
+
+        @pl.when((s >= 4) & (s < 8))
+        def _():
+            put(tn(work[3], work[s % 2]))
+
         store(s, lambda copy: copy.start())
         pl.when(s < OUTERS - 2)(lambda: stream(s + 2, lambda copy: copy.start()))
         pl.when(s == 3)(lambda: whole_da.start())
@@ -843,21 +863,26 @@
         dk_sum[...] = jnp.zeros_like(dk_sum)
         dv_sum[...] = jnp.zeros_like(dv_sum)
         masks = head_masks()
-        for b, first, width in windows():
-            if b == 2:
-                pump(1)
-            block = slice(b * BAND, (b + 1) * BAND)
-            span = slice(first, first + width)
+        places = list(windows())
+
+        def begin(b, first, width):
+            block, span = slice(b * BAND, (b + 1) * BAND), slice(first, first + width)
             qc = spread_heads(q_ref[block, :], masks)
             dcc = spread_heads(dc_ref[block, :], masks)
-            t = nt(k_ref[span, :], qc) * SCORE
-            t = t + mask_bias(col_ref.at[0], row_ref.at[0], b, first, width)
+            return qc, dcc, nt(k_ref[span, :], qc), nt(v_ref[span, :], dcc)
+
+        ahead = begin(*places[0])
+        for b, first, width in places:
+            span = slice(first, first + width)
+            qc, dcc, t, dp = ahead
+            if b + 1 < len(places):
+                ahead = begin(*places[b + 1])
+            t = t * SCORE + mask_bias(col_ref.at[0], row_ref.at[0], b, first, width)
             p = jnp.exp2(t - lse_ref[0, b : b + 1, :])
-            dp = nt(v_ref[span, :], dcc)
-            dv_sum[span, :] += nn(p.astype(bf16), dcc)
             pdp = p * dp
             weighted = jnp.sum(pdp, axis=0, keepdims=True)
             ds = (pdp - p * weighted).astype(bf16)
+            dv_sum[span, :] += nn(p.astype(bf16), dcc)
             dk_sum[span, :] += nn(ds, qc)
             dqt = nn(kt[:, span], ds)
             dq = (pick_heads(dqt).T * HEAD_DIM ** (-0.5)).astype(bf16)
@@ -916,11 +941,9 @@
     def _():
         half = SEQ // 2
         for h in range(2):
-            if h == 1:
-                pump(1)
-                if comm:
-                    pl.when(s == end)(lambda: reduce.act(2, last))
-                    pl.when(s == end + 1)(lambda: reduce.act(4, last))
+            if h == 1 and comm:
+                pl.when(s == end)(lambda: reduce.act(2, last))
+                pl.when(s == end + 1)(lambda: reduce.act(4, last))
             rows = pl.ds(pl.multiple_of((s - end) * SEQ + h * half, half), half)
             total = dy1_ref[h * half : (h + 1) * half, :]
             for hg in range(GROUPS):
@@ -1064,8 +1087,20 @@
 
 
 def update_kernel(tokens_all, *refs):
-    grad_ref, down_ref = refs[:2]
-    states, outs = refs[2:14], refs[14:]
+    grad_ref, down_ref, dx_ref = refs[:3]
+    states, outs, dx_out, kept, sem = refs[3:15], refs[15:31], *refs[31:34]
+    parts = kept.shape[0]
+    spans = [pl.ds(i * kept.shape[1], kept.shape[1]) for i in range(parts)]
+    loads = [
+        pltpu.make_async_copy(dx_ref.at[span], kept.at[i], sem.at[0, i])
+        for i, span in enumerate(spans)
+    ]
+    saves = [
+        pltpu.make_async_copy(kept.at[i], dx_out.at[span], sem.at[1, i])
+        for i, span in enumerate(spans)
+    ]
+    for load in loads:
+        load.start()
 
     def one(i, index, grad):
         master, moment, average = (states[i + 4 * j][index] for j in range(3))
@@ -1075,6 +1110,9 @@
             outs[i + 4 * (j + 1)][index] = new[j]
 
     rows = grad_ref.shape[1]
+    for i in range(parts):
+        loads[i].wait()
+        saves[i].start()
     for hg in range(GROUPS):
         for i in range(3):
             cols = slice(i * D + hg * WIDE, i * D + (hg + 1) * WIDE)
@@ -1084,19 +1122,25 @@
         one(2, (slice(None), slice(f * CHUNK, (f + 1) * CHUNK)), grad_ref[f])
     for i in range(2):
         one(3, (slice(2 * rows * i, 2 * rows * (i + 1)), slice(None)), down_ref[i])
-
-
-def update_weights(grads, grads_down, states, tokens_all):
+    for save in saves:
+        save.wait()
+
+
+def update_weights(grads, grads_down, dx, states, tokens_all):
     whole = pl.BlockSpec(memory_space=pltpu.VMEM)
+    anywhere = pl.BlockSpec(memory_space=pl.ANY)
     shapes = [jax.ShapeDtypeStruct(w.shape, f32) for w in states[:4]]
     return pl.pallas_call(
         partial(update_kernel, tokens_all),
-        in_specs=[whole] * 14,
-        out_specs=[whole] * 16,
-        out_shape=shapes * 4,
+        in_specs=[whole] * 2 + [anywhere] + [whole] * 12,
+        out_specs=[whole] * 16 + [anywhere],
+        out_shape=shapes * 4 + [jax.ShapeDtypeStruct(dx.shape, f32)],
+        scratch_shapes=[
+            pltpu.VMEM((8, dx.shape[0] // 8, D), f32), pltpu.SemaphoreType.DMA((2, 8)),
+        ],
         compiler_params=pltpu.CompilerParams(vmem_limit_bytes=VMEM),
         name="update",
-    )(grads, grads_down, *states)
+    )(grads, grads_down, dx, *states)
 
 
 def group_columns(w):
@@ -1179,8 +1223,9 @@
     )
     if fine:
         grads, grads_down, terms = results[2:5]
-        new = update_weights(grads, grads_down, states, tokens_all)
-        shares, masters, moments, averages = new[:4], new[4:8], new[8:12], new[12:]
+        new = update_weights(grads, grads_down, input_grad, states, tokens_all)
+        shares, masters, moments, averages = new[:4], new[4:8], new[8:12], new[12:16]
+        input_grad = new[16]
         terms = terms.reshape(-1)
         gain_share = lax.dynamic_slice(terms, (place * gain_len,), (gain_len,))
         bias_share = lax.dynamic_slice(terms, (gains + place * bias_len,), (bias_len,))

time: 310 us -> 291 us (0.939)
  Pallas kernels: 295 us -> 282 us
  local copies, waits for them, and re-layouts: 9.8 us -> 3.91 us
    pallas_call x1, Pallas kernels: 114 us -> 105 us  [front(): pl.pallas_call(partial(front_kernel, nz), grid=(att + rows,), in_specs=in...]
    pallas_call x1, Pallas kernels: 122 us -> 115 us  [back(): pl.pallas_call(kernel, grid=(end + rows,), in_specs=[anywhere, pl.BlockSp...]
    unnamed x13 -> x12, local copies, waits for them, and re-layouts: 5.93 us -> 0.04 us
    pallas_call x1, Pallas kernels: 3.81 us -> 9.25 us  [update_weights(): pl.pallas_call(partial(update_kernel, tokens_all), in_specs=[whole] * 2 +...]
    pallas_call x1, Pallas kernels: 55.2 us -> 51.7 us  [middle(): pl.pallas_call(middle_kernel, grid=(tokens // tile,), in_specs=[narrow, w...]
where the time goes in v4:
time: 291 us
  Pallas kernels  282 us (97%)
  other arithmetic  4.03 us (1%)
  local copies, waits for them, and re-layouts  3.91 us (1%)
    pallas_call x1, Pallas kernels, back(): pl.pallas_call(kernel, grid=(end + rows,), in_specs=[anywhere, pl.BlockSp...  115 us
    pallas_call x1, Pallas kernels, front(): pl.pallas_call(partial(front_kernel, nz), grid=(att + rows,), in_specs=in...  105 us
    pallas_call x1, Pallas kernels, middle(): pl.pallas_call(middle_kernel, grid=(tokens // tile,), in_specs=[narrow, w...  51.7 us
    pallas_call x1, Pallas kernels, update_weights(): pl.pallas_call(partial(update_kernel, tokens_all), in_specs=[whole] * 2 +...  9.25 us

profile of v4, /device:TPU:0, one launch (start us, length us, event | category | flops | bytes accessed | tf_op | source)
XLA Modules:
  0.0 290.6 jit_solution(11455523254103694231)
XLA Ops:
  0.7 0.7 broadcast_subtract_fusion
  1.3 0.7 convert_element_type.10
  2.0 0.7 convert_element_type.11
  2.7 0.8 convert_add_fusion
  3.4 0.2 dynamic_update_slice.6
  3.7 0.2 dynamic_update_slice.7
  3.9 0.7 reshape.67.refs_3_
  4.5 0.6 broadcast_in_dim.6.refs_1_
  5.2 1.4 broadcast_in_dim.7.refs_2_
  6.5 105.4 %front.1 = (bf16[2048,768]{1,0:T(8,128)(2,1)}, bf16[2048,768]{1,0:T(8,128)(2,1)}, bf16[2048,768]{1,0:T(8,128)(2,1)}, f32[12,8,512]{2,1,0:T(8,128)}, bf16[2048,76...) custom-call(bf16[2048,768]{1,0:T(8,128)(2,1)} %refs_0_.3, ...), custom_call_target="tpu_custom_call" | custom-call | tf_op jit(solution)/shard_map/front/pallas_call | solution.py:501
  111.9 51.7 %middle.1 = (bf16[2048,768]{1,0:T(8,128)(2,1)}, bf16[2048,768]{1,0:T(8,128)(2,1)}, bf16[2048,3072]{1,0:T(8,128)(2,1)}, f32[2048,768]{1,0:T(8,128)}, bf16[2048,76...) custom-call(f32[2048,768]{1,0:T(8,128)} %get-tuple-element.66.y1_ref, ...), custom_call_target="tpu_custom_call" | custom-call | tf_op jit(solution)/shard_map/middle/pallas_call | solution.py:605
  163.6 0.0 copy-start.3
  163.7 0.0 copy-start.4
  163.7 0.0 copy-start.5
  163.7 0.0 copy-start
  163.7 0.0 copy-start.1
  163.7 0.0 copy-start.2
  163.7 115.4 %back.1 = (bf16[4,4,4,48,768]{4,3,2,1,0:T(8,128)(2,1)}, bf16[5,4,4,48,768]{4,3,2,1,0:T(8,128)(2,1)}, f32[8,24,768]{2,1,0:T(8,128)}, f32[2,48,768]{2,1,0:T(8,128)...) custom-call(bf16[2048,768]{1,0:T(8,128)(2,1)} %refs_0_.3, s32[4,8,512]{2,1,0:T(8,128)} %broadcast_in_dim.6.refs_1_, ...), custom_call_target="tpu_custom_call" | custom-call | tf_op jit(solution)/shard_map/back/pallas_call | solution.py:1051
  279.1 0.8 reshape.70
  279.9 0.0 copy-done.3
  279.9 0.6 subtract_multiply_fusion
  280.6 0.0 copy-done
  280.6 0.7 multiply_add_fusion
  281.2 9.3 %update.1 = (f32[24,2304]{1,0:T(8,128)}, f32[24,768]{1,0:T(8,128)}, f32[24,3072]{1,0:T(8,128)}, f32[96,768]{1,0:T(8,128)}, f32[24,2304]{1,0:T(8,128)}, /*index=5...) custom-call(f32[8,24,768]{2,1,0:T(8,128)} %get-tuple-element.85.refs, ...), custom_call_target="tpu_custom_call" | custom-call | tf_op jit(solution)/shard_map/update/pallas_call | solution.py:1133
  (5 shorter events, 0.0 us)
Async XLA Ops:
  163.6 116.3 %copy-start.3 = (f32[48]{0:T(128)S(1)}, f32[48]{0:T(128)}, u32[]{:S(2)}) copy-start(f32[48]{0:T(128)} %param.30) | copy-start | bytes 580
  163.7 116.3 %copy-start.4 = (f32[48]{0:T(128)S(1)}, f32[48]{0:T(128)}, u32[]{:S(2)}) copy-start(f32[48]{0:T(128)} %param.42) | copy-start | bytes 580
  163.7 116.3 %copy-start.5 = (f32[48]{0:T(128)S(1)}, f32[48]{0:T(128)}, u32[]{:S(2)}) copy-start(f32[48]{0:T(128)} %param.36) | copy-start | bytes 580
  163.7 116.9 %copy-start = (f32[240]{0:T(256)S(1)}, f32[240]{0:T(256)}, u32[]{:S(2)}) copy-start(f32[240]{0:T(256)} %param.31) | copy-start | bytes 2884
  163.7 116.9 %copy-start.1 = (f32[240]{0:T(256)S(1)}, f32[240]{0:T(256)}, u32[]{:S(2)}) copy-start(f32[240]{0:T(256)} %param.43) | copy-start | bytes 2884
  163.7 116.8 %copy-start.2 = (f32[240]{0:T(256)S(1)}, f32[240]{0:T(256)}, u32[]{:S(2)}) copy-start(f32[240]{0:T(256)} %param.37) | copy-start | bytes 2884

commit v5 on v4

--- a/solution.py
+++ b/solution.py
@@ -149,7 +149,7 @@
 
 
 class Gather:
-    TURNS = (0, 2, 4, 6, 7, 8)
+    TURNS = (-2, 0, 2, 4, 5, 6)
 
     def __init__(self, nz, wa, wb, held, stage, z_sem, s_sem, own_sem, out_sem):
         self.at = Place(nz)
@@ -158,8 +158,28 @@
 
     def pump(self, s):
         for j in (5, 4, 3, 2, 1, 0):
-            k = s + 3 - self.TURNS[j]
-            pl.when((k >= (2 if j else 3)) & (k < CHUNKS))(partial(self.act, j, k))
+            turn = s + 3 - self.TURNS[j]
+            k = (2 * turn + 1) // 3
+            due = (turn % 3 != 2) & (k >= (4, 2, 2, 2, 2, 2)[j]) & (k < CHUNKS - 2)
+            pl.when(due)(partial(self.act, j, k))
+
+        @pl.when(s <= 5)
+        def _():
+            for j, turn in ((2, 1), (3, 3), (4, 4), (5, 5)):
+                pl.when(s == turn)(partial(self.act, j, 1))
+
+        @pl.when(s >= 10)
+        def _():
+            for k in (CHUNKS - 2, CHUNKS - 1):
+                for j in range(6):
+                    turn = k + (0, 2, 3, 4, 5, 6)[j]
+                    pl.when(s == turn)(partial(self.act, j, k))
+
+    def rest(self):
+        self.act(5, CHUNKS - 3)
+        self.act(5, CHUNKS - 2)
+        self.act(4, CHUNKS - 1)
+        self.act(5, CHUNKS - 1)
 
     def act(self, j, k):
         at, nz = self.at, self.nz
@@ -311,11 +331,13 @@
         copy.start()
     gather.act(0, 1)
     gather.act(0, 2)
+    gather.act(0, 3)
     gather.act(2, 0)
     gather.act(3, 0)
     for copy in near:
         copy.wait()
     table_ref[...] = (sums[1] + got[nz] + got[nz + 1] + got[nz + 2]).astype(f32)
+    gather.act(1, 1)
     gather.act(4, 0)
 
 
@@ -343,8 +365,6 @@
                 x_sem, v_sem, gather,
             )
 
-        for j in (1, 2, 3, 4, 5):
-            pl.when(s == j - 1)(partial(gather.act, j, 1))
         pl.when(s == 2)(partial(gather.act, 5, 0))
         gather.pump(s)
     else:
@@ -419,7 +439,7 @@
             g_ref[:, cols] = (u * cdf).astype(bf16)
             gp_ref[:, cols] = (cdf + u * (gauss * 0.3989422804014327)).astype(bf16)
         if nz:
-            pl.when(s == att + 3)(partial(gather.act, 5, CHUNKS - 1))
+            pl.when(s == att + 3)(gather.rest)
 
 
 def constant(shape):
@@ -628,7 +648,7 @@
     )(y1, g, gp, cot, table, wa, wa, w2)
 
 
-DOWN, UP, PROJ, QKV = 0, 4, 8, 9
+UP, PROJ, DOWN, QKV = 0, 4, 5, 9
 OUTERS = 9
 
 
@@ -639,27 +659,28 @@
         self.bufs, self.fin, self.outs = bufs, fin, outs
         self.c_sem, self.l_sem, self.q_sem, self.z_sem, self.f_sem = sems
 
-    TURNS = (0, 1, 3, 5, 7, 8)
-    LATE_TURNS = (0, 1, 3, 4, 6, 7)
+    TURNS = (-1, 0, 2, 4, 6, 7)
 
     def pump(self, s):
         for j in (5, 4, 3, 2, 1, 0):
-            r = s - 5 - self.TURNS[j]
-            pl.when((r >= 0) & (r < QKV))(partial(self.act, j, r))
-
-        @pl.when(s >= 5 + QKV)
-        def _():
-            for hg, start, turns in ((0, 5 + QKV, self.TURNS), (1, 17, self.LATE_TURNS)):
-                for j in range(6):
-                    pl.when(s == start + turns[j])(partial(self.act, j, QKV + hg))
+            turn = s - 4 - self.TURNS[j]
+            r = (2 * turn + 1) // 3
+            due = (turn >= 0) & (turn % 3 != 2) & (r < QKV)
+            pl.when(due)(partial(self.act, j, r))
+
+        @pl.when(s >= 16)
+        def _():
+            for hg, turns in ((0, (16, 17, 19, 21, 22, 23)), (1, (18, 19, 21, 22, 23, 24))):
+                for j in (5, 4, 3, 2, 1, 0):
+                    pl.when(s == turns[j])(partial(self.act, j, QKV + hg))
 
     def source(self, r, lanes, fn):
         g2, g19 = self.grads
         if isinstance(r, int):
             fn(self.made.at[r - QKV, :, :, :, lanes])
             return
-        pl.when(r < UP)(lambda: fn(g2.at[:, :, r, :, lanes]))
-        pl.when(r >= UP)(lambda: fn(g19.at[r - UP, :, :, :, lanes]))
+        pl.when(r >= DOWN)(lambda: fn(g2.at[:, :, r - DOWN, :, lanes]))
+        pl.when(r < DOWN)(lambda: fn(g19.at[r, :, :, :, lanes]))
 
     def act(self, j, r):
         at, nz = self.at, self.nz
@@ -749,20 +770,20 @@
             )
 
         def down():
-            @pl.when(c == r // 2)
+            @pl.when(c == (r - DOWN) // 2)
             def _():
-                out_down[r % 2] = sides(fin[r], got[r])
+                out_down[(r - DOWN) % 2] = sides(fin[r], got[r])
 
         def rest():
             own = jnp.where(even, fin[r, :rows, :], fin[r, rows:, :])
             other = jnp.where(even, got[r, :rows, :], got[r, rows:, :])
-            out[r - UP] = sides(own, other)
+            out[r if not isinstance(r, int) else r - QKV + DOWN] = sides(own, other)
 
         if isinstance(r, int):
             rest()
         else:
-            pl.when(r < UP)(down)
-            pl.when(r >= UP)(rest)
+            pl.when(r >= DOWN)(down)
+            pl.when(r < DOWN)(rest)
 
 
 def back_kernel(comm, nz, *refs):
@@ -784,39 +805,40 @@
         at = reduce.at
 
         pl.when(s == 0)(at.greet)
-        pl.when(s == 5)(at.meet)
+        pl.when(s == 3)(at.meet)
 
     def bring(src, dst, i):
         return pltpu.make_async_copy(src, dst, in_sem.at[i])
 
     def stream(i, fn):
         cols = pl.ds(pl.multiple_of(i % 4 * CHUNK, CHUNK), CHUNK)
+        down = pl.ds(pl.multiple_of((i + 3) % 4 * CHUNK, CHUNK), CHUNK)
         slot = i % 2
-        pl.when(i < 4)(lambda: fn(bring(g_hbm.at[:, cols], work.at[slot], slot)))
-        pl.when((i >= 4) & (i < 8))(lambda: fn(bring(du_hbm.at[:, cols], work.at[slot], slot)))
-        pl.when(i == 8)(lambda: fn(bring(c_hbm, work.at[slot], slot)))
+        pl.when(i < PROJ)(lambda: fn(bring(du_hbm.at[:, cols], work.at[slot], slot)))
+        pl.when(i == PROJ)(lambda: fn(bring(c_hbm, work.at[slot], slot)))
+        pl.when(i >= DOWN)(lambda: fn(bring(g_hbm.at[:, down], work.at[slot], slot)))
 
     def store(i, fn):
         slot = i % 2
-        pl.when(i < 4)(
-            lambda: fn(pltpu.make_async_copy(res.at[slot], g2_hbm.at[i], res_sem.at[slot]))
+        pl.when(i >= DOWN)(
+            lambda: fn(pltpu.make_async_copy(res.at[slot], g2_hbm.at[i - DOWN], res_sem.at[slot]))
         )
-        pl.when(i >= 4)(
-            lambda: fn(pltpu.make_async_copy(res.at[slot], g19_hbm.at[i - 4], res_sem.at[slot]))
+        pl.when(i < DOWN)(
+            lambda: fn(pltpu.make_async_copy(res.at[slot], g19_hbm.at[i], res_sem.at[slot]))
         )
 
-    whole_df, whole_da = bring(df_hbm, work.at[2], 2), bring(da_hbm, work.at[2], 2)
-    whole_n1 = bring(n1_hbm, work.at[3], 3)
+    whole_da = bring(da_hbm, work.at[2], 2)
+    whole_n1, whole_df = bring(n1_hbm, work.at[3], 3), bring(df_hbm, work.at[3], 3)
     whole_x = bring(x_hbm, x_ref, 4)
     whole_w = bring(wa_hbm.at[0:GROUPS], wqkv_ref, 5)
 
     @pl.when(s == 0)
     def _():
         stream(s, lambda copy: copy.start())
-        whole_df.start()
+        whole_n1.start()
         stream(s + 1, lambda copy: copy.start())
-        whole_n1.start()
-        whole_df.wait()
+        whole_da.start()
+        whole_n1.wait()
         qv_sum[...] = jnp.zeros_like(qv_sum)
 
     pl.when((s >= 2) & (s < OUTERS + 2))(lambda: store(s - 2, lambda copy: copy.wait()))
@@ -826,22 +848,26 @@
     @pl.when(s < OUTERS)
     def _():
         stream(s, lambda copy: copy.wait())
-        pl.when(s == 4)(lambda: whole_n1.wait())
-        pl.when(s == 8)(lambda: whole_da.wait())
+        pl.when(s == PROJ)(lambda: whole_da.wait())
+        pl.when(s == DOWN)(lambda: whole_df.wait())
         def put(product):
             res[s % 2] = product.astype(bf16).reshape(res.shape[1:])
 
-        @pl.when((s < 4) | (s == 8))
+        @pl.when(s < PROJ)
+        def _():
+            put(tn(work[3], work[s % 2]))
+
+        @pl.when(s == PROJ)
         def _():
             put(tn(work[s % 2], work[2]))
 
-        @pl.when((s >= 4) & (s < 8))
-        def _():
-            put(tn(work[3], work[s % 2]))
+        @pl.when(s >= DOWN)
+        def _():
+            put(tn(work[s % 2], work[3]))
 
         store(s, lambda copy: copy.start())
         pl.when(s < OUTERS - 2)(lambda: stream(s + 2, lambda copy: copy.start()))
-        pl.when(s == 3)(lambda: whole_da.start())
+        pl.when(s == PROJ - 1)(lambda: whole_df.start())
 
         @pl.when(s == 2)
         def _():

time: 291 us -> 279 us (0.959)
  Pallas kernels: 282 us -> 270 us
    pallas_call x1, Pallas kernels: 105 us -> 94.5 us  [front(): pl.pallas_call(partial(front_kernel, nz), grid=(att + rows,), in_specs=in...]
where the time goes in v5:
time: 279 us
  Pallas kernels  270 us (97%)
  other arithmetic  4.03 us (1%)
  local copies, waits for them, and re-layouts  3.91 us (1%)
    pallas_call x1, Pallas kernels, back(): pl.pallas_call(kernel, grid=(end + rows,), in_specs=[anywhere, pl.BlockSp...  114 us
    pallas_call x1, Pallas kernels, front(): pl.pallas_call(partial(front_kernel, nz), grid=(att + rows,), in_specs=in...  94.5 us
    pallas_call x1, Pallas kernels, middle(): pl.pallas_call(middle_kernel, grid=(tokens // tile,), in_specs=[narrow, w...  51.7 us
    pallas_call x1, Pallas kernels, update_weights(): pl.pallas_call(partial(update_kernel, tokens_all), in_specs=[whole] * 2 +...  9.25 us

profile of v5, /device:TPU:0, one launch (start us, length us, event | category | flops | bytes accessed | tf_op | source)
XLA Modules:
  0.0 278.6 jit_solution(13765046378835570954)
XLA Ops:
  0.7 0.7 broadcast_subtract_fusion
  1.3 0.7 convert_element_type.10
  2.0 0.7 convert_element_type.11
  2.7 0.8 convert_add_fusion
  3.4 0.2 dynamic_update_slice.6
  3.7 0.2 dynamic_update_slice.7
  3.9 0.7 reshape.67.refs_3_
  4.5 0.6 broadcast_in_dim.6.refs_1_
  5.2 1.4 broadcast_in_dim.7.refs_2_
  6.5 94.5 %front.1 = (bf16[2048,768]{1,0:T(8,128)(2,1)}, bf16[2048,768]{1,0:T(8,128)(2,1)}, bf16[2048,768]{1,0:T(8,128)(2,1)}, f32[12,8,512]{2,1,0:T(8,128)}, bf16[2048,76...) custom-call(bf16[2048,768]{1,0:T(8,128)(2,1)} %refs_0_.3, ...), custom_call_target="tpu_custom_call" | custom-call | tf_op jit(solution)/shard_map/front/pallas_call | solution.py:521
  101.0 51.7 %middle.1 = (bf16[2048,768]{1,0:T(8,128)(2,1)}, bf16[2048,768]{1,0:T(8,128)(2,1)}, bf16[2048,3072]{1,0:T(8,128)(2,1)}, f32[2048,768]{1,0:T(8,128)}, bf16[2048,76...) custom-call(f32[2048,768]{1,0:T(8,128)} %get-tuple-element.66.y1_ref, ...), custom_call_target="tpu_custom_call" | custom-call | tf_op jit(solution)/shard_map/middle/pallas_call | solution.py:625
  152.8 0.0 copy-start.3
  152.8 0.0 copy-start.4
  152.8 0.0 copy-start.5
  152.8 0.0 copy-start
  152.8 0.0 copy-start.1
  152.8 0.0 copy-start.2
  152.8 114.2 %back.1 = (bf16[4,4,4,48,768]{4,3,2,1,0:T(8,128)(2,1)}, bf16[5,4,4,48,768]{4,3,2,1,0:T(8,128)(2,1)}, f32[8,24,768]{2,1,0:T(8,128)}, f32[2,48,768]{2,1,0:T(8,128)...) custom-call(bf16[2048,768]{1,0:T(8,128)(2,1)} %refs_0_.3, s32[4,8,512]{2,1,0:T(8,128)} %broadcast_in_dim.6.refs_1_, ...), custom_call_target="tpu_custom_call" | custom-call | tf_op jit(solution)/shard_map/back/pallas_call | solution.py:1077
  267.1 0.8 reshape.70
  267.9 0.0 copy-done.3
  267.9 0.0 copy-done.4
  267.9 0.6 subtract_multiply_fusion
  268.5 0.7 multiply_add_fusion
  269.2 9.3 %update.1 = (f32[24,2304]{1,0:T(8,128)}, f32[24,768]{1,0:T(8,128)}, f32[24,3072]{1,0:T(8,128)}, f32[96,768]{1,0:T(8,128)}, f32[24,2304]{1,0:T(8,128)}, /*index=5...) custom-call(f32[8,24,768]{2,1,0:T(8,128)} %get-tuple-element.85.refs, ...), custom_call_target="tpu_custom_call" | custom-call | tf_op jit(solution)/shard_map/update/pallas_call | solution.py:1159
  (5 shorter events, 0.0 us)
Async XLA Ops:
  152.8 115.1 %copy-start.3 = (f32[48]{0:T(128)S(1)}, f32[48]{0:T(128)}, u32[]{:S(2)}) copy-start(f32[48]{0:T(128)} %param.30) | copy-start | bytes 580
  152.8 115.1 %copy-start.4 = (f32[48]{0:T(128)S(1)}, f32[48]{0:T(128)}, u32[]{:S(2)}) copy-start(f32[48]{0:T(128)} %param.42) | copy-start | bytes 580
  152.8 115.1 %copy-start.5 = (f32[48]{0:T(128)S(1)}, f32[48]{0:T(128)}, u32[]{:S(2)}) copy-start(f32[48]{0:T(128)} %param.36) | copy-start | bytes 580
  152.8 115.7 %copy-start = (f32[240]{0:T(256)S(1)}, f32[240]{0:T(256)}, u32[]{:S(2)}) copy-start(f32[240]{0:T(256)} %param.31) | copy-start | bytes 2884
  152.8 115.7 %copy-start.1 = (f32[240]{0:T(256)S(1)}, f32[240]{0:T(256)}, u32[]{:S(2)}) copy-start(f32[240]{0:T(256)} %param.43) | copy-start | bytes 2884
  152.8 115.7 %copy-start.2 = (f32[240]{0:T(256)S(1)}, f32[240]{0:T(256)}, u32[]{:S(2)}) copy-start(f32[240]{0:T(256)} %param.37) | copy-start | bytes 2884

commit v6 on v5

--- a/solution.py
+++ b/solution.py
@@ -149,7 +149,7 @@
 
 
 class Gather:
-    TURNS = (-2, 0, 2, 4, 5, 6)
+    TURNS = (-3, 0, 2, 4, 5, 6)
 
     def __init__(self, nz, wa, wb, held, stage, z_sem, s_sem, own_sem, out_sem):
         self.at = Place(nz)
@@ -168,11 +168,11 @@
             for j, turn in ((2, 1), (3, 3), (4, 4), (5, 5)):
                 pl.when(s == turn)(partial(self.act, j, 1))
 
-        @pl.when(s >= 10)
+        @pl.when(s >= 9)
         def _():
             for k in (CHUNKS - 2, CHUNKS - 1):
                 for j in range(6):
-                    turn = k + (0, 2, 3, 4, 5, 6)[j]
+                    turn = k + (-1, 2, 3, 4, 5, 6)[j]
                     pl.when(s == turn)(partial(self.act, j, k))
 
     def rest(self):
@@ -659,7 +659,7 @@
         self.bufs, self.fin, self.outs = bufs, fin, outs
         self.c_sem, self.l_sem, self.q_sem, self.z_sem, self.f_sem = sems
 
-    TURNS = (-1, 0, 2, 4, 6, 7)
+    TURNS = (-1, 0, 3, 5, 7, 8)
 
     def pump(self, s):
         for j in (5, 4, 3, 2, 1, 0):
@@ -668,9 +668,9 @@
             due = (turn >= 0) & (turn % 3 != 2) & (r < QKV)
             pl.when(due)(partial(self.act, j, r))
 
-        @pl.when(s >= 16)
-        def _():
-            for hg, turns in ((0, (16, 17, 19, 21, 22, 23)), (1, (18, 19, 21, 22, 23, 24))):
+        @pl.when(s >= 15)
+        def _():
+            for hg, turns in ((0, (15, 16, 19, 21, 23, 24)), (1, (17, 18, 21, 22, 23, 24))):
                 for j in (5, 4, 3, 2, 1, 0):
                     pl.when(s == turns[j])(partial(self.act, j, QKV + hg))
 

time: 279 us -> 274 us (0.982)
  Pallas kernels: 270 us -> 265 us
    pallas_call x1, Pallas kernels: 114 us -> 109 us  [back(): pl.pallas_call(kernel, grid=(end + rows,), in_specs=[anywhere, pl.BlockSp...]
where the time goes in v6:
time: 274 us; the launch traced here: 273 us
  Pallas kernels  265 us (97%)
  other arithmetic  4.03 us (1%)
  local copies, waits for them, and re-layouts  3.91 us (1%)
    pallas_call x1, Pallas kernels, back(): pl.pallas_call(kernel, grid=(end + rows,), in_specs=[anywhere, pl.BlockSp...  109 us
    pallas_call x1, Pallas kernels, front(): pl.pallas_call(partial(front_kernel, nz), grid=(att + rows,), in_specs=in...  94.3 us
    pallas_call x1, Pallas kernels, middle(): pl.pallas_call(middle_kernel, grid=(tokens // tile,), in_specs=[narrow, w...  51.7 us
    pallas_call x1, Pallas kernels, update_weights(): pl.pallas_call(partial(update_kernel, tokens_all), in_specs=[whole] * 2 +...  9.25 us

profile of v6, /device:TPU:0, one launch (start us, length us, event | category | flops | bytes accessed | tf_op | source)
XLA Modules:
  0.0 273.4 jit_solution(14118475994389848339)
XLA Ops:
  0.7 0.7 broadcast_subtract_fusion
  1.3 0.7 convert_element_type.10
  2.0 0.7 convert_element_type.11
  2.7 0.8 convert_add_fusion
  3.4 0.2 dynamic_update_slice.6
  3.7 0.2 dynamic_update_slice.7
  3.9 0.7 reshape.67.refs_3_
  4.5 0.6 broadcast_in_dim.6.refs_1_
  5.2 1.4 broadcast_in_dim.7.refs_2_
  6.5 94.3 %front.1 = (bf16[2048,768]{1,0:T(8,128)(2,1)}, bf16[2048,768]{1,0:T(8,128)(2,1)}, bf16[2048,768]{1,0:T(8,128)(2,1)}, f32[12,8,512]{2,1,0:T(8,128)}, bf16[2048,76...) custom-call(bf16[2048,768]{1,0:T(8,128)(2,1)} %refs_0_.3, ...), custom_call_target="tpu_custom_call" | custom-call | tf_op jit(solution)/shard_map/front/pallas_call | solution.py:521
  100.8 51.7 %middle.1 = (bf16[2048,768]{1,0:T(8,128)(2,1)}, bf16[2048,768]{1,0:T(8,128)(2,1)}, bf16[2048,3072]{1,0:T(8,128)(2,1)}, f32[2048,768]{1,0:T(8,128)}, bf16[2048,76...) custom-call(f32[2048,768]{1,0:T(8,128)} %get-tuple-element.66.y1_ref, ...), custom_call_target="tpu_custom_call" | custom-call | tf_op jit(solution)/shard_map/middle/pallas_call | solution.py:625
  152.6 0.0 copy-start.3
  152.6 0.0 copy-start.4
  152.6 0.0 copy-start.5
  152.6 0.0 copy-start
  152.6 0.0 copy-start.1
  152.6 0.0 copy-start.2
  152.6 109.3 %back.1 = (bf16[4,4,4,48,768]{4,3,2,1,0:T(8,128)(2,1)}, bf16[5,4,4,48,768]{4,3,2,1,0:T(8,128)(2,1)}, f32[8,24,768]{2,1,0:T(8,128)}, f32[2,48,768]{2,1,0:T(8,128)...) custom-call(bf16[2048,768]{1,0:T(8,128)(2,1)} %refs_0_.3, s32[4,8,512]{2,1,0:T(8,128)} %broadcast_in_dim.6.refs_1_, ...), custom_call_target="tpu_custom_call" | custom-call | tf_op jit(solution)/shard_map/back/pallas_call | solution.py:1077
  261.9 0.8 reshape.70
  262.7 0.0 copy-done.4
  262.7 0.6 subtract_multiply_fusion
  263.3 0.0 copy-done
  263.3 0.7 multiply_add_fusion
  264.0 9.3 %update.1 = (f32[24,2304]{1,0:T(8,128)}, f32[24,768]{1,0:T(8,128)}, f32[24,3072]{1,0:T(8,128)}, f32[96,768]{1,0:T(8,128)}, f32[24,2304]{1,0:T(8,128)}, /*index=5...) custom-call(f32[8,24,768]{2,1,0:T(8,128)} %get-tuple-element.85.refs, ...), custom_call_target="tpu_custom_call" | custom-call | tf_op jit(solution)/shard_map/update/pallas_call | solution.py:1159
  (5 shorter events, 0.0 us)
Async XLA Ops:
  152.6 110.1 %copy-start.3 = (f32[48]{0:T(128)S(1)}, f32[48]{0:T(128)}, u32[]{:S(2)}) copy-start(f32[48]{0:T(128)} %param.30) | copy-start | bytes 580
  152.6 110.1 %copy-start.4 = (f32[48]{0:T(128)S(1)}, f32[48]{0:T(128)}, u32[]{:S(2)}) copy-start(f32[48]{0:T(128)} %param.42) | copy-start | bytes 580
  152.6 110.1 %copy-start.5 = (f32[48]{0:T(128)S(1)}, f32[48]{0:T(128)}, u32[]{:S(2)}) copy-start(f32[48]{0:T(128)} %param.36) | copy-start | bytes 580
  152.6 110.7 %copy-start = (f32[240]{0:T(256)S(1)}, f32[240]{0:T(256)}, u32[]{:S(2)}) copy-start(f32[240]{0:T(256)} %param.31) | copy-start | bytes 2884
  152.6 110.7 %copy-start.1 = (f32[240]{0:T(256)S(1)}, f32[240]{0:T(256)}, u32[]{:S(2)}) copy-start(f32[240]{0:T(256)} %param.43) | copy-start | bytes 2884
  152.6 110.7 %copy-start.2 = (f32[240]{0:T(256)S(1)}, f32[240]{0:T(256)}, u32[]{:S(2)}) copy-start(f32[240]{0:T(256)} %param.37) | copy-start | bytes 2884

commit v7 on v6

--- a/solution.py
+++ b/solution.py
@@ -903,7 +903,7 @@
             qc, dcc, t, dp = ahead
             if b + 1 < len(places):
                 ahead = begin(*places[b + 1])
-            t = t * SCORE + mask_bias(col_ref.at[0], row_ref.at[0], b, first, width)
+            t = t * SCORE + mask_bias(col_ref.at[r], row_ref.at[r], b, first, width)
             p = jnp.exp2(t - lse_ref[0, b : b + 1, :])
             pdp = p * dp
             weighted = jnp.sum(pdp, axis=0, keepdims=True)
@@ -1002,9 +1002,6 @@
 
     def turn(s):
         return jnp.clip(s - OUTERS, 0, att - 1)
-
-    def code_at(s):
-        return (turn(s) % rows, 0, 0)
 
     def head_at(s):
         return (turn(s) % rows, turn(s) // rows)
@@ -1079,8 +1076,8 @@
         grid=(end + rows,),
         in_specs=[
             anywhere,
-            pl.BlockSpec((1, 8, SEQ), code_at),
-            pl.BlockSpec((1, SEQ, BAND), code_at),
+            constant((rows, 8, SEQ)),
+            constant((rows, SEQ, BAND)),
             anywhere,
             head, head, head, head,
             pl.BlockSpec((1, 8, PACK * BAND), lambda s: (turn(s), 0, 0)),

time: 274 us -> 274 us (level)
  no operation moved by 1% of the time
where the time goes in v7:
time: 274 us
  Pallas kernels  265 us (97%)
  other arithmetic  4.03 us (1%)
  local copies, waits for them, and re-layouts  3.91 us (1%)
    pallas_call x1, Pallas kernels, back(): pl.pallas_call(kernel, grid=(end + rows,), in_specs=[anywhere, constant((...  109 us
    pallas_call x1, Pallas kernels, front(): pl.pallas_call(partial(front_kernel, nz), grid=(att + rows,), in_specs=in...  94.3 us
    pallas_call x1, Pallas kernels, middle(): pl.pallas_call(middle_kernel, grid=(tokens // tile,), in_specs=[narrow, w...  51.7 us
    pallas_call x1, Pallas kernels, update_weights(): pl.pallas_call(partial(update_kernel, tokens_all), in_specs=[whole] * 2 +...  9.25 us

profile of v7, /device:TPU:0, one launch (start us, length us, event | category | flops | bytes accessed | tf_op | source)
XLA Modules:
  0.0 273.5 jit_solution(7557876257605890659)
XLA Ops:
  0.7 0.7 broadcast_subtract_fusion
  1.3 0.7 convert_element_type.10
  2.0 0.7 convert_element_type.11
  2.7 0.8 convert_add_fusion
  3.4 0.2 dynamic_update_slice.6
  3.7 0.2 dynamic_update_slice.7
  3.9 0.7 reshape.67.refs_3_
  4.5 0.6 broadcast_in_dim.6.refs_1_
  5.2 1.4 broadcast_in_dim.7.refs_2_
  6.5 94.3 %front.1 = (bf16[2048,768]{1,0:T(8,128)(2,1)}, bf16[2048,768]{1,0:T(8,128)(2,1)}, bf16[2048,768]{1,0:T(8,128)(2,1)}, f32[12,8,512]{2,1,0:T(8,128)}, bf16[2048,76...) custom-call(bf16[2048,768]{1,0:T(8,128)(2,1)} %refs_0_.3, ...), custom_call_target="tpu_custom_call" | custom-call | tf_op jit(solution)/shard_map/front/pallas_call | solution.py:521
  100.8 51.7 %middle.1 = (bf16[2048,768]{1,0:T(8,128)(2,1)}, bf16[2048,768]{1,0:T(8,128)(2,1)}, bf16[2048,3072]{1,0:T(8,128)(2,1)}, f32[2048,768]{1,0:T(8,128)}, bf16[2048,76...) custom-call(f32[2048,768]{1,0:T(8,128)} %get-tuple-element.66.y1_ref, ...), custom_call_target="tpu_custom_call" | custom-call | tf_op jit(solution)/shard_map/middle/pallas_call | solution.py:625
  152.6 0.0 copy-start.3
  152.6 0.0 copy-start.4
  152.6 0.0 copy-start.5
  152.6 0.0 copy-start
  152.6 0.0 copy-start.1
  152.6 0.0 copy-start.2
  152.6 109.4 %back.1 = (bf16[4,4,4,48,768]{4,3,2,1,0:T(8,128)(2,1)}, bf16[5,4,4,48,768]{4,3,2,1,0:T(8,128)(2,1)}, f32[8,24,768]{2,1,0:T(8,128)}, f32[2,48,768]{2,1,0:T(8,128)...) custom-call(bf16[2048,768]{1,0:T(8,128)(2,1)} %refs_0_.3, s32[4,8,512]{2,1,0:T(8,128)} %broadcast_in_dim.6.refs_1_, ...), custom_call_target="tpu_custom_call" | custom-call | tf_op jit(solution)/shard_map/back/pallas_call | solution.py:1074
  262.0 0.8 reshape.70
  262.8 0.0 copy-done.3
  262.8 0.6 subtract_multiply_fusion
  263.5 0.0 copy-done.1
  263.5 0.7 multiply_add_fusion
  264.1 9.3 %update.1 = (f32[24,2304]{1,0:T(8,128)}, f32[24,768]{1,0:T(8,128)}, f32[24,3072]{1,0:T(8,128)}, f32[96,768]{1,0:T(8,128)}, f32[24,2304]{1,0:T(8,128)}, /*index=5...) custom-call(f32[8,24,768]{2,1,0:T(8,128)} %get-tuple-element.85.refs, ...), custom_call_target="tpu_custom_call" | custom-call | tf_op jit(solution)/shard_map/update/pallas_call | solution.py:1156
  (5 shorter events, 0.0 us)
Async XLA Ops:
  152.6 110.3 %copy-start.3 = (f32[48]{0:T(128)S(1)}, f32[48]{0:T(128)}, u32[]{:S(2)}) copy-start(f32[48]{0:T(128)} %param.30) | copy-start | bytes 580
  152.6 110.3 %copy-start.4 = (f32[48]{0:T(128)S(1)}, f32[48]{0:T(128)}, u32[]{:S(2)}) copy-start(f32[48]{0:T(128)} %param.42) | copy-start | bytes 580
  152.6 110.3 %copy-start.5 = (f32[48]{0:T(128)S(1)}, f32[48]{0:T(128)}, u32[]{:S(2)}) copy-start(f32[48]{0:T(128)} %param.36) | copy-start | bytes 580
  152.6 110.9 %copy-start = (f32[240]{0:T(256)S(1)}, f32[240]{0:T(256)}, u32[]{:S(2)}) copy-start(f32[240]{0:T(256)} %param.31) | copy-start | bytes 2884
  152.6 110.8 %copy-start.1 = (f32[240]{0:T(256)S(1)}, f32[240]{0:T(256)}, u32[]{:S(2)}) copy-start(f32[240]{0:T(256)} %param.43) | copy-start | bytes 2884
  152.6 110.8 %copy-start.2 = (f32[240]{0:T(256)S(1)}, f32[240]{0:T(256)}, u32[]{:S(2)}) copy-start(f32[240]{0:T(256)} %param.37) | copy-start | bytes 2884
